TPU v7x, 256 devices: a whole 4x4x8 slice. The times are simulated.
256 devices in a mesh: dp: 16 (over y, x), tensor: 16 (over z, core).
Axes of the slice: x: 4, y: 4, z: 8, core: 2. Of those that a mesh axis runs over, the one named last changes fastest.
Arguments:
- tokens: bfloat16 [1024, 8192], P('tensor', 'dp'), may hold values from -6 to 6
- gate_weight: bfloat16 [8192, 14336], P('dp', 'tensor'), may hold values from -0.0625 to 0.0625
- up_weight: bfloat16 [8192, 14336], P('dp', 'tensor'), may hold values from -0.0625 to 0.0625
- down_weight: bfloat16 [14336, 8192], P('tensor', 'dp'), may hold values from -0.046875 to 0.046875
- out_grad: bfloat16 [1024, 8192], P('tensor', 'dp'), may hold values from -6 to 6
Outputs:
- ffn_output: bfloat16 [1024, 8192], P('tensor', 'dp')
- input_grad: bfloat16 [1024, 8192], P('tensor', 'dp')
- gate_weight_grad: float32 [8192, 14336], P('dp', 'tensor')
- up_weight_grad: float32 [8192, 14336], P('dp', 'tensor')
- down_weight_grad: float32 [14336, 8192], P('tensor', 'dp')
All inputs are finite; a program needn't handle non-finite values.
Results may differ from a plain program's by a relative error of at most 0.0049.
Values may be sent and summed in bfloat16 or wider, within the bound.
No kernel may reach another device: no remote copies, remote signals or barrier semaphores. Data moves between devices by JAX's collectives and lax.ppermute only.
A program may use at most 128 MiB of HBM per device.

v0:
```python
import functools
import math

import jax
import jax.numpy as jnp
from jax import lax
from jax.experimental import pallas as pl
from jax.experimental.pallas import tpu as pltpu
from jax.sharding import PartitionSpec as P

MIB = 1024 * 1024
BF16 = jnp.bfloat16
F32 = jnp.float32
BOTH = ("dp", "tensor")
RING = 4
DEPTH = 8


def dot(a, b, contract):
    return lax.dot_general(a, b, ((contract[:1], contract[1:]), ((), ())), preferred_element_type=F32)


def place():
    dp, tensor = lax.axis_index("dp"), lax.axis_index("tensor")
    y, x, z, core = dp // RING, dp % RING, tensor // 2, tensor % 2
    return jnp.where(core == 0, x, y), jnp.where(core == 0, y, x), z, core


def tile_at(i, j):
    p, q, _, core = place()
    tile = RING * ((p + i) % RING) + (q + j) % RING
    return (tile % 2) ^ core, tile // 2


def call(kernel, out, *args, flops=0):
    outs = out if isinstance(out, list) else [out]
    size = sum(a.size * a.dtype.itemsize for a in (*args, *outs))
    return pl.pallas_call(
        kernel,
        out_shape=out,
        compiler_params=pltpu.CompilerParams(vmem_limit_bytes=24 * MIB),
        cost_estimate=pl.CostEstimate(flops=0, bytes_accessed=0, transcendentals=0),
    )(*args)


def shape(dims, dtype):
    return jax.ShapeDtypeStruct(dims, dtype)


def along(first, k):
    pairs = []
    for y in range(RING):
        for x in range(RING):
            for z in range(DEPTH):
                for core in range(2):
                    if (core == 0) == first:
                        to = (y, (x + k) % RING)
                    else:
                        to = ((y + k) % RING, x)
                    t = z * 2 + core
                    pairs.append(((y * RING + x) * 2 * DEPTH + t, (to[0] * RING + to[1]) * 2 * DEPTH + t))
    return pairs


def send_p(a, k):
    return lax.ppermute(a, BOTH, along(True, k % RING))


def send_q(a, k):
    return lax.ppermute(a, BOTH, along(False, k % RING))


def send_core(a):
    return lax.ppermute(a, "tensor", [(i, i ^ 1) for i in range(2 * DEPTH)])


ORDER = (2, 1, 3)
CORES = [[z * 2 + c for z in range(DEPTH)] for c in range(2)]


def row_block(mine, other, i):
    tiles = []
    for j in range(RING):
        foreign, z = tile_at(i, j)
        tiles.append(jnp.where(foreign == 0, mine[z], other[z]))
    return jnp.concatenate(tiles, 0)


def join(*tiles):
    rows, columns = tiles[0].shape

    def kernel(*refs):
        for j, ref in enumerate(refs[:-1]):
            refs[-1][pl.ds(j * rows, rows)] = ref[...]

    return call(kernel, shape((len(tiles) * rows, columns), tiles[0].dtype), *tiles)


def gather_z(a):
    copies = jnp.broadcast_to(a, (DEPTH, *a.shape))
    mine = lax.all_to_all(copies, "tensor", 0, 0, tiled=True, axis_index_groups=CORES)
    return mine, send_core(mine)


def project(mine, other, gate_weight, up_weight, i, dtype):
    width, hidden = gate_weight.shape
    rows = RING * mine.shape[1]

    def kernel(mine_ref, other_ref, gate_ref, up_ref, out_ref):
        block = row_block(mine_ref, other_ref, i)
        out_ref[:, :hidden] = dot(block, gate_ref[...], (1, 0)).astype(dtype)
        out_ref[:, hidden:] = dot(block, up_ref[...], (1, 0)).astype(dtype)

    return call(
        kernel, shape((rows, 2 * hidden), dtype), mine, other, gate_weight, up_weight, flops=4 * rows * width * hidden
    )


def grad_block(grads, i):
    core = place()[3]
    tiles = []
    for j in range(RING):
        foreign, z = tile_at(i, j)
        tiles.append(grads[2 * z + (foreign ^ core)])
    return jnp.concatenate(tiles, 0)


def project_grad(grads, down_weight, i, dtype):
    hidden, width = down_weight.shape
    rows = RING * grads.shape[1]

    def kernel(grads_ref, down_ref, out_ref):
        out_ref[...] = dot(grad_block(grads_ref, i), down_ref[...], (1, 1)).astype(dtype)

    return call(kernel, shape((rows, hidden), dtype), grads, down_weight, flops=2 * rows * width * hidden)


def add_blocks(own, parts):
    rows, columns = own.shape
    tile = rows // RING

    def kernel(own_ref, a_ref, b_ref, c_ref, *outs):
        for j, out in enumerate(outs):
            at = pl.ds(j * tile, tile)
            out[...] = own_ref[at] + (a_ref[at].astype(F32) + b_ref[at].astype(F32) + c_ref[at].astype(F32))

    return call(kernel, [shape((tile, columns), F32)] * RING, own, *parts)


def spread(tiles):
    return [tiles[0]] + [send_q(tiles[j], j) for j in ORDER]


def activate(terms):
    rows, columns = terms[0].shape
    hidden = columns // 2

    def kernel(a, b, c, d, hidden_ref, up_factor, gate_factor):
        def total(at):
            return (a[:, at] + b[:, at]) + (c[:, at] + d[:, at])

        gate, up = total(pl.ds(0, hidden)), total(pl.ds(hidden, hidden))
        s = jax.nn.sigmoid(gate)
        activated = gate * s
        hidden_ref[...] = (activated * up).astype(BF16)
        up_factor[...] = activated
        gate_factor[...] = up * s * (1.0 + gate * (1.0 - s))

    return call(
        kernel, [shape((rows, hidden), BF16), shape((rows, hidden), F32), shape((rows, hidden), F32)], *terms
    )


def activate_grad(terms, up_factor, gate_factor):
    rows, hidden = up_factor.shape

    def kernel(a, b, c, d, up_ref, gate_ref, out_ref):
        hidden_grad = (a[...] + b[...]) + (c[...] + d[...])
        out_ref[:, :hidden] = (hidden_grad * gate_ref[...]).astype(BF16)
        out_ref[:, hidden:] = (hidden_grad * up_ref[...]).astype(BF16)

    return call(kernel, shape((rows, 2 * hidden), BF16), *terms, up_factor, gate_factor)


def gather_q(tile):
    return [tile] + [send_q(tile, -j) for j in range(1, RING)]


def gather_p(block):
    return [block] + [send_p(block, -i) for i in range(1, RING)]


def store_tile(mine, other, foreign, at, part):
    @pl.when(foreign == 0)
    def _():
        mine[at] = part

    @pl.when(foreign == 1)
    def _():
        other[at] = part


def store_tiles(mine, other, i, result):
    tile = mine.shape[1]
    for j in range(RING):
        store_tile(mine, other, *tile_at(i, j), result[j * tile : (j + 1) * tile])


def back(blocks, weights):
    hidden, width = weights.shape
    rows = blocks[0].shape[0]

    def kernel(a, b, c, d, weights_ref, mine, other):
        for i, block in enumerate((a, b, c, d)):
            store_tiles(mine, other, i, dot(block[...], weights_ref[...], (1, 0)))

    half = shape((DEPTH, rows // RING, width), F32)
    return call(kernel, [half, half], *blocks, weights, flops=2 * RING * rows * width * hidden)


def transposed(gate_weight, up_weight):
    width, hidden = gate_weight.shape

    def kernel(gate_ref, up_ref, out_ref):
        out_ref[:hidden] = gate_ref[...].T
        out_ref[hidden:] = up_ref[...].T

    return call(kernel, shape((2 * hidden, width), BF16), gate_weight, up_weight)


def reduce_z(mine, other, done):
    arrived = send_core(other)
    depth, rows, width = mine.shape

    def split(mine_ref, arrived_ref, own, out):
        own[...] = mine_ref[place()[2]] + arrived_ref[place()[2]]
        for k in range(depth):
            out[k] = (mine_ref[k] + arrived_ref[k]).astype(BF16)

    own, parts = call(split, [shape((rows, width), F32), shape(mine.shape, BF16)], mine, arrived)
    parts = lax.all_to_all(parts, "tensor", 0, 0, tiled=True, axis_index_groups=CORES)

    def add(own_ref, parts_ref, done_ref, out, done_out):
        total = own_ref[...]
        for k in range(depth):
            total += jnp.where(place()[2] == k, 0.0, parts_ref[k].astype(F32))
        out[...] = total.astype(BF16)
        done_out[...] = done_ref[...].astype(BF16)

    return call(add, [shape((rows, width), BF16)] * 2, own, parts, done)


def hidden_weight_grad(blocks, grads, factor):
    rows, hidden = blocks[0].shape
    width = grads.shape[2]

    def kernel(a, b, c, d, grads_ref, out_ref):
        for i, block in enumerate((a, b, c, d)):
            part = dot(block[...], grad_block(grads_ref, i), (0, 0)) * factor
            if i == 0:
                out_ref[...] = part
            else:
                out_ref[...] += part

    return call(
        kernel, shape((hidden, width), F32), *blocks, grads, flops=2 * RING * rows * width * hidden
    )


def token_weight_grads(blocks, mine, other, factor):
    rows, hidden = blocks[0].shape[0], blocks[0].shape[1] // 2
    width = mine.shape[2]

    def kernel(a, b, c, d, mine_ref, other_ref, gate_ref, up_ref):
        for i, block in enumerate((a, b, c, d)):
            tokens = row_block(mine_ref, other_ref, i)
            gate = dot(tokens, block[:, :hidden], (0, 0)) * factor
            up = dot(tokens, block[:, hidden:], (0, 0)) * factor
            if i == 0:
                gate_ref[...] = gate
                up_ref[...] = up
            else:
                gate_ref[...] += gate
                up_ref[...] += up

    out = shape((width, hidden), F32)
    return call(kernel, [out, out], *blocks, mine, other, flops=4 * RING * rows * width * hidden)


def body(tokens, gate_weight, up_weight, down_weight, out_grad):
    shard, width = tokens.shape
    rows = shard * 2 * DEPTH
    factor = 1.0 / math.sqrt(rows)

    rows_of = list(gather_z(tokens))
    grads = lax.all_gather(out_grad, "tensor", axis=0)
    blocks = {i: project(*rows_of, gate_weight, up_weight, i, BF16) for i in ORDER}
    rows_of[0], grads = lax.optimization_barrier((rows_of[0], grads))
    blocks[0] = project(*rows_of, gate_weight, up_weight, 0, F32)
    grad_blocks = {i: project_grad(grads, down_weight, i, BF16 if i else F32) for i in (*ORDER, 0)}

    blocks[0], *sent = lax.optimization_barrier((blocks[0], *(grad_blocks[i] for i in ORDER)))
    grad_blocks.update(zip(ORDER, sent))
    tiles = add_blocks(blocks[0], [send_p(blocks[i], i) for i in ORDER])
    grad_tiles = list(add_blocks(grad_blocks[0], [send_p(grad_blocks[i], i) for i in ORDER]))
    terms = spread(tiles)
    terms[0], *grad_tiles = lax.optimization_barrier((terms[0], *grad_tiles))
    hidden, up_factor, gate_factor = activate(terms)
    near = gather_q(hidden)
    grad_terms = spread(grad_tiles)
    near[0], *grad_terms = lax.optimization_barrier((near[0], *grad_terms))
    grad_near = gather_q(activate_grad(grad_terms, up_factor, gate_factor))
    hidden_blocks = gather_p(join(*near))
    grad_block = join(*grad_near)
    hidden_blocks[0], _ = lax.optimization_barrier((hidden_blocks[0], grad_block))
    grad_blocks = gather_p(grad_block)

    keep, give = back(hidden_blocks, down_weight)
    half = (keep + send_core(give)).reshape(rows // 2, width)
    down_weight_grad = hidden_weight_grad(hidden_blocks, grads, factor)
    grad_blocks[0], down_weight_grad, half = lax.optimization_barrier((grad_blocks[0], down_weight_grad, half))
    ffn_output = lax.psum_scatter(half, "tensor", scatter_dimension=0, tiled=True, axis_index_groups=CORES)
    input_grad, ffn_output = reduce_z(*back(grad_blocks, transposed(gate_weight, up_weight)), ffn_output)
    gate_weight_grad, up_weight_grad = token_weight_grads(grad_blocks, *rows_of, factor)
    return ffn_output, input_grad, gate_weight_grad, up_weight_grad, down_weight_grad


def solution(mesh):
    return jax.shard_map(
        body,
        mesh=mesh,
        in_specs=(
            P("tensor", "dp"),
            P("dp", "tensor"),
            P("dp", "tensor"),
            P("tensor", "dp"),
            P("tensor", "dp"),
        ),
        out_specs=(
            P("tensor", "dp"),
            P("tensor", "dp"),
            P("dp", "tensor"),
            P("dp", "tensor"),
            P("tensor", "dp"),
        ),
        check_vma=False,
    )
```

profile of v0, /device:TPU:1, one launch (start us, length us, event | category | flops | bytes accessed | tf_op | source)
XLA Modules:
  0.0 194.5 jit_solution(4224903229446115345)
XLA Ops:
  7.2 1.8 broadcast_in_dim.3
  8.9 9.0 %all-to-all-start = ((bf16[8,64,512]{2,1,0:T(8,128)(2,1)}), bf16[8,64,512]{2,1,0:T(8,128)(2,1)S(1)}, u32[]{:S(2)}, u32[]{:S(2)}) async-start(bf16[8,64,512]{2,1,0:T(8,128)(2,1)} %broadcast_in_dim.3), calls=%async_computation | async-start | bytes 1048576 | tf_op jit(solution)/shard_map/all_to_all | solution.py:101
  18.7 17.2 %all-to-all-done.mine_ref = bf16[8,64,512]{2,1,0:T(8,128)(2,1)S(1)} async-done(((bf16[8,64,512]{2,1,0:T(8,128)(2,1)}), bf16[8,64,512]{2,1,0:T(8,128)(2,1)S(1)}, u32[]{:S(2)}, u32[]{:S(2)}) %all-to-all-start) | async-done | bytes 524320 | tf_op jit(solution)/shard_map/all_to_all | solution.py:101
  36.4 1.5 collective-permute-done.other_ref
  37.9 1.2 copy-done.4
  39.1 1.6 shard_map.96
  40.8 2.9 %collective-permute-start.1 = (bf16[256,1792]{1,0:T(8,128)(2,1)}, bf16[256,1792]{1,0:T(8,128)(2,1)}, u32[]{:S(2)}, u32[]{:S(2)}) collective-permute-start(bf16[256,1792]{1,0:T(8,128)(2,1)} %shard_map.96), channel_id=1, source_target_pairs={{0,32},{1,129},{2,34},{3,131},{4,36},{5,133},{6,38},{7,135},{8,40}... | collective-permute-start | bytes 2752520 | tf_op jit(solution)/shard_map/ppermute | solution.py:66
  43.7 1.6 shard_map.97
  45.7 1.6 shard_map.98
  47.4 2.3 %collective-permute-start.3 = (bf16[256,1792]{1,0:T(8,128)(2,1)}, bf16[256,1792]{1,0:T(8,128)(2,1)}, u32[]{:S(2)}, u32[]{:S(2)}) collective-permute-start(bf16[256,1792]{1,0:T(8,128)(2,1)} %shard_map.98), channel_id=1, source_target_pairs={{0,48},{1,193},{2,50},{3,195},{4,52},{5,197},{6,54},{7,199},{8,56}... | collective-permute-start | bytes 2752520 | tf_op jit(solution)/shard_map/ppermute | solution.py:66
  49.7 11.9 %all-gather.3.cloned.1.call-done = bf16[1024,512]{1,0:T(8,128)(2,1)} async-done(((bf16[64,512]{1,0:T(8,128)(2,1)}), bf16[1024,512]{1,0:T(8,128)(2,1)}) %all-gather.3.cloned.1.call-update) | async-done | bytes 1048592 | tf_op jit(solution)/shard_map/all_gather | solution.py:296
  61.6 1.2 copy-done
  65.4 2.8 %collective-permute-start.4 = (bf16[256,896]{1,0:T(8,128)(2,1)S(1)}, bf16[256,896]{1,0:T(8,128)(2,1)S(1)}, u32[]{:S(2)}, u32[]{:S(2)}) collective-permute-start(bf16[256,896]{1,0:T(8,128)(2,1)S(1)} %shard_map.93), channel_id=1, source_target_pairs={{0,32},{1,129},{2,34},{3,131},{4,36},{5,133},{6,38},{7,135},{8,40}... | collective-permute-start | bytes 1376264 | tf_op jit(solution)/shard_map/ppermute | solution.py:66
  68.5 2.4 %collective-permute-start.6 = (bf16[256,896]{1,0:T(8,128)(2,1)S(1)}, bf16[256,896]{1,0:T(8,128)(2,1)S(1)}, u32[]{:S(2)}, u32[]{:S(2)}) collective-permute-start(bf16[256,896]{1,0:T(8,128)(2,1)S(1)} %shard_map.95), channel_id=1, source_target_pairs={{0,48},{1,193},{2,50},{3,195},{4,52},{5,197},{6,54},{7,199},{8,56}... | collective-permute-start | bytes 1376264 | tf_op jit(solution)/shard_map/ppermute | solution.py:66
  70.9 2.1 %shard_map.99 = (f32[64,1792]{1,0:T(8,128)S(1)}, f32[64,1792]{1,0:T(8,128)S(1)}, f32[64,1792]{1,0:T(8,128)S(1)}, f32[64,1792]{1,0:T(8,128)S(1)}) custom-call(f32[256,1792]{1,0:T(8,128)S(1)} %shard_map.92.own_ref, bf16[256,1792]{1,0:T(8,128)(2,1)} %collective-permute-done.1.a_ref, bf16[256,1792]{1,0:T(8,128)(2,1)} %collective-permute-done.2.b_ref, ...), custom_call_target="tpu_custom_call" | custom-call | tf_op jit(solution)/shard_map/pallas_call | solution.py:38
  73.0 2.8 %collective-permute-start.7 = (f32[64,1792]{1,0:T(8,128)S(1)}, f32[64,1792]{1,0:T(8,128)S(1)}, u32[]{:S(2)}, u32[]{:S(2)}) collective-permute-start(f32[64,1792]{1,0:T(8,128)S(1)} %get-tuple-element.58), channel_id=1, source_target_pairs={{0,128},{1,33},{2,130},{3,35},{4,132},{5,37},{6,134},{7,39},{8,136... | collective-permute-start | bytes 1376264 | tf_op jit(solution)/shard_map/ppermute | solution.py:70
  76.0 2.4 %collective-permute-start.9 = (f32[64,1792]{1,0:T(8,128)S(1)}, f32[64,1792]{1,0:T(8,128)S(1)}, u32[]{:S(2)}, u32[]{:S(2)}) collective-permute-start(f32[64,1792]{1,0:T(8,128)S(1)} %get-tuple-element.60), channel_id=1, source_target_pairs={{0,192},{1,49},{2,194},{3,51},{4,196},{5,53},{6,198},{7,55},{8,200... | collective-permute-start | bytes 1376264 | tf_op jit(solution)/shard_map/ppermute | solution.py:70
  78.9 1.2 collective-permute-done.5.b_ref
  80.5 9.7 %collective-permute-start.10 = (f32[64,896]{1,0:T(8,128)S(1)}, f32[64,896]{1,0:T(8,128)S(1)}, u32[]{:S(2)}, u32[]{:S(2)}) collective-permute-start(f32[64,896]{1,0:T(8,128)S(1)} %get-tuple-element.63), channel_id=1, source_target_pairs={{0,128},{1,33},{2,130},{3,35},{4,132},{5,37},{6,134},{7,39},{8,136... | collective-permute-start | bytes 688136 | tf_op jit(solution)/shard_map/ppermute | solution.py:70
  90.2 2.7 %collective-permute-start.12 = (f32[64,896]{1,0:T(8,128)S(1)}, f32[64,896]{1,0:T(8,128)S(1)}, u32[]{:S(2)}, u32[]{:S(2)}) collective-permute-start(f32[64,896]{1,0:T(8,128)S(1)} %get-tuple-element.65), channel_id=1, source_target_pairs={{0,192},{1,49},{2,194},{3,51},{4,196},{5,53},{6,198},{7,55},{8,200... | collective-permute-start | bytes 688136 | tf_op jit(solution)/shard_map/ppermute | solution.py:70
  93.7 0.9 collective-permute-start.18
  94.6 2.0 %collective-permute-done.11.c = f32[64,896]{1,0:T(8,128)S(1)} collective-permute-done((f32[64,896]{1,0:T(8,128)S(1)}, f32[64,896]{1,0:T(8,128)S(1)}, u32[]{:S(2)}, u32[]{:S(2)}) %collective-permute-start.11) | collective-permute-done | bytes 229408 | tf_op jit(solution)/shard_map/ppermute | solution.py:70
  96.7 2.5 %collective-permute-start.13 = (bf16[64,1792]{1,0:T(8,128)(2,1)S(1)}, bf16[64,1792]{1,0:T(8,128)(2,1)S(1)}, u32[]{:S(2)}, u32[]{:S(2)}) collective-permute-start(bf16[64,1792]{1,0:T(8,128)(2,1)S(1)} %shard_map.103.refs_0_), channel_id=1, source_target_pairs={{0,192},{1,49},{2,194},{3,51},{4,196},{5,53},{6,198},{7,55},{8,200... | collective-permute-start | bytes 688136 | tf_op jit(solution)/shard_map/ppermute | solution.py:70
  99.1 0.8 collective-permute-done.18.refs_3_
  99.9 1.7 collective-permute-start.19
  101.6 1.1 collective-permute-start.20
  102.7 0.8 collective-permute-start.21
  103.5 2.2 %collective-permute-start.14 = (bf16[64,1792]{1,0:T(8,128)(2,1)S(1)}, bf16[64,1792]{1,0:T(8,128)(2,1)S(1)}, u32[]{:S(2)}, u32[]{:S(2)}) collective-permute-start(bf16[64,1792]{1,0:T(8,128)(2,1)S(1)} %shard_map.103.refs_0_), channel_id=1, source_target_pairs={{0,128},{1,33},{2,130},{3,35},{4,132},{5,37},{6,134},{7,39},{8,136... | collective-permute-start | bytes 688136 | tf_op jit(solution)/shard_map/ppermute | solution.py:70
  106.0 3.9 %collective-permute-done.14.refs_2_ = bf16[64,1792]{1,0:T(8,128)(2,1)S(1)} collective-permute-done((bf16[64,1792]{1,0:T(8,128)(2,1)S(1)}, bf16[64,1792]{1,0:T(8,128)(2,1)S(1)}, u32[]{:S(2)}, u32[]{:S(2)}) %collective-permute-start.14) | collective-permute-done | bytes 229408 | tf_op jit(solution)/shard_map/ppermute | solution.py:70
  109.9 8.3 %collective-permute-done.15.refs_3_ = bf16[64,1792]{1,0:T(8,128)(2,1)S(1)} collective-permute-done((bf16[64,1792]{1,0:T(8,128)(2,1)S(1)}, bf16[64,1792]{1,0:T(8,128)(2,1)S(1)}, u32[]{:S(2)}, u32[]{:S(2)}) %collective-permute-start.15) | collective-permute-done | bytes 229408 | tf_op jit(solution)/shard_map/ppermute | solution.py:70
  118.2 1.0 shard_map.104.a
  119.2 2.0 %shard_map.107 = (f32[8,64,512]{2,1,0:T(8,128)S(1)}, f32[8,64,512]{2,1,0:T(8,128)S(1)}) custom-call(bf16[256,896]{1,0:T(8,128)(2,1)S(1)} %shard_map.105.a, bf16[256,896]{1,0:T(8,128)(2,1)S(1)} %collective-permute-done.19.b, bf16[256,896]{1,0:T(8,128)(2,1)S(1)} %collective-permute-done.20.c, bf16[256,896]{1,0:T(8,128)(2,1)S(1)} %collective-permute-done.21.d, ...), custom_call_target="tpu_custom_call" | custom-call | tf_op jit(solution)/shard_map/pallas_call | solution.py:38
  121.3 7.1 %collective-permute-start.22 = (f32[8,64,512]{2,1,0:T(8,128)S(1)}, f32[8,64,512]{2,1,0:T(8,128)S(1)}, u32[]{:S(2)}, u32[]{:S(2)}) collective-permute-start(f32[8,64,512]{2,1,0:T(8,128)S(1)} %get-tuple-element.75), channel_id=1, source_target_pairs={{0,1},{1,0},{2,3},{3,2},{4,5},{5,4},{6,7},{7,6},{8,9},{9,8},{10,11... | collective-permute-start | bytes 3145736 | tf_op jit(solution)/shard_map/ppermute | solution.py:74
  128.4 1.8 collective-permute-start.23
  130.8 2.4 %shard_map.106 = f32[896,512]{1,0:T(8,128)} custom-call(bf16[256,896]{1,0:T(8,128)(2,1)S(1)} %shard_map.105.a, bf16[256,896]{1,0:T(8,128)(2,1)S(1)} %collective-permute-done.19.b, bf16[256,896]{1,0:T(8,128)(2,1)S(1)} %collective-permute-done.20.c, bf16[256,896]{1,0:T(8,128)(2,1)S(1)} %collective-permute-done.21.d, bf16[16,64,512]{2,1,0:T(8,128)(2,1)S(1)} %bitcast.6), custom_call_target="tpu_custom_call" | custom-call | tf_op jit(solution)/shard_map/pallas_call | solution.py:38
  133.2 1.2 add.5
  134.9 15.8 %collective-permute-done.23.b = bf16[256,1792]{1,0:T(8,128)(2,1)S(1)} collective-permute-done((bf16[256,1792]{1,0:T(8,128)(2,1)}, bf16[256,1792]{1,0:T(8,128)(2,1)S(1)}, u32[]{:S(2)}, u32[]{:S(2)}) %collective-permute-start.23) | collective-permute-done | bytes 917536 | tf_op jit(solution)/shard_map/ppermute | solution.py:66
  150.7 3.4 %collective-permute-done.25.d = bf16[256,1792]{1,0:T(8,128)(2,1)} collective-permute-done((bf16[256,1792]{1,0:T(8,128)(2,1)}, bf16[256,1792]{1,0:T(8,128)(2,1)}, u32[]{:S(2)}, u32[]{:S(2)}) %collective-permute-start.25) | collective-permute-done | bytes 917536 | tf_op jit(solution)/shard_map/ppermute | solution.py:66
  154.1 4.6 %shard_map.109 = (f32[8,64,512]{2,1,0:T(8,128)S(1)}, f32[8,64,512]{2,1,0:T(8,128)S(1)}) custom-call(bf16[256,1792]{1,0:T(8,128)(2,1)} %shard_map.104.a, bf16[256,1792]{1,0:T(8,128)(2,1)S(1)} %collective-permute-done.23.b, bf16[256,1792]{1,0:T(8,128)(2,1)} %collective-permute-done.24.c, bf16[256,1792]{1,0:T(8,128)(2,1)} %collective-permute-done.25.d, ...), custom_call_target="tpu_custom_call" | custom-call | tf_op jit(solution)/shard_map/pallas_call | solution.py:38
  158.7 0.9 copy-done.9
  159.6 1.1 collective-permute-start.26
  160.7 2.3 %collective-permute-done.26.arrived_ref = f32[8,64,512]{2,1,0:T(8,128)S(1)} collective-permute-done((f32[8,64,512]{2,1,0:T(8,128)S(1)}, f32[8,64,512]{2,1,0:T(8,128)S(1)}, u32[]{:S(2)}, u32[]{:S(2)}) %collective-permute-start.26) | collective-permute-done | bytes 1048608 | tf_op jit(solution)/shard_map/ppermute | solution.py:74
  163.0 0.9 shard_map.110
  163.9 4.1 %all-to-all-start.1 = ((bf16[8,64,512]{2,1,0:T(8,128)(2,1)}), bf16[8,64,512]{2,1,0:T(8,128)(2,1)S(1)}, u32[]{:S(2)}, u32[]{:S(2)}) async-start(bf16[8,64,512]{2,1,0:T(8,128)(2,1)} %get-tuple-element.80), calls=%async_computation.1 | async-start | bytes 1048576 | tf_op jit(solution)/shard_map/all_to_all | solution.py:241
  168.0 5.7 %shard_map.112 = (f32[512,896]{1,0:T(8,128)}, f32[512,896]{1,0:T(8,128)}) custom-call(bf16[256,1792]{1,0:T(8,128)(2,1)} %shard_map.104.a, bf16[256,1792]{1,0:T(8,128)(2,1)S(1)} %copy-done.10, bf16[256,1792]{1,0:T(8,128)(2,1)} %collective-permute-done.24.c, bf16[256,1792]{1,0:T(8,128)(2,1)} %collective-permute-done.25.d, ...), custom_call_target="tpu_custom_call" | custom-call | tf_op jit(solution)/shard_map/pallas_call | solution.py:38
  173.7 12.2 %all-to-all-done.1.parts_ref = bf16[8,64,512]{2,1,0:T(8,128)(2,1)S(1)} async-done(((bf16[8,64,512]{2,1,0:T(8,128)(2,1)}), bf16[8,64,512]{2,1,0:T(8,128)(2,1)S(1)}, u32[]{:S(2)}, u32[]{:S(2)}) %all-to-all-start.1) | async-done | bytes 524320 | tf_op jit(solution)/shard_map/all_to_all | solution.py:241
  186.0 0.9 copy-done.11
  186.9 0.8 shard_map.111
  (63 shorter events, 7.9 us)
Async XLA Ops:
  7.2 30.8 %copy-start.3 = (bf16[512,896]{1,0:T(8,128)(2,1)S(1)}, bf16[512,896]{1,0:T(8,128)(2,1)}, u32[]{:S(2)}) copy-start(bf16[512,896]{1,0:T(8,128)(2,1)} %gate_ref.9) | copy-start | bytes 2752516
  8.9 27.0 %all-to-all-start = ((bf16[8,64,512]{2,1,0:T(8,128)(2,1)}), bf16[8,64,512]{2,1,0:T(8,128)(2,1)S(1)}, u32[]{:S(2)}, u32[]{:S(2)}) async-start(bf16[8,64,512]{2,1,0:T(8,128)(2,1)} %broadcast_in_dim.3), calls=%async_computation | async-start | bytes 1048576 | tf_op jit(solution)/shard_map/all_to_all | solution.py:101
  17.9 43.7 %all-gather.3.cloned.1.call-start = ((), (), s32[]{:S(2)}) async-start(), calls=%async_computation.4 | async-start | bytes 1114112 | tf_op jit(solution)/shard_map/all_gather | solution.py:296
  18.7 167.3 %reduce-scatter.2.cloned.1.call-start = ((), (), s32[]{:S(2)}) async-start(), calls=%async_computation.3 | async-start | bytes 1179648 | tf_op jit(solution)/shard_map/reduce_scatter | solution.py:322
  35.9 2.0 %collective-permute-start = (bf16[8,64,512]{2,1,0:T(8,128)(2,1)S(1)}, bf16[8,64,512]{2,1,0:T(8,128)(2,1)S(1)}, u32[]{:S(2)}, u32[]{:S(2)}) collective-permute-start(bf16[8,64,512]{2,1,0:T(8,128)(2,1)S(1)} %all-to-all-done.mine_ref), channel_id=1, source_target_pairs={{0,1},{1,0},{2,3},{3,2},{4,5},{5,4},{6,7},{7,6},{8,9},{9,8},{10,11... | collective-permute-start | bytes 1572872 | tf_op jit(solution)/shard_map/ppermute | solution.py:74
  37.9 1.2 copy-start.4
  39.1 6.6 %copy-start.6 = (bf16[8,64,512]{2,1,0:T(8,128)(2,1)}, bf16[8,64,512]{2,1,0:T(8,128)(2,1)S(1)}, u32[]{:S(2)}) copy-start(bf16[8,64,512]{2,1,0:T(8,128)(2,1)S(1)} %collective-permute-done.other_ref) | copy-start | bytes 1572868
  40.8 27.7 %collective-permute-start.1 = (bf16[256,1792]{1,0:T(8,128)(2,1)}, bf16[256,1792]{1,0:T(8,128)(2,1)}, u32[]{:S(2)}, u32[]{:S(2)}) collective-permute-start(bf16[256,1792]{1,0:T(8,128)(2,1)} %shard_map.96), channel_id=1, source_target_pairs={{0,32},{1,129},{2,34},{3,131},{4,36},{5,133},{6,38},{7,135},{8,40}... | collective-permute-start | bytes 2752520 | tf_op jit(solution)/shard_map/ppermute | solution.py:66
  45.3 16.3 %copy-start.2 = (bf16[896,512]{1,0:T(8,128)(2,1)S(1)}, bf16[896,512]{1,0:T(8,128)(2,1)}, u32[]{:S(2)}) copy-start(bf16[896,512]{1,0:T(8,128)(2,1)} %weights_ref.1) | copy-start | bytes 2752516
  45.3 25.5 %collective-permute-start.2 = (bf16[256,1792]{1,0:T(8,128)(2,1)}, bf16[256,1792]{1,0:T(8,128)(2,1)}, u32[]{:S(2)}, u32[]{:S(2)}) collective-permute-start(bf16[256,1792]{1,0:T(8,128)(2,1)} %shard_map.97), channel_id=1, source_target_pairs={{0,16},{1,65},{2,18},{3,67},{4,20},{5,69},{6,22},{7,71},{8,24},{9,... | collective-permute-start | bytes 2752520 | tf_op jit(solution)/shard_map/ppermute | solution.py:66
  47.4 23.5 %collective-permute-start.3 = (bf16[256,1792]{1,0:T(8,128)(2,1)}, bf16[256,1792]{1,0:T(8,128)(2,1)}, u32[]{:S(2)}, u32[]{:S(2)}) collective-permute-start(bf16[256,1792]{1,0:T(8,128)(2,1)} %shard_map.98), channel_id=1, source_target_pairs={{0,48},{1,193},{2,50},{3,195},{4,52},{5,197},{6,54},{7,199},{8,56}... | collective-permute-start | bytes 2752520 | tf_op jit(solution)/shard_map/ppermute | solution.py:66
  61.6 1.2 copy-start
  63.3 1.2 copy-start.5
  63.3 1.3 copy-start.7
  65.4 13.1 %copy-start.1 = (bf16[1024,512]{1,0:T(8,128)(2,1)S(1)}, bf16[1024,512]{1,0:T(8,128)(2,1)}, u32[]{:S(2)}) copy-start(bf16[1024,512]{1,0:T(8,128)(2,1)} %all-gather.3.cloned.1.call-done) | copy-start | bytes 3145732
  65.4 10.7 %collective-permute-start.4 = (bf16[256,896]{1,0:T(8,128)(2,1)S(1)}, bf16[256,896]{1,0:T(8,128)(2,1)S(1)}, u32[]{:S(2)}, u32[]{:S(2)}) collective-permute-start(bf16[256,896]{1,0:T(8,128)(2,1)S(1)} %shard_map.93), channel_id=1, source_target_pairs={{0,32},{1,129},{2,34},{3,131},{4,36},{5,133},{6,38},{7,135},{8,40}... | collective-permute-start | bytes 1376264 | tf_op jit(solution)/shard_map/ppermute | solution.py:66
  68.2 12.0 %collective-permute-start.5 = (bf16[256,896]{1,0:T(8,128)(2,1)S(1)}, bf16[256,896]{1,0:T(8,128)(2,1)S(1)}, u32[]{:S(2)}, u32[]{:S(2)}) collective-permute-start(bf16[256,896]{1,0:T(8,128)(2,1)S(1)} %shard_map.94), channel_id=1, source_target_pairs={{0,16},{1,65},{2,18},{3,67},{4,20},{5,69},{6,22},{7,71},{8,24},{9,... | collective-permute-start | bytes 1376264 | tf_op jit(solution)/shard_map/ppermute | solution.py:66
  68.5 11.8 %collective-permute-start.6 = (bf16[256,896]{1,0:T(8,128)(2,1)S(1)}, bf16[256,896]{1,0:T(8,128)(2,1)S(1)}, u32[]{:S(2)}, u32[]{:S(2)}) collective-permute-start(bf16[256,896]{1,0:T(8,128)(2,1)S(1)} %shard_map.95), channel_id=1, source_target_pairs={{0,48},{1,193},{2,50},{3,195},{4,52},{5,197},{6,54},{7,199},{8,56}... | collective-permute-start | bytes 1376264 | tf_op jit(solution)/shard_map/ppermute | solution.py:66
  73.0 17.2 %collective-permute-start.7 = (f32[64,1792]{1,0:T(8,128)S(1)}, f32[64,1792]{1,0:T(8,128)S(1)}, u32[]{:S(2)}, u32[]{:S(2)}) collective-permute-start(f32[64,1792]{1,0:T(8,128)S(1)} %get-tuple-element.58), channel_id=1, source_target_pairs={{0,128},{1,33},{2,130},{3,35},{4,132},{5,37},{6,134},{7,39},{8,136... | collective-permute-start | bytes 1376264 | tf_op jit(solution)/shard_map/ppermute | solution.py:70
  75.7 17.1 %collective-permute-start.8 = (f32[64,1792]{1,0:T(8,128)S(1)}, f32[64,1792]{1,0:T(8,128)S(1)}, u32[]{:S(2)}, u32[]{:S(2)}) collective-permute-start(f32[64,1792]{1,0:T(8,128)S(1)} %get-tuple-element.59), channel_id=1, source_target_pairs={{0,64},{1,17},{2,66},{3,19},{4,68},{5,21},{6,70},{7,23},{8,72},{9,... | collective-permute-start | bytes 1376264 | tf_op jit(solution)/shard_map/ppermute | solution.py:70
  76.0 16.8 %collective-permute-start.9 = (f32[64,1792]{1,0:T(8,128)S(1)}, f32[64,1792]{1,0:T(8,128)S(1)}, u32[]{:S(2)}, u32[]{:S(2)}) collective-permute-start(f32[64,1792]{1,0:T(8,128)S(1)} %get-tuple-element.60), channel_id=1, source_target_pairs={{0,192},{1,49},{2,194},{3,51},{4,196},{5,53},{6,198},{7,55},{8,200... | collective-permute-start | bytes 1376264 | tf_op jit(solution)/shard_map/ppermute | solution.py:70
  80.5 13.2 %collective-permute-start.10 = (f32[64,896]{1,0:T(8,128)S(1)}, f32[64,896]{1,0:T(8,128)S(1)}, u32[]{:S(2)}, u32[]{:S(2)}) collective-permute-start(f32[64,896]{1,0:T(8,128)S(1)} %get-tuple-element.63), channel_id=1, source_target_pairs={{0,128},{1,33},{2,130},{3,35},{4,132},{5,37},{6,134},{7,39},{8,136... | collective-permute-start | bytes 688136 | tf_op jit(solution)/shard_map/ppermute | solution.py:70
  90.2 6.4 %collective-permute-start.11 = (f32[64,896]{1,0:T(8,128)S(1)}, f32[64,896]{1,0:T(8,128)S(1)}, u32[]{:S(2)}, u32[]{:S(2)}) collective-permute-start(f32[64,896]{1,0:T(8,128)S(1)} %get-tuple-element.64), channel_id=1, source_target_pairs={{0,64},{1,17},{2,66},{3,19},{4,68},{5,21},{6,70},{7,23},{8,72},{9,... | collective-permute-start | bytes 688136 | tf_op jit(solution)/shard_map/ppermute | solution.py:70
  90.2 6.4 %collective-permute-start.12 = (f32[64,896]{1,0:T(8,128)S(1)}, f32[64,896]{1,0:T(8,128)S(1)}, u32[]{:S(2)}, u32[]{:S(2)}) collective-permute-start(f32[64,896]{1,0:T(8,128)S(1)} %get-tuple-element.65), channel_id=1, source_target_pairs={{0,192},{1,49},{2,194},{3,51},{4,196},{5,53},{6,198},{7,55},{8,200... | collective-permute-start | bytes 688136 | tf_op jit(solution)/shard_map/ppermute | solution.py:70
  93.0 6.1 %collective-permute-start.16 = (bf16[64,896]{1,0:T(8,128)(2,1)S(1)}, bf16[64,896]{1,0:T(8,128)(2,1)S(1)}, u32[]{:S(2)}, u32[]{:S(2)}) collective-permute-start(bf16[64,896]{1,0:T(8,128)(2,1)S(1)} %get-tuple-element.72.refs_0_), channel_id=1, source_target_pairs={{0,192},{1,49},{2,194},{3,51},{4,196},{5,53},{6,198},{7,55},{8,200... | collective-permute-start | bytes 344072 | tf_op jit(solution)/shard_map/ppermute | solution.py:70
  93.1 6.0 %collective-permute-start.17 = (bf16[64,896]{1,0:T(8,128)(2,1)S(1)}, bf16[64,896]{1,0:T(8,128)(2,1)S(1)}, u32[]{:S(2)}, u32[]{:S(2)}) collective-permute-start(bf16[64,896]{1,0:T(8,128)(2,1)S(1)} %get-tuple-element.72.refs_0_), channel_id=1, source_target_pairs={{0,128},{1,33},{2,130},{3,35},{4,132},{5,37},{6,134},{7,39},{8,136... | collective-permute-start | bytes 344072 | tf_op jit(solution)/shard_map/ppermute | solution.py:70
  93.7 6.2 %collective-permute-start.18 = (bf16[64,896]{1,0:T(8,128)(2,1)S(1)}, bf16[64,896]{1,0:T(8,128)(2,1)S(1)}, u32[]{:S(2)}, u32[]{:S(2)}) collective-permute-start(bf16[64,896]{1,0:T(8,128)(2,1)S(1)} %get-tuple-element.72.refs_0_), channel_id=1, source_target_pairs={{0,64},{1,17},{2,66},{3,19},{4,68},{5,21},{6,70},{7,23},{8,72},{9,... | collective-permute-start | bytes 344072 | tf_op jit(solution)/shard_map/ppermute | solution.py:70
  96.7 9.1 %collective-permute-start.13 = (bf16[64,1792]{1,0:T(8,128)(2,1)S(1)}, bf16[64,1792]{1,0:T(8,128)(2,1)S(1)}, u32[]{:S(2)}, u32[]{:S(2)}) collective-permute-start(bf16[64,1792]{1,0:T(8,128)(2,1)S(1)} %shard_map.103.refs_0_), channel_id=1, source_target_pairs={{0,192},{1,49},{2,194},{3,51},{4,196},{5,53},{6,198},{7,55},{8,200... | collective-permute-start | bytes 688136 | tf_op jit(solution)/shard_map/ppermute | solution.py:70
  99.9 19.3 %collective-permute-start.19 = (bf16[256,896]{1,0:T(8,128)(2,1)S(1)}, bf16[256,896]{1,0:T(8,128)(2,1)S(1)}, u32[]{:S(2)}, u32[]{:S(2)}) collective-permute-start(bf16[256,896]{1,0:T(8,128)(2,1)S(1)} %shard_map.105.a), channel_id=1, source_target_pairs={{0,48},{1,193},{2,50},{3,195},{4,52},{5,197},{6,54},{7,199},{8,56}... | collective-permute-start | bytes 1376264 | tf_op jit(solution)/shard_map/ppermute | solution.py:66
  101.6 17.6 %collective-permute-start.20 = (bf16[256,896]{1,0:T(8,128)(2,1)S(1)}, bf16[256,896]{1,0:T(8,128)(2,1)S(1)}, u32[]{:S(2)}, u32[]{:S(2)}) collective-permute-start(bf16[256,896]{1,0:T(8,128)(2,1)S(1)} %shard_map.105.a), channel_id=1, source_target_pairs={{0,32},{1,129},{2,34},{3,131},{4,36},{5,133},{6,38},{7,135},{8,40}... | collective-permute-start | bytes 1376264 | tf_op jit(solution)/shard_map/ppermute | solution.py:66
  102.7 16.5 %collective-permute-start.21 = (bf16[256,896]{1,0:T(8,128)(2,1)S(1)}, bf16[256,896]{1,0:T(8,128)(2,1)S(1)}, u32[]{:S(2)}, u32[]{:S(2)}) collective-permute-start(bf16[256,896]{1,0:T(8,128)(2,1)S(1)} %shard_map.105.a), channel_id=1, source_target_pairs={{0,16},{1,65},{2,18},{3,67},{4,20},{5,69},{6,22},{7,71},{8,24},{9,... | collective-permute-start | bytes 1376264 | tf_op jit(solution)/shard_map/ppermute | solution.py:66
  103.5 6.4 %collective-permute-start.14 = (bf16[64,1792]{1,0:T(8,128)(2,1)S(1)}, bf16[64,1792]{1,0:T(8,128)(2,1)S(1)}, u32[]{:S(2)}, u32[]{:S(2)}) collective-permute-start(bf16[64,1792]{1,0:T(8,128)(2,1)S(1)} %shard_map.103.refs_0_), channel_id=1, source_target_pairs={{0,128},{1,33},{2,130},{3,35},{4,132},{5,37},{6,134},{7,39},{8,136... | collective-permute-start | bytes 688136 | tf_op jit(solution)/shard_map/ppermute | solution.py:70
  105.7 12.5 %collective-permute-start.15 = (bf16[64,1792]{1,0:T(8,128)(2,1)S(1)}, bf16[64,1792]{1,0:T(8,128)(2,1)S(1)}, u32[]{:S(2)}, u32[]{:S(2)}) collective-permute-start(bf16[64,1792]{1,0:T(8,128)(2,1)S(1)} %shard_map.103.refs_0_), channel_id=1, source_target_pairs={{0,64},{1,17},{2,66},{3,19},{4,68},{5,21},{6,70},{7,23},{8,72},{9,... | collective-permute-start | bytes 688136 | tf_op jit(solution)/shard_map/ppermute | solution.py:70
  121.3 11.9 %collective-permute-start.22 = (f32[8,64,512]{2,1,0:T(8,128)S(1)}, f32[8,64,512]{2,1,0:T(8,128)S(1)}, u32[]{:S(2)}, u32[]{:S(2)}) collective-permute-start(f32[8,64,512]{2,1,0:T(8,128)S(1)} %get-tuple-element.75), channel_id=1, source_target_pairs={{0,1},{1,0},{2,3},{3,2},{4,5},{5,4},{6,7},{7,6},{8,9},{9,8},{10,11... | collective-permute-start | bytes 3145736 | tf_op jit(solution)/shard_map/ppermute | solution.py:74
  128.4 22.3 %collective-permute-start.23 = (bf16[256,1792]{1,0:T(8,128)(2,1)}, bf16[256,1792]{1,0:T(8,128)(2,1)S(1)}, u32[]{:S(2)}, u32[]{:S(2)}) collective-permute-start(bf16[256,1792]{1,0:T(8,128)(2,1)} %shard_map.104.a), channel_id=1, source_target_pairs={{0,48},{1,193},{2,50},{3,195},{4,52},{5,197},{6,54},{7,199},{8,56}... | collective-permute-start | bytes 2752520 | tf_op jit(solution)/shard_map/ppermute | solution.py:66
  130.2 20.5 %collective-permute-start.24 = (bf16[256,1792]{1,0:T(8,128)(2,1)}, bf16[256,1792]{1,0:T(8,128)(2,1)}, u32[]{:S(2)}, u32[]{:S(2)}) collective-permute-start(bf16[256,1792]{1,0:T(8,128)(2,1)} %shard_map.104.a), channel_id=1, source_target_pairs={{0,32},{1,129},{2,34},{3,131},{4,36},{5,133},{6,38},{7,135},{8,40}... | collective-permute-start | bytes 2752520 | tf_op jit(solution)/shard_map/ppermute | solution.py:66
  130.2 23.9 %collective-permute-start.25 = (bf16[256,1792]{1,0:T(8,128)(2,1)}, bf16[256,1792]{1,0:T(8,128)(2,1)}, u32[]{:S(2)}, u32[]{:S(2)}) collective-permute-start(bf16[256,1792]{1,0:T(8,128)(2,1)} %shard_map.104.a), channel_id=1, source_target_pairs={{0,16},{1,65},{2,18},{3,67},{4,20},{5,69},{6,22},{7,71},{8,24},{9,... | collective-permute-start | bytes 2752520 | tf_op jit(solution)/shard_map/ppermute | solution.py:66
  158.7 0.9 copy-start.9
  159.6 8.4 %copy-start.8 = (bf16[8,64,512]{2,1,0:T(8,128)(2,1)S(1)}, bf16[8,64,512]{2,1,0:T(8,128)(2,1)}, u32[]{:S(2)}) copy-start(bf16[8,64,512]{2,1,0:T(8,128)(2,1)} %copy-done.6) | copy-start | bytes 1572868
  159.6 8.4 %copy-start.10 = (bf16[256,1792]{1,0:T(8,128)(2,1)S(1)}, bf16[256,1792]{1,0:T(8,128)(2,1)}, u32[]{:S(2)}) copy-start(bf16[256,1792]{1,0:T(8,128)(2,1)} %copy-done.9) | copy-start | bytes 2752516
  159.6 3.4 %collective-permute-start.26 = (f32[8,64,512]{2,1,0:T(8,128)S(1)}, f32[8,64,512]{2,1,0:T(8,128)S(1)}, u32[]{:S(2)}, u32[]{:S(2)}) collective-permute-start(f32[8,64,512]{2,1,0:T(8,128)S(1)} %get-tuple-element.78), channel_id=1, source_target_pairs={{0,1},{1,0},{2,3},{3,2},{4,5},{5,4},{6,7},{7,6},{8,9},{9,8},{10,11... | collective-permute-start | bytes 3145736 | tf_op jit(solution)/shard_map/ppermute | solution.py:74
  163.9 22.0 %all-to-all-start.1 = ((bf16[8,64,512]{2,1,0:T(8,128)(2,1)}), bf16[8,64,512]{2,1,0:T(8,128)(2,1)S(1)}, u32[]{:S(2)}, u32[]{:S(2)}) async-start(bf16[8,64,512]{2,1,0:T(8,128)(2,1)} %get-tuple-element.80), calls=%async_computation.1 | async-start | bytes 1048576 | tf_op jit(solution)/shard_map/all_to_all | solution.py:241
  186.0 0.9 copy-start.11
Sparse Core Ops, SparseCore 0:
  20.6 40.9 all-gather.2
  134.5 32.7 reduce-scatter.1
where the time goes:
time: 195 us; the launch traced here: 194 us
  waiting for transfers between devices  81.4 us (42%)
  starting transfers between devices  63.3 us (32%)
  Pallas kernels  28 us (14%)
  between operations  14.2 us (7%)
  local copies, waits for them, and re-layouts  6.39 us (3%)
    pallas_call x21, Pallas kernels, call(): pl.pallas_call(kernel, out_shape=out, compiler_params=pltpu.CompilerParam...  28 us
    ppermute x12, starting transfers between devices, send_q(): return lax.ppermute(a, BOTH, along(False, k % RING))  24.4 us
    ppermute x12, waiting for transfers between devices, send_p(): return lax.ppermute(a, BOTH, along(True, k % RING))  20.6 us
    all_to_all x1, waiting for transfers between devices, gather_z(): lax.all_to_all(copies, 'tensor', 0, 0, tiled=True, axis_index_groups=CORES)  17.2 us
    ppermute x12, starting transfers between devices, send_p(): return lax.ppermute(a, BOTH, along(True, k % RING))  17 us
    ppermute x12, waiting for transfers between devices, send_q(): return lax.ppermute(a, BOTH, along(False, k % RING))  15 us
    all_to_all x1, waiting for transfers between devices, reduce_z(): lax.all_to_all(parts, 'tensor', 0, 0, tiled=True, axis_index_groups=CORES)  12.2 us
    all_gather x1, waiting for transfers between devices, body(): grads = lax.all_gather(out_grad, 'tensor', axis=0)  11.9 us
  transfers between devices with their start and end apart: 31, of which 13 were waited for; matrix products, arithmetic and copies ran while one was open for 1% of the time, Pallas kernels for 13%

commit v1 on v0

--- a/solution.py
+++ b/solution.py
@@ -32,15 +32,17 @@
     return (tile % 2) ^ core, tile // 2
 
 
-def call(kernel, out, *args, flops=0):
-    outs = out if isinstance(out, list) else [out]
-    size = sum(a.size * a.dtype.itemsize for a in (*args, *outs))
+def call(kernel, out, *args, after=()):
+    def run(*refs):
+        kernel(*refs[: len(args)], *refs[len(args) + len(after) :])
+
     return pl.pallas_call(
-        kernel,
+        run,
+        in_specs=[pl.BlockSpec(memory_space=pltpu.VMEM)] * len(args) + [pl.BlockSpec(memory_space=pl.ANY)] * len(after),
         out_shape=out,
         compiler_params=pltpu.CompilerParams(vmem_limit_bytes=24 * MIB),
         cost_estimate=pl.CostEstimate(flops=0, bytes_accessed=0, transcendentals=0),
-    )(*args)
+    )(*args, *after)
 
 
 def shape(dims, dtype):
@@ -86,14 +88,14 @@
     return jnp.concatenate(tiles, 0)
 
 
-def join(*tiles):
+def join(*tiles, after=()):
     rows, columns = tiles[0].shape
 
     def kernel(*refs):
         for j, ref in enumerate(refs[:-1]):
             refs[-1][pl.ds(j * rows, rows)] = ref[...]
 
-    return call(kernel, shape((len(tiles) * rows, columns), tiles[0].dtype), *tiles)
+    return call(kernel, shape((len(tiles) * rows, columns), tiles[0].dtype), *tiles, after=after)
 
 
 def gather_z(a):
@@ -102,7 +104,7 @@
     return mine, send_core(mine)
 
 
-def project(mine, other, gate_weight, up_weight, i, dtype):
+def project(mine, other, gate_weight, up_weight, i, dtype, after=()):
     width, hidden = gate_weight.shape
     rows = RING * mine.shape[1]
 
@@ -111,9 +113,7 @@
         out_ref[:, :hidden] = dot(block, gate_ref[...], (1, 0)).astype(dtype)
         out_ref[:, hidden:] = dot(block, up_ref[...], (1, 0)).astype(dtype)
 
-    return call(
-        kernel, shape((rows, 2 * hidden), dtype), mine, other, gate_weight, up_weight, flops=4 * rows * width * hidden
-    )
+    return call(kernel, shape((rows, 2 * hidden), dtype), mine, other, gate_weight, up_weight, after=after)
 
 
 def grad_block(grads, i):
@@ -132,10 +132,10 @@
     def kernel(grads_ref, down_ref, out_ref):
         out_ref[...] = dot(grad_block(grads_ref, i), down_ref[...], (1, 1)).astype(dtype)
 
-    return call(kernel, shape((rows, hidden), dtype), grads, down_weight, flops=2 * rows * width * hidden)
-
-
-def add_blocks(own, parts):
+    return call(kernel, shape((rows, hidden), dtype), grads, down_weight)
+
+
+def add_blocks(own, parts, after=()):
     rows, columns = own.shape
     tile = rows // RING
 
@@ -144,14 +144,14 @@
             at = pl.ds(j * tile, tile)
             out[...] = own_ref[at] + (a_ref[at].astype(F32) + b_ref[at].astype(F32) + c_ref[at].astype(F32))
 
-    return call(kernel, [shape((tile, columns), F32)] * RING, own, *parts)
+    return call(kernel, [shape((tile, columns), F32)] * RING, own, *parts, after=after)
 
 
 def spread(tiles):
     return [tiles[0]] + [send_q(tiles[j], j) for j in ORDER]
 
 
-def activate(terms):
+def activate(terms, after=()):
     rows, columns = terms[0].shape
     hidden = columns // 2
 
@@ -166,9 +166,8 @@
         up_factor[...] = activated
         gate_factor[...] = up * s * (1.0 + gate * (1.0 - s))
 
-    return call(
-        kernel, [shape((rows, hidden), BF16), shape((rows, hidden), F32), shape((rows, hidden), F32)], *terms
-    )
+    outs = [shape((rows, hidden), BF16), shape((rows, hidden), F32), shape((rows, hidden), F32)]
+    return call(kernel, outs, *terms, after=after)
 
 
 def activate_grad(terms, up_factor, gate_factor):
@@ -206,7 +205,7 @@
         store_tile(mine, other, *tile_at(i, j), result[j * tile : (j + 1) * tile])
 
 
-def back(blocks, weights):
+def back(blocks, weights, after=()):
     hidden, width = weights.shape
     rows = blocks[0].shape[0]
 
@@ -215,7 +214,22 @@
             store_tiles(mine, other, i, dot(block[...], weights_ref[...], (1, 0)))
 
     half = shape((DEPTH, rows // RING, width), F32)
-    return call(kernel, [half, half], *blocks, weights, flops=2 * RING * rows * width * hidden)
+    return call(kernel, [half, half], *blocks, weights, after=after)
+
+
+def back_hidden(blocks, weights, after=()):
+    width = weights.shape[1]
+    rows = blocks[0].shape[0]
+    tile = rows // RING
+
+    def kernel(a, b, c, d, weights_ref, out):
+        for i, block in enumerate((a, b, c, d)):
+            result = dot(block[...], weights_ref[...], (1, 0))
+            for j in range(RING):
+                foreign, z = tile_at(i, j)
+                out[z, pl.ds(pl.multiple_of(foreign * tile, tile), tile)] = result[j * tile : (j + 1) * tile]
+
+    return call(kernel, shape((DEPTH, 2 * tile, width), F32), *blocks, weights, after=after)
 
 
 def transposed(gate_weight, up_weight):
@@ -240,14 +254,14 @@
     own, parts = call(split, [shape((rows, width), F32), shape(mine.shape, BF16)], mine, arrived)
     parts = lax.all_to_all(parts, "tensor", 0, 0, tiled=True, axis_index_groups=CORES)
 
-    def add(own_ref, parts_ref, done_ref, out, done_out):
+    def add(own_ref, parts_ref, done_ref, more_ref, out, done_out):
         total = own_ref[...]
         for k in range(depth):
             total += jnp.where(place()[2] == k, 0.0, parts_ref[k].astype(F32))
         out[...] = total.astype(BF16)
-        done_out[...] = done_ref[...].astype(BF16)
-
-    return call(add, [shape((rows, width), BF16)] * 2, own, parts, done)
+        done_out[...] = (done_ref[...] + more_ref[...]).astype(BF16)
+
+    return call(add, [shape((rows, width), BF16)] * 2, own, parts, *done)
 
 
 def hidden_weight_grad(blocks, grads, factor):
@@ -263,7 +277,7 @@
                 out_ref[...] += part
 
     return call(
-        kernel, shape((hidden, width), F32), *blocks, grads, flops=2 * RING * rows * width * hidden
+        kernel, shape((hidden, width), F32), *blocks, grads
     )
 
 
@@ -284,7 +298,7 @@
                 up_ref[...] += up
 
     out = shape((width, hidden), F32)
-    return call(kernel, [out, out], *blocks, mine, other, flops=4 * RING * rows * width * hidden)
+    return call(kernel, [out, out], *blocks, mine, other)
 
 
 def body(tokens, gate_weight, up_weight, down_weight, out_grad):
@@ -292,35 +306,28 @@
     rows = shard * 2 * DEPTH
     factor = 1.0 / math.sqrt(rows)
 
-    rows_of = list(gather_z(tokens))
+    rows_of = gather_z(tokens)
     grads = lax.all_gather(out_grad, "tensor", axis=0)
     blocks = {i: project(*rows_of, gate_weight, up_weight, i, BF16) for i in ORDER}
-    rows_of[0], grads = lax.optimization_barrier((rows_of[0], grads))
-    blocks[0] = project(*rows_of, gate_weight, up_weight, 0, F32)
+    blocks[0] = project(*rows_of, gate_weight, up_weight, 0, F32, after=[grads])
     grad_blocks = {i: project_grad(grads, down_weight, i, BF16 if i else F32) for i in (*ORDER, 0)}
 
-    blocks[0], *sent = lax.optimization_barrier((blocks[0], *(grad_blocks[i] for i in ORDER)))
-    grad_blocks.update(zip(ORDER, sent))
-    tiles = add_blocks(blocks[0], [send_p(blocks[i], i) for i in ORDER])
-    grad_tiles = list(add_blocks(grad_blocks[0], [send_p(grad_blocks[i], i) for i in ORDER]))
-    terms = spread(tiles)
-    terms[0], *grad_tiles = lax.optimization_barrier((terms[0], *grad_tiles))
-    hidden, up_factor, gate_factor = activate(terms)
+    sent = [grad_blocks[i] for i in ORDER]
+    tiles = add_blocks(blocks[0], [send_p(blocks[i], i) for i in ORDER], after=sent)
+    grad_tiles = add_blocks(grad_blocks[0], [send_p(grad_blocks[i], i) for i in ORDER])
+    hidden, up_factor, gate_factor = activate(spread(tiles), after=grad_tiles[:1])
     near = gather_q(hidden)
     grad_terms = spread(grad_tiles)
-    near[0], *grad_terms = lax.optimization_barrier((near[0], *grad_terms))
-    grad_near = gather_q(activate_grad(grad_terms, up_factor, gate_factor))
-    hidden_blocks = gather_p(join(*near))
-    grad_block = join(*grad_near)
-    hidden_blocks[0], _ = lax.optimization_barrier((hidden_blocks[0], grad_block))
+    grad_block = join(*gather_q(activate_grad(grad_terms, up_factor, gate_factor)))
+    hidden_blocks = gather_p(join(*near, after=grad_terms[1:]))
     grad_blocks = gather_p(grad_block)
 
-    keep, give = back(hidden_blocks, down_weight)
-    half = (keep + send_core(give)).reshape(rows // 2, width)
+    partial = back_hidden(hidden_blocks, down_weight, after=[grad_block])
     down_weight_grad = hidden_weight_grad(hidden_blocks, grads, factor)
-    grad_blocks[0], down_weight_grad, half = lax.optimization_barrier((grad_blocks[0], down_weight_grad, half))
-    ffn_output = lax.psum_scatter(half, "tensor", scatter_dimension=0, tiled=True, axis_index_groups=CORES)
-    input_grad, ffn_output = reduce_z(*back(grad_blocks, transposed(gate_weight, up_weight)), ffn_output)
+    partial = partial.reshape(rows, width)
+    both = lax.psum_scatter(partial, "tensor", scatter_dimension=0, tiled=True, axis_index_groups=CORES)
+    done = [both[:shard], send_core(both[shard:])]
+    input_grad, ffn_output = reduce_z(*back(grad_blocks, transposed(gate_weight, up_weight), after=[down_weight_grad]), done)
     gate_weight_grad, up_weight_grad = token_weight_grads(grad_blocks, *rows_of, factor)
     return ffn_output, input_grad, gate_weight_grad, up_weight_grad, down_weight_grad
 

time: 195 us -> 191 us (0.979)
  local copies, waits for them, and re-layouts: 6.39 us -> 12.7 us
  waiting for transfers between devices: 81.4 us -> 75.6 us
  Pallas kernels: 28 us -> 23.9 us
    all_to_all x1, waiting for transfers between devices: 12.2 us -> 6.27 us  [reduce_z(): lax.all_to_all(parts, 'tensor', 0, 0, tiled=True, axis_index_groups=CORES)]
    unnamed x24 -> x58, local copies, waits for them, and re-layouts: 4.64 us -> 9.98 us
    pallas_call x21, Pallas kernels: 28 us -> 23.9 us  [call(): pl.pallas_call(run, in_specs=[pl.BlockSpec(memory_space=pltpu.VMEM)] * le...]
  transfers between devices with their start and end apart: 31 -> 31, of which waited for: 13 -> 12; matrix products, arithmetic and copies ran while one was open for 1% -> 1% of each run, Pallas kernels for 13% -> 11%
where the time goes in v1:
time: 191 us
  waiting for transfers between devices  75.6 us (40%)
  starting transfers between devices  63.8 us (33%)
  Pallas kernels  23.9 us (13%)
  between operations  14.4 us (8%)
  local copies, waits for them, and re-layouts  12.7 us (7%)
    pallas_call x21, Pallas kernels, call(): pl.pallas_call(run, in_specs=[pl.BlockSpec(memory_space=pltpu.VMEM)] * le...  23.9 us
    ppermute x12, starting transfers between devices, send_q(): return lax.ppermute(a, BOTH, along(False, k % RING))  22.9 us
    ppermute x12, waiting for transfers between devices, send_p(): return lax.ppermute(a, BOTH, along(True, k % RING))  20.2 us
    ppermute x12, starting transfers between devices, send_p(): return lax.ppermute(a, BOTH, along(True, k % RING))  18.6 us
    all_to_all x1, waiting for transfers between devices, gather_z(): lax.all_to_all(copies, 'tensor', 0, 0, tiled=True, axis_index_groups=CORES)  17.2 us
    ppermute x12, waiting for transfers between devices, send_q(): return lax.ppermute(a, BOTH, along(False, k % RING))  15.5 us
    all_gather x1, waiting for transfers between devices, body(): grads = lax.all_gather(out_grad, 'tensor', axis=0)  11.9 us
    unnamed x58, local copies, waits for them, and re-layouts  9.98 us
  transfers between devices with their start and end apart: 31, of which 12 were waited for; matrix products, arithmetic and copies ran while one was open for 1% of the time, Pallas kernels for 11%

profile of v1, /device:TPU:1, one launch (start us, length us, event | category | flops | bytes accessed | tf_op | source)
XLA Modules:
  0.0 190.5 jit_solution(12135351084783783823)
XLA Ops:
  7.2 1.8 broadcast_in_dim.3
  8.9 9.0 %all-to-all-start = ((bf16[8,64,512]{2,1,0:T(8,128)(2,1)}), bf16[8,64,512]{2,1,0:T(8,128)(2,1)S(1)}, u32[]{:S(2)}, u32[]{:S(2)}) async-start(bf16[8,64,512]{2,1,0:T(8,128)(2,1)} %broadcast_in_dim.3), calls=%async_computation | async-start | bytes 1048576 | tf_op jit(solution)/shard_map/all_to_all | solution.py:103
  18.7 17.2 %all-to-all-done.refs_0_.refs_4_ = bf16[8,64,512]{2,1,0:T(8,128)(2,1)S(1)} async-done(((bf16[8,64,512]{2,1,0:T(8,128)(2,1)}), bf16[8,64,512]{2,1,0:T(8,128)(2,1)S(1)}, u32[]{:S(2)}, u32[]{:S(2)}) %all-to-all-start) | async-done | bytes 524320 | tf_op jit(solution)/shard_map/all_to_all | solution.py:103
  36.4 1.5 collective-permute-done.6.refs_1_.refs_5_
  37.9 1.2 copy-done.4
  39.1 1.6 shard_map.98
  40.8 2.9 %collective-permute-start.7 = (bf16[256,1792]{1,0:T(8,128)(2,1)}, bf16[256,1792]{1,0:T(8,128)(2,1)}, u32[]{:S(2)}, u32[]{:S(2)}) collective-permute-start(bf16[256,1792]{1,0:T(8,128)(2,1)} %shard_map.98), channel_id=1, source_target_pairs={{0,32},{1,129},{2,34},{3,131},{4,36},{5,133},{6,38},{7,135},{8,40}... | collective-permute-start | bytes 2752520 | tf_op jit(solution)/shard_map/ppermute | solution.py:68
  43.7 1.6 shard_map.99
  45.7 1.6 shard_map.100
  47.4 2.3 %collective-permute-start.9 = (bf16[256,1792]{1,0:T(8,128)(2,1)}, bf16[256,1792]{1,0:T(8,128)(2,1)}, u32[]{:S(2)}, u32[]{:S(2)}) collective-permute-start(bf16[256,1792]{1,0:T(8,128)(2,1)} %shard_map.100), channel_id=1, source_target_pairs={{0,48},{1,193},{2,50},{3,195},{4,52},{5,197},{6,54},{7,199},{8,56}... | collective-permute-start | bytes 2752520 | tf_op jit(solution)/shard_map/ppermute | solution.py:68
  49.7 11.9 %all-gather.3.cloned.1.call-done = bf16[1024,512]{1,0:T(8,128)(2,1)} async-done(((bf16[64,512]{1,0:T(8,128)(2,1)}), bf16[1024,512]{1,0:T(8,128)(2,1)}) %all-gather.3.cloned.1.call-update) | async-done | bytes 1048592 | tf_op jit(solution)/shard_map/all_gather | solution.py:310
  61.6 1.2 copy-done
  63.3 2.8 %collective-permute-start = (bf16[256,896]{1,0:T(8,128)(2,1)S(1)}, bf16[256,896]{1,0:T(8,128)(2,1)S(1)}, u32[]{:S(2)}, u32[]{:S(2)}) collective-permute-start(bf16[256,896]{1,0:T(8,128)(2,1)S(1)} %shard_map.93.refs_4_), channel_id=1, source_target_pairs={{0,32},{1,129},{2,34},{3,131},{4,36},{5,133},{6,38},{7,135},{8,40}... | collective-permute-start | bytes 1376264 | tf_op jit(solution)/shard_map/ppermute | solution.py:68
  67.5 2.4 %collective-permute-start.2 = (bf16[256,896]{1,0:T(8,128)(2,1)S(1)}, bf16[256,896]{1,0:T(8,128)(2,1)S(1)}, u32[]{:S(2)}, u32[]{:S(2)}) collective-permute-start(bf16[256,896]{1,0:T(8,128)(2,1)S(1)} %shard_map.95.refs_6_), channel_id=1, source_target_pairs={{0,48},{1,193},{2,50},{3,195},{4,52},{5,197},{6,54},{7,199},{8,56}... | collective-permute-start | bytes 1376264 | tf_op jit(solution)/shard_map/ppermute | solution.py:68
  70.6 2.2 %shard_map.101 = (f32[64,1792]{1,0:T(8,128)S(1)}, f32[64,1792]{1,0:T(8,128)S(1)}, f32[64,1792]{1,0:T(8,128)S(1)}, f32[64,1792]{1,0:T(8,128)S(1)}) custom-call(f32[256,1792]{1,0:T(8,128)S(1)} %shard_map.97.refs_0_, bf16[256,1792]{1,0:T(8,128)(2,1)} %collective-permute-done.7.refs_1_, bf16[256,1792]{1,0:T(8,128)(2,1)} %collective-permute-done.8.refs_2_, ...), custom_call_target="tpu_custom_call" | custom-call | tf_op jit(solution)/shard_map/pallas_call | solution.py:39
  72.8 2.8 %collective-permute-start.10 = (f32[64,1792]{1,0:T(8,128)S(1)}, f32[64,1792]{1,0:T(8,128)S(1)}, u32[]{:S(2)}, u32[]{:S(2)}) collective-permute-start(f32[64,1792]{1,0:T(8,128)S(1)} %get-tuple-element.29), channel_id=1, source_target_pairs={{0,128},{1,33},{2,130},{3,35},{4,132},{5,37},{6,134},{7,39},{8,136... | collective-permute-start | bytes 1376264 | tf_op jit(solution)/shard_map/ppermute | solution.py:72
  75.9 2.4 %collective-permute-start.12 = (f32[64,1792]{1,0:T(8,128)S(1)}, f32[64,1792]{1,0:T(8,128)S(1)}, u32[]{:S(2)}, u32[]{:S(2)}) collective-permute-start(f32[64,1792]{1,0:T(8,128)S(1)} %get-tuple-element.31), channel_id=1, source_target_pairs={{0,192},{1,49},{2,194},{3,51},{4,196},{5,53},{6,198},{7,55},{8,200... | collective-permute-start | bytes 1376264 | tf_op jit(solution)/shard_map/ppermute | solution.py:72
  78.9 7.3 %collective-permute-start.3 = (f32[64,896]{1,0:T(8,128)S(1)}, f32[64,896]{1,0:T(8,128)S(1)}, u32[]{:S(2)}, u32[]{:S(2)}) collective-permute-start(f32[64,896]{1,0:T(8,128)S(1)} %get-tuple-element.25), channel_id=1, source_target_pairs={{0,128},{1,33},{2,130},{3,35},{4,132},{5,37},{6,134},{7,39},{8,136... | collective-permute-start | bytes 688136 | tf_op jit(solution)/shard_map/ppermute | solution.py:72
  86.2 2.7 %collective-permute-start.5 = (f32[64,896]{1,0:T(8,128)S(1)}, f32[64,896]{1,0:T(8,128)S(1)}, u32[]{:S(2)}, u32[]{:S(2)}) collective-permute-start(f32[64,896]{1,0:T(8,128)S(1)} %get-tuple-element.27), channel_id=1, source_target_pairs={{0,192},{1,49},{2,194},{3,51},{4,196},{5,53},{6,198},{7,55},{8,200... | collective-permute-start | bytes 688136 | tf_op jit(solution)/shard_map/ppermute | solution.py:72
  89.1 1.3 collective-permute-start.19
  91.6 1.4 collective-permute-done.4.refs_2_.refs_5_
  93.1 2.5 %collective-permute-start.13 = (bf16[64,1792]{1,0:T(8,128)(2,1)S(1)}, bf16[64,1792]{1,0:T(8,128)(2,1)S(1)}, u32[]{:S(2)}, u32[]{:S(2)}) collective-permute-start(bf16[64,1792]{1,0:T(8,128)(2,1)S(1)} %shard_map.103.refs_0_), channel_id=1, source_target_pairs={{0,192},{1,49},{2,194},{3,51},{4,196},{5,53},{6,198},{7,55},{8,200... | collective-permute-start | bytes 688136 | tf_op jit(solution)/shard_map/ppermute | solution.py:72
  95.6 1.1 collective-permute-done.21.refs_3_
  96.8 2.8 %collective-permute-start.22 = (bf16[256,896]{1,0:T(8,128)(2,1)S(1)}, bf16[256,896]{1,0:T(8,128)(2,1)S(1)}, u32[]{:S(2)}, u32[]{:S(2)}) collective-permute-start(bf16[256,896]{1,0:T(8,128)(2,1)S(1)} %shard_map.106.refs_0_), channel_id=1, source_target_pairs={{0,48},{1,193},{2,50},{3,195},{4,52},{5,197},{6,54},{7,199},{8,56}... | collective-permute-start | bytes 1376264 | tf_op jit(solution)/shard_map/ppermute | solution.py:68
  99.6 1.2 collective-permute-start.23
  101.6 2.2 %collective-permute-start.14 = (bf16[64,1792]{1,0:T(8,128)(2,1)S(1)}, bf16[64,1792]{1,0:T(8,128)(2,1)S(1)}, u32[]{:S(2)}, u32[]{:S(2)}) collective-permute-start(bf16[64,1792]{1,0:T(8,128)(2,1)S(1)} %shard_map.103.refs_0_), channel_id=1, source_target_pairs={{0,128},{1,33},{2,130},{3,35},{4,132},{5,37},{6,134},{7,39},{8,136... | collective-permute-start | bytes 688136 | tf_op jit(solution)/shard_map/ppermute | solution.py:72
  104.2 3.9 %collective-permute-done.14.refs_2_ = bf16[64,1792]{1,0:T(8,128)(2,1)S(1)} collective-permute-done((bf16[64,1792]{1,0:T(8,128)(2,1)S(1)}, bf16[64,1792]{1,0:T(8,128)(2,1)S(1)}, u32[]{:S(2)}, u32[]{:S(2)}) %collective-permute-start.14) | collective-permute-done | bytes 229408 | tf_op jit(solution)/shard_map/ppermute | solution.py:72
  108.0 9.0 %collective-permute-done.15.refs_3_ = bf16[64,1792]{1,0:T(8,128)(2,1)S(1)} collective-permute-done((bf16[64,1792]{1,0:T(8,128)(2,1)S(1)}, bf16[64,1792]{1,0:T(8,128)(2,1)S(1)}, u32[]{:S(2)}, u32[]{:S(2)}) %collective-permute-start.15) | collective-permute-done | bytes 229408 | tf_op jit(solution)/shard_map/ppermute | solution.py:72
  117.2 1.2 shard_map.110
  118.5 1.3 copy-done.13
  119.9 1.6 collective-permute-start.16
  123.1 2.4 %shard_map.107.refs_5_ = f32[896,512]{1,0:T(8,128)} custom-call(bf16[256,896]{1,0:T(8,128)(2,1)S(1)} %copy-done.16, bf16[256,896]{1,0:T(8,128)(2,1)S(1)} %copy-done.24, bf16[256,896]{1,0:T(8,128)(2,1)S(1)} %copy-done.26, bf16[256,896]{1,0:T(8,128)(2,1)S(1)} %copy-done.28, bf16[16,64,512]{2,1,0:T(8,128)(2,1)S(1)} %bitcast.7), custom_call_target="tpu_custom_call" | custom-call | tf_op jit(solution)/shard_map/pallas_call | solution.py:39
  125.4 16.6 %collective-permute-done.16.refs_1_ = bf16[256,1792]{1,0:T(8,128)(2,1)S(1)} collective-permute-done((bf16[256,1792]{1,0:T(8,128)(2,1)}, bf16[256,1792]{1,0:T(8,128)(2,1)S(1)}, u32[]{:S(2)}, u32[]{:S(2)}) %collective-permute-start.16) | collective-permute-done | bytes 917536 | tf_op jit(solution)/shard_map/ppermute | solution.py:68
  142.0 3.6 %collective-permute-done.18.refs_3_ = bf16[256,1792]{1,0:T(8,128)(2,1)S(1)} collective-permute-done((bf16[256,1792]{1,0:T(8,128)(2,1)}, bf16[256,1792]{1,0:T(8,128)(2,1)S(1)}, u32[]{:S(2)}, u32[]{:S(2)}) %collective-permute-start.18) | collective-permute-done | bytes 917536 | tf_op jit(solution)/shard_map/ppermute | solution.py:68
  145.6 1.5 copy-done.14
  147.1 2.8 %shard_map.108 = (f32[8,64,512]{2,1,0:T(8,128)S(1)}, f32[8,64,512]{2,1,0:T(8,128)S(1)}) custom-call(bf16[256,1792]{1,0:T(8,128)(2,1)S(1)} %copy-done.8, bf16[256,1792]{1,0:T(8,128)(2,1)S(1)} %collective-permute-done.16.refs_1_, bf16[256,1792]{1,0:T(8,128)(2,1)S(1)} %collective-permute-done.17.refs_2_, bf16[256,1792]{1,0:T(8,128)(2,1)S(1)} %collective-permute-done.18.refs_3_, ...), custom_call_target="tpu_custom_call" | custom-call | tf_op jit(solution)/shard_map/pallas_call | solution.py:39
  150.0 6.3 %collective-permute-start.25 = (f32[8,64,512]{2,1,0:T(8,128)S(1)}, f32[8,64,512]{2,1,0:T(8,128)S(1)}, u32[]{:S(2)}, u32[]{:S(2)}) collective-permute-start(f32[8,64,512]{2,1,0:T(8,128)S(1)} %get-tuple-element.36), channel_id=1, source_target_pairs={{0,1},{1,0},{2,3},{3,2},{4,5},{5,4},{6,7},{7,6},{8,9},{9,8},{10,11... | collective-permute-start | bytes 3145736 | tf_op jit(solution)/shard_map/ppermute | solution.py:76
  156.3 2.3 %collective-permute-done.25.refs_1_ = f32[8,64,512]{2,1,0:T(8,128)S(1)} collective-permute-done((f32[8,64,512]{2,1,0:T(8,128)S(1)}, f32[8,64,512]{2,1,0:T(8,128)S(1)}, u32[]{:S(2)}, u32[]{:S(2)}) %collective-permute-start.25) | collective-permute-done | bytes 1048608 | tf_op jit(solution)/shard_map/ppermute | solution.py:76
  159.5 4.3 %all-to-all-start.1 = ((bf16[8,64,512]{2,1,0:T(8,128)(2,1)}), bf16[8,64,512]{2,1,0:T(8,128)(2,1)}, u32[]{:S(2)}, u32[]{:S(2)}) async-start(bf16[8,64,512]{2,1,0:T(8,128)(2,1)} %get-tuple-element.38), calls=%async_computation.1 | async-start | bytes 1048576 | tf_op jit(solution)/shard_map/all_to_all | solution.py:255
  163.8 1.0 fusion
  164.8 2.1 %collective-permute-start.26 = (f32[64,512]{1,0:T(8,128)S(1)}, f32[64,512]{1,0:T(8,128)}, u32[]{:S(2)}, u32[]{:S(2)}) collective-permute-start(f32[64,512]{1,0:T(8,128)S(1)} %get-tuple-element.43), channel_id=1, source_target_pairs={{0,1},{1,0},{2,3},{3,2},{4,5},{5,4},{6,7},{7,6},{8,9},{9,8},{10,11... | collective-permute-start | bytes 393224 | tf_op jit(solution)/shard_map/ppermute | solution.py:76
  167.0 1.2 copy-done.9
  168.2 1.0 copy-done.12
  169.2 1.2 copy-done.20
  170.4 1.2 copy-done.22
  171.6 4.0 %shard_map.112 = (f32[512,896]{1,0:T(8,128)}, f32[512,896]{1,0:T(8,128)}) custom-call(bf16[256,1792]{1,0:T(8,128)(2,1)S(1)} %copy-done.9, bf16[256,1792]{1,0:T(8,128)(2,1)S(1)} %copy-done.18, bf16[256,1792]{1,0:T(8,128)(2,1)S(1)} %copy-done.20, bf16[256,1792]{1,0:T(8,128)(2,1)S(1)} %copy-done.22, bf16[8,64,512]{2,1,0:T(8,128)(2,1)S(1)} %all-to-all-done.refs_0_.refs_4_, ...), custom_call_target="tpu_custom_call" | custom-call | tf_op jit(solution)/shard_map/pallas_call | solution.py:39
  175.6 6.3 %all-to-all-done.1.refs_1_ = bf16[8,64,512]{2,1,0:T(8,128)(2,1)} async-done(((bf16[8,64,512]{2,1,0:T(8,128)(2,1)}), bf16[8,64,512]{2,1,0:T(8,128)(2,1)}, u32[]{:S(2)}, u32[]{:S(2)}) %all-to-all-start.1) | async-done | bytes 524320 | tf_op jit(solution)/shard_map/all_to_all | solution.py:255
  181.8 1.8 shard_map.111
  (97 shorter events, 10.3 us)
Async XLA Ops:
  7.2 30.8 %copy-start.3 = (bf16[512,896]{1,0:T(8,128)(2,1)S(1)}, bf16[512,896]{1,0:T(8,128)(2,1)}, u32[]{:S(2)}) copy-start(bf16[512,896]{1,0:T(8,128)(2,1)} %refs_0_.1) | copy-start | bytes 2752516
  8.9 27.0 %all-to-all-start = ((bf16[8,64,512]{2,1,0:T(8,128)(2,1)}), bf16[8,64,512]{2,1,0:T(8,128)(2,1)S(1)}, u32[]{:S(2)}, u32[]{:S(2)}) async-start(bf16[8,64,512]{2,1,0:T(8,128)(2,1)} %broadcast_in_dim.3), calls=%async_computation | async-start | bytes 1048576 | tf_op jit(solution)/shard_map/all_to_all | solution.py:103
  17.9 43.7 %all-gather.3.cloned.1.call-start = ((), (), s32[]{:S(2)}) async-start(), calls=%async_computation.4 | async-start | bytes 1114112 | tf_op jit(solution)/shard_map/all_gather | solution.py:310
  18.7 145.2 %reduce-scatter.2.cloned.1.call-start = ((), (), s32[]{:S(2)}) async-start(), calls=%async_computation.3 | async-start | bytes 2359296 | tf_op jit(solution)/shard_map/reduce_scatter | solution.py:328
  35.9 2.0 %collective-permute-start.6 = (bf16[8,64,512]{2,1,0:T(8,128)(2,1)S(1)}, bf16[8,64,512]{2,1,0:T(8,128)(2,1)S(1)}, u32[]{:S(2)}, u32[]{:S(2)}) collective-permute-start(bf16[8,64,512]{2,1,0:T(8,128)(2,1)S(1)} %all-to-all-done.refs_0_.refs_4_), channel_id=1, source_target_pairs={{0,1},{1,0},{2,3},{3,2},{4,5},{5,4},{6,7},{7,6},{8,9},{9,8},{10,11... | collective-permute-start | bytes 1572872 | tf_op jit(solution)/shard_map/ppermute | solution.py:76
  39.1 6.6 %copy-start.10 = (bf16[8,64,512]{2,1,0:T(8,128)(2,1)}, bf16[8,64,512]{2,1,0:T(8,128)(2,1)S(1)}, u32[]{:S(2)}) copy-start(bf16[8,64,512]{2,1,0:T(8,128)(2,1)S(1)} %collective-permute-done.6.refs_1_.refs_5_) | copy-start | bytes 1572868
  40.8 26.7 %collective-permute-start.7 = (bf16[256,1792]{1,0:T(8,128)(2,1)}, bf16[256,1792]{1,0:T(8,128)(2,1)}, u32[]{:S(2)}, u32[]{:S(2)}) collective-permute-start(bf16[256,1792]{1,0:T(8,128)(2,1)} %shard_map.98), channel_id=1, source_target_pairs={{0,32},{1,129},{2,34},{3,131},{4,36},{5,133},{6,38},{7,135},{8,40}... | collective-permute-start | bytes 2752520 | tf_op jit(solution)/shard_map/ppermute | solution.py:68
  45.3 16.3 %copy-start.2 = (bf16[896,512]{1,0:T(8,128)(2,1)S(1)}, bf16[896,512]{1,0:T(8,128)(2,1)}, u32[]{:S(2)}) copy-start(bf16[896,512]{1,0:T(8,128)(2,1)} %refs_4_.1) | copy-start | bytes 2752516
  45.3 25.3 %collective-permute-start.8 = (bf16[256,1792]{1,0:T(8,128)(2,1)}, bf16[256,1792]{1,0:T(8,128)(2,1)}, u32[]{:S(2)}, u32[]{:S(2)}) collective-permute-start(bf16[256,1792]{1,0:T(8,128)(2,1)} %shard_map.99), channel_id=1, source_target_pairs={{0,16},{1,65},{2,18},{3,67},{4,20},{5,69},{6,22},{7,71},{8,24},{9,... | collective-permute-start | bytes 2752520 | tf_op jit(solution)/shard_map/ppermute | solution.py:68
  47.4 23.2 %collective-permute-start.9 = (bf16[256,1792]{1,0:T(8,128)(2,1)}, bf16[256,1792]{1,0:T(8,128)(2,1)}, u32[]{:S(2)}, u32[]{:S(2)}) collective-permute-start(bf16[256,1792]{1,0:T(8,128)(2,1)} %shard_map.100), channel_id=1, source_target_pairs={{0,48},{1,193},{2,50},{3,195},{4,52},{5,197},{6,54},{7,199},{8,56}... | collective-permute-start | bytes 2752520 | tf_op jit(solution)/shard_map/ppermute | solution.py:68
  63.3 6.5 %copy-start.5 = (bf16[512,896]{1,0:T(8,128)(2,1)S(1)}, bf16[512,896]{1,0:T(8,128)(2,1)}, u32[]{:S(2)}) copy-start(bf16[512,896]{1,0:T(8,128)(2,1)} %refs_1_.9) | copy-start | bytes 2752516
  63.3 6.5 %copy-start.11 = (bf16[8,64,512]{2,1,0:T(8,128)(2,1)S(1)}, bf16[8,64,512]{2,1,0:T(8,128)(2,1)}, u32[]{:S(2)}) copy-start(bf16[8,64,512]{2,1,0:T(8,128)(2,1)} %copy-done.10) | copy-start | bytes 1572868
  63.3 12.5 %collective-permute-start = (bf16[256,896]{1,0:T(8,128)(2,1)S(1)}, bf16[256,896]{1,0:T(8,128)(2,1)S(1)}, u32[]{:S(2)}, u32[]{:S(2)}) collective-permute-start(bf16[256,896]{1,0:T(8,128)(2,1)S(1)} %shard_map.93.refs_4_), channel_id=1, source_target_pairs={{0,32},{1,129},{2,34},{3,131},{4,36},{5,133},{6,38},{7,135},{8,40}... | collective-permute-start | bytes 1376264 | tf_op jit(solution)/shard_map/ppermute | solution.py:68
  67.1 11.6 %collective-permute-start.1 = (bf16[256,896]{1,0:T(8,128)(2,1)S(1)}, bf16[256,896]{1,0:T(8,128)(2,1)S(1)}, u32[]{:S(2)}, u32[]{:S(2)}) collective-permute-start(bf16[256,896]{1,0:T(8,128)(2,1)S(1)} %shard_map.94.refs_5_), channel_id=1, source_target_pairs={{0,16},{1,65},{2,18},{3,67},{4,20},{5,69},{6,22},{7,71},{8,24},{9,... | collective-permute-start | bytes 1376264 | tf_op jit(solution)/shard_map/ppermute | solution.py:68
  67.5 11.3 %collective-permute-start.2 = (bf16[256,896]{1,0:T(8,128)(2,1)S(1)}, bf16[256,896]{1,0:T(8,128)(2,1)S(1)}, u32[]{:S(2)}, u32[]{:S(2)}) collective-permute-start(bf16[256,896]{1,0:T(8,128)(2,1)S(1)} %shard_map.95.refs_6_), channel_id=1, source_target_pairs={{0,48},{1,193},{2,50},{3,195},{4,52},{5,197},{6,54},{7,199},{8,56}... | collective-permute-start | bytes 1376264 | tf_op jit(solution)/shard_map/ppermute | solution.py:68
  70.6 7.7 %copy-start.1 = (bf16[1024,512]{1,0:T(8,128)(2,1)S(1)}, bf16[1024,512]{1,0:T(8,128)(2,1)}, u32[]{:S(2)}) copy-start(bf16[1024,512]{1,0:T(8,128)(2,1)} %all-gather.3.cloned.1.call-done) | copy-start | bytes 3145732
  72.8 13.4 %collective-permute-start.10 = (f32[64,1792]{1,0:T(8,128)S(1)}, f32[64,1792]{1,0:T(8,128)S(1)}, u32[]{:S(2)}, u32[]{:S(2)}) collective-permute-start(f32[64,1792]{1,0:T(8,128)S(1)} %get-tuple-element.29), channel_id=1, source_target_pairs={{0,128},{1,33},{2,130},{3,35},{4,132},{5,37},{6,134},{7,39},{8,136... | collective-permute-start | bytes 1376264 | tf_op jit(solution)/shard_map/ppermute | solution.py:72
  75.6 13.3 %collective-permute-start.11 = (f32[64,1792]{1,0:T(8,128)S(1)}, f32[64,1792]{1,0:T(8,128)S(1)}, u32[]{:S(2)}, u32[]{:S(2)}) collective-permute-start(f32[64,1792]{1,0:T(8,128)S(1)} %get-tuple-element.30), channel_id=1, source_target_pairs={{0,64},{1,17},{2,66},{3,19},{4,68},{5,21},{6,70},{7,23},{8,72},{9,... | collective-permute-start | bytes 1376264 | tf_op jit(solution)/shard_map/ppermute | solution.py:72
  75.9 13.0 %collective-permute-start.12 = (f32[64,1792]{1,0:T(8,128)S(1)}, f32[64,1792]{1,0:T(8,128)S(1)}, u32[]{:S(2)}, u32[]{:S(2)}) collective-permute-start(f32[64,1792]{1,0:T(8,128)S(1)} %get-tuple-element.31), channel_id=1, source_target_pairs={{0,192},{1,49},{2,194},{3,51},{4,196},{5,53},{6,198},{7,55},{8,200... | collective-permute-start | bytes 1376264 | tf_op jit(solution)/shard_map/ppermute | solution.py:72
  78.9 12.1 %collective-permute-start.3 = (f32[64,896]{1,0:T(8,128)S(1)}, f32[64,896]{1,0:T(8,128)S(1)}, u32[]{:S(2)}, u32[]{:S(2)}) collective-permute-start(f32[64,896]{1,0:T(8,128)S(1)} %get-tuple-element.25), channel_id=1, source_target_pairs={{0,128},{1,33},{2,130},{3,35},{4,132},{5,37},{6,134},{7,39},{8,136... | collective-permute-start | bytes 688136 | tf_op jit(solution)/shard_map/ppermute | solution.py:72
  86.2 6.7 %collective-permute-start.4 = (f32[64,896]{1,0:T(8,128)S(1)}, f32[64,896]{1,0:T(8,128)S(1)}, u32[]{:S(2)}, u32[]{:S(2)}) collective-permute-start(f32[64,896]{1,0:T(8,128)S(1)} %get-tuple-element.26), channel_id=1, source_target_pairs={{0,64},{1,17},{2,66},{3,19},{4,68},{5,21},{6,70},{7,23},{8,72},{9,... | collective-permute-start | bytes 688136 | tf_op jit(solution)/shard_map/ppermute | solution.py:72
  86.2 6.8 %collective-permute-start.5 = (f32[64,896]{1,0:T(8,128)S(1)}, f32[64,896]{1,0:T(8,128)S(1)}, u32[]{:S(2)}, u32[]{:S(2)}) collective-permute-start(f32[64,896]{1,0:T(8,128)S(1)} %get-tuple-element.27), channel_id=1, source_target_pairs={{0,192},{1,49},{2,194},{3,51},{4,196},{5,53},{6,198},{7,55},{8,200... | collective-permute-start | bytes 688136 | tf_op jit(solution)/shard_map/ppermute | solution.py:72
  89.1 6.5 %collective-permute-start.19 = (bf16[64,896]{1,0:T(8,128)(2,1)S(1)}, bf16[64,896]{1,0:T(8,128)(2,1)S(1)}, u32[]{:S(2)}, u32[]{:S(2)}) collective-permute-start(bf16[64,896]{1,0:T(8,128)(2,1)S(1)} %get-tuple-element.34.refs_0_), channel_id=1, source_target_pairs={{0,192},{1,49},{2,194},{3,51},{4,196},{5,53},{6,198},{7,55},{8,200... | collective-permute-start | bytes 344072 | tf_op jit(solution)/shard_map/ppermute | solution.py:72
  90.4 5.2 %collective-permute-start.20 = (bf16[64,896]{1,0:T(8,128)(2,1)S(1)}, bf16[64,896]{1,0:T(8,128)(2,1)S(1)}, u32[]{:S(2)}, u32[]{:S(2)}) collective-permute-start(bf16[64,896]{1,0:T(8,128)(2,1)S(1)} %get-tuple-element.34.refs_0_), channel_id=1, source_target_pairs={{0,128},{1,33},{2,130},{3,35},{4,132},{5,37},{6,134},{7,39},{8,136... | collective-permute-start | bytes 344072 | tf_op jit(solution)/shard_map/ppermute | solution.py:72
  91.0 5.7 %collective-permute-start.21 = (bf16[64,896]{1,0:T(8,128)(2,1)S(1)}, bf16[64,896]{1,0:T(8,128)(2,1)S(1)}, u32[]{:S(2)}, u32[]{:S(2)}) collective-permute-start(bf16[64,896]{1,0:T(8,128)(2,1)S(1)} %get-tuple-element.34.refs_0_), channel_id=1, source_target_pairs={{0,64},{1,17},{2,66},{3,19},{4,68},{5,21},{6,70},{7,23},{8,72},{9,... | collective-permute-start | bytes 344072 | tf_op jit(solution)/shard_map/ppermute | solution.py:72
  93.1 10.8 %collective-permute-start.13 = (bf16[64,1792]{1,0:T(8,128)(2,1)S(1)}, bf16[64,1792]{1,0:T(8,128)(2,1)S(1)}, u32[]{:S(2)}, u32[]{:S(2)}) collective-permute-start(bf16[64,1792]{1,0:T(8,128)(2,1)S(1)} %shard_map.103.refs_0_), channel_id=1, source_target_pairs={{0,192},{1,49},{2,194},{3,51},{4,196},{5,53},{6,198},{7,55},{8,200... | collective-permute-start | bytes 688136 | tf_op jit(solution)/shard_map/ppermute | solution.py:72
  96.8 21.6 %copy-start.15 = (bf16[256,896]{1,0:T(8,128)(2,1)}, bf16[256,896]{1,0:T(8,128)(2,1)S(1)}, u32[]{:S(2)}) copy-start(bf16[256,896]{1,0:T(8,128)(2,1)S(1)} %shard_map.106.refs_0_) | copy-start | bytes 1376260
  96.8 20.3 %collective-permute-start.22 = (bf16[256,896]{1,0:T(8,128)(2,1)S(1)}, bf16[256,896]{1,0:T(8,128)(2,1)S(1)}, u32[]{:S(2)}, u32[]{:S(2)}) collective-permute-start(bf16[256,896]{1,0:T(8,128)(2,1)S(1)} %shard_map.106.refs_0_), channel_id=1, source_target_pairs={{0,48},{1,193},{2,50},{3,195},{4,52},{5,197},{6,54},{7,199},{8,56}... | collective-permute-start | bytes 1376264 | tf_op jit(solution)/shard_map/ppermute | solution.py:68
  99.6 17.5 %collective-permute-start.23 = (bf16[256,896]{1,0:T(8,128)(2,1)S(1)}, bf16[256,896]{1,0:T(8,128)(2,1)S(1)}, u32[]{:S(2)}, u32[]{:S(2)}) collective-permute-start(bf16[256,896]{1,0:T(8,128)(2,1)S(1)} %shard_map.106.refs_0_), channel_id=1, source_target_pairs={{0,32},{1,129},{2,34},{3,131},{4,36},{5,133},{6,38},{7,135},{8,40}... | collective-permute-start | bytes 1376264 | tf_op jit(solution)/shard_map/ppermute | solution.py:68
  100.8 16.3 %collective-permute-start.24 = (bf16[256,896]{1,0:T(8,128)(2,1)S(1)}, bf16[256,896]{1,0:T(8,128)(2,1)S(1)}, u32[]{:S(2)}, u32[]{:S(2)}) collective-permute-start(bf16[256,896]{1,0:T(8,128)(2,1)S(1)} %shard_map.106.refs_0_), channel_id=1, source_target_pairs={{0,16},{1,65},{2,18},{3,67},{4,20},{5,69},{6,22},{7,71},{8,24},{9,... | collective-permute-start | bytes 1376264 | tf_op jit(solution)/shard_map/ppermute | solution.py:68
  101.6 6.4 %collective-permute-start.14 = (bf16[64,1792]{1,0:T(8,128)(2,1)S(1)}, bf16[64,1792]{1,0:T(8,128)(2,1)S(1)}, u32[]{:S(2)}, u32[]{:S(2)}) collective-permute-start(bf16[64,1792]{1,0:T(8,128)(2,1)S(1)} %shard_map.103.refs_0_), channel_id=1, source_target_pairs={{0,128},{1,33},{2,130},{3,35},{4,132},{5,37},{6,134},{7,39},{8,136... | collective-permute-start | bytes 688136 | tf_op jit(solution)/shard_map/ppermute | solution.py:72
  103.8 13.2 %collective-permute-start.15 = (bf16[64,1792]{1,0:T(8,128)(2,1)S(1)}, bf16[64,1792]{1,0:T(8,128)(2,1)S(1)}, u32[]{:S(2)}, u32[]{:S(2)}) collective-permute-start(bf16[64,1792]{1,0:T(8,128)(2,1)S(1)} %shard_map.103.refs_0_), channel_id=1, source_target_pairs={{0,64},{1,17},{2,66},{3,19},{4,68},{5,21},{6,70},{7,23},{8,72},{9,... | collective-permute-start | bytes 688136 | tf_op jit(solution)/shard_map/ppermute | solution.py:72
  119.8 2.7 %copy-start.6 = (bf16[512,896]{1,0:T(8,128)(2,1)S(1)}, bf16[512,896]{1,0:T(8,128)(2,1)}, u32[]{:S(2)}) copy-start(bf16[512,896]{1,0:T(8,128)(2,1)} %refs_1_.9) | copy-start | bytes 2752516
  119.8 3.2 %copy-start.16 = (bf16[256,896]{1,0:T(8,128)(2,1)S(1)}, bf16[256,896]{1,0:T(8,128)(2,1)}, u32[]{:S(2)}) copy-start(bf16[256,896]{1,0:T(8,128)(2,1)} %copy-done.15) | copy-start | bytes 1376260
  119.8 3.2 %copy-start.24 = (bf16[256,896]{1,0:T(8,128)(2,1)S(1)}, bf16[256,896]{1,0:T(8,128)(2,1)}, u32[]{:S(2)}) copy-start(bf16[256,896]{1,0:T(8,128)(2,1)} %copy-done.23) | copy-start | bytes 1376260
  119.9 3.2 %copy-start.26 = (bf16[256,896]{1,0:T(8,128)(2,1)S(1)}, bf16[256,896]{1,0:T(8,128)(2,1)}, u32[]{:S(2)}) copy-start(bf16[256,896]{1,0:T(8,128)(2,1)} %copy-done.25) | copy-start | bytes 1376260
  119.9 3.2 %copy-start.28 = (bf16[256,896]{1,0:T(8,128)(2,1)S(1)}, bf16[256,896]{1,0:T(8,128)(2,1)}, u32[]{:S(2)}) copy-start(bf16[256,896]{1,0:T(8,128)(2,1)} %copy-done.27) | copy-start | bytes 1376260
  119.9 22.2 %collective-permute-start.16 = (bf16[256,1792]{1,0:T(8,128)(2,1)}, bf16[256,1792]{1,0:T(8,128)(2,1)S(1)}, u32[]{:S(2)}, u32[]{:S(2)}) collective-permute-start(bf16[256,1792]{1,0:T(8,128)(2,1)} %copy-done.7), channel_id=1, source_target_pairs={{0,48},{1,193},{2,50},{3,195},{4,52},{5,197},{6,54},{7,199},{8,56}... | collective-permute-start | bytes 2752520 | tf_op jit(solution)/shard_map/ppermute | solution.py:68
  121.5 20.5 %collective-permute-start.17 = (bf16[256,1792]{1,0:T(8,128)(2,1)}, bf16[256,1792]{1,0:T(8,128)(2,1)S(1)}, u32[]{:S(2)}, u32[]{:S(2)}) collective-permute-start(bf16[256,1792]{1,0:T(8,128)(2,1)} %copy-done.7), channel_id=1, source_target_pairs={{0,32},{1,129},{2,34},{3,131},{4,36},{5,133},{6,38},{7,135},{8,40}... | collective-permute-start | bytes 2752520 | tf_op jit(solution)/shard_map/ppermute | solution.py:68
  122.5 23.1 %collective-permute-start.18 = (bf16[256,1792]{1,0:T(8,128)(2,1)}, bf16[256,1792]{1,0:T(8,128)(2,1)S(1)}, u32[]{:S(2)}, u32[]{:S(2)}) collective-permute-start(bf16[256,1792]{1,0:T(8,128)(2,1)} %copy-done.7), channel_id=1, source_target_pairs={{0,16},{1,65},{2,18},{3,67},{4,20},{5,69},{6,22},{7,71},{8,24},{9,... | collective-permute-start | bytes 2752520 | tf_op jit(solution)/shard_map/ppermute | solution.py:68
  123.0 22.6 %copy-start.8 = (bf16[256,1792]{1,0:T(8,128)(2,1)S(1)}, bf16[256,1792]{1,0:T(8,128)(2,1)}, u32[]{:S(2)}) copy-start(bf16[256,1792]{1,0:T(8,128)(2,1)} %copy-done.7) | copy-start | bytes 2752516
  142.0 7.9 %copy-start.17 = (bf16[256,1792]{1,0:T(8,128)(2,1)}, bf16[256,1792]{1,0:T(8,128)(2,1)S(1)}, u32[]{:S(2)}) copy-start(bf16[256,1792]{1,0:T(8,128)(2,1)S(1)} %collective-permute-done.16.refs_1_) | copy-start | bytes 2752516
  142.0 7.9 %copy-start.19 = (bf16[256,1792]{1,0:T(8,128)(2,1)}, bf16[256,1792]{1,0:T(8,128)(2,1)S(1)}, u32[]{:S(2)}) copy-start(bf16[256,1792]{1,0:T(8,128)(2,1)S(1)} %collective-permute-done.17.refs_2_) | copy-start | bytes 2752516
  147.1 2.9 %copy-start.21 = (bf16[256,1792]{1,0:T(8,128)(2,1)}, bf16[256,1792]{1,0:T(8,128)(2,1)S(1)}, u32[]{:S(2)}) copy-start(bf16[256,1792]{1,0:T(8,128)(2,1)S(1)} %collective-permute-done.18.refs_3_) | copy-start | bytes 2752516
  150.0 8.6 %collective-permute-start.25 = (f32[8,64,512]{2,1,0:T(8,128)S(1)}, f32[8,64,512]{2,1,0:T(8,128)S(1)}, u32[]{:S(2)}, u32[]{:S(2)}) collective-permute-start(f32[8,64,512]{2,1,0:T(8,128)S(1)} %get-tuple-element.36), channel_id=1, source_target_pairs={{0,1},{1,0},{2,3},{3,2},{4,5},{5,4},{6,7},{7,6},{8,9},{9,8},{10,11... | collective-permute-start | bytes 3145736 | tf_op jit(solution)/shard_map/ppermute | solution.py:76
  159.5 7.4 %copy-start.18 = (bf16[256,1792]{1,0:T(8,128)(2,1)S(1)}, bf16[256,1792]{1,0:T(8,128)(2,1)}, u32[]{:S(2)}) copy-start(bf16[256,1792]{1,0:T(8,128)(2,1)} %copy-done.17) | copy-start | bytes 2752516
  159.5 22.3 %all-to-all-start.1 = ((bf16[8,64,512]{2,1,0:T(8,128)(2,1)}), bf16[8,64,512]{2,1,0:T(8,128)(2,1)}, u32[]{:S(2)}, u32[]{:S(2)}) async-start(bf16[8,64,512]{2,1,0:T(8,128)(2,1)} %get-tuple-element.38), calls=%async_computation.1 | async-start | bytes 1048576 | tf_op jit(solution)/shard_map/all_to_all | solution.py:255
  164.8 17.0 %collective-permute-start.26 = (f32[64,512]{1,0:T(8,128)S(1)}, f32[64,512]{1,0:T(8,128)}, u32[]{:S(2)}, u32[]{:S(2)}) collective-permute-start(f32[64,512]{1,0:T(8,128)S(1)} %get-tuple-element.43), channel_id=1, source_target_pairs={{0,1},{1,0},{2,3},{3,2},{4,5},{5,4},{6,7},{7,6},{8,9},{9,8},{10,11... | collective-permute-start | bytes 393224 | tf_op jit(solution)/shard_map/ppermute | solution.py:76
  (12 other events, 15.2 us)
Sparse Core Ops, SparseCore 0:
  20.6 40.9 all-gather.2
  120.0 40.7 reduce-scatter.1

commit v2 on v1

--- a/solution.py
+++ b/solution.py
@@ -47,6 +47,9 @@
 
 def shape(dims, dtype):
     return jax.ShapeDtypeStruct(dims, dtype)
+
+
+MARK = shape((8, 128), F32)
 
 
 def along(first, k):
@@ -206,15 +209,30 @@
 
 
 def back(blocks, weights, after=()):
-    hidden, width = weights.shape
-    rows = blocks[0].shape[0]
-
-    def kernel(a, b, c, d, weights_ref, mine, other):
-        for i, block in enumerate((a, b, c, d)):
+    width = weights.shape[1]
+    tile = blocks[0].shape[0] // RING
+
+    def kernel(a, b, c, weights_ref, mine, other):
+        for i, block in enumerate((a, b, c)):
             store_tiles(mine, other, i, dot(block[...], weights_ref[...], (1, 0)))
-
-    half = shape((DEPTH, rows // RING, width), F32)
-    return call(kernel, [half, half], *blocks, weights, after=after)
+        store_tiles(mine, other, RING - 1, jnp.zeros((RING * tile, width), F32))
+
+    half = shape((DEPTH, tile, width), F32)
+    return call(kernel, [half, half], *blocks[:-1], weights, after=after)
+
+
+def back_last(block, weights):
+    width = weights.shape[1]
+    tile = block.shape[0] // RING
+
+    def kernel(block_ref, weights_ref, mine, other):
+        result = dot(block_ref[...], weights_ref[...], (1, 0))
+        for j in range(RING):
+            foreign, z = tile_at(RING - 1, j)
+            store_tile(mine, other, foreign, z % 2, result[j * tile : (j + 1) * tile])
+
+    half = shape((2, tile, width), F32)
+    return call(kernel, [half, half], block, weights)
 
 
 def back_hidden(blocks, weights, after=()):
@@ -242,16 +260,25 @@
     return call(kernel, shape((2 * hidden, width), BF16), gate_weight, up_weight)
 
 
-def reduce_z(mine, other, done):
-    arrived = send_core(other)
+def reduce_z(first, last, done):
+    (mine, other), (mine_last, other_last) = first, last
+    arrived, arrived_last = send_core(other), send_core(other_last)
     depth, rows, width = mine.shape
 
-    def split(mine_ref, arrived_ref, own, out):
-        own[...] = mine_ref[place()[2]] + arrived_ref[place()[2]]
+    def split(mine_ref, arrived_ref, mine_last_ref, arrived_last_ref, own, out):
+        p, q, z, _ = place()
+        last_mine, last_arrived = (p + RING - 1) % RING, (q + RING - 1) % RING
+
+        def total(k):
+            a = jnp.where(k // 2 == last_mine, mine_last_ref[k % 2], mine_ref[k])
+            return a + jnp.where(k // 2 == last_arrived, arrived_last_ref[k % 2], arrived_ref[k])
+
+        own[...] = total(z)
         for k in range(depth):
-            out[k] = (mine_ref[k] + arrived_ref[k]).astype(BF16)
-
-    own, parts = call(split, [shape((rows, width), F32), shape(mine.shape, BF16)], mine, arrived)
+            out[k] = total(k).astype(BF16)
+
+    outs = [shape((rows, width), F32), shape(mine.shape, BF16)]
+    own, parts = call(split, outs, mine, arrived, mine_last, arrived_last)
     parts = lax.all_to_all(parts, "tensor", 0, 0, tiled=True, axis_index_groups=CORES)
 
     def add(own_ref, parts_ref, done_ref, more_ref, out, done_out):
@@ -268,7 +295,8 @@
     rows, hidden = blocks[0].shape
     width = grads.shape[2]
 
-    def kernel(a, b, c, d, grads_ref, out_ref):
+    def kernel(a, b, c, d, grads_ref, out_ref, mark):
+        mark[...] = jnp.zeros_like(mark)
         for i, block in enumerate((a, b, c, d)):
             part = dot(block[...], grad_block(grads_ref, i), (0, 0)) * factor
             if i == 0:
@@ -276,16 +304,15 @@
             else:
                 out_ref[...] += part
 
-    return call(
-        kernel, shape((hidden, width), F32), *blocks, grads
-    )
+    return call(kernel, [shape((hidden, width), F32), MARK], *blocks, grads)
 
 
 def token_weight_grads(blocks, mine, other, factor):
     rows, hidden = blocks[0].shape[0], blocks[0].shape[1] // 2
     width = mine.shape[2]
 
-    def kernel(a, b, c, d, mine_ref, other_ref, gate_ref, up_ref):
+    def kernel(a, b, c, d, mine_ref, other_ref, gate_ref, up_ref, mark):
+        mark[...] = jnp.zeros_like(mark)
         for i, block in enumerate((a, b, c, d)):
             tokens = row_block(mine_ref, other_ref, i)
             gate = dot(tokens, block[:, :hidden], (0, 0)) * factor
@@ -298,7 +325,17 @@
                 up_ref[...] += up
 
     out = shape((width, hidden), F32)
-    return call(kernel, [out, out], *blocks, mine, other)
+    return call(kernel, [out, out, MARK], *blocks, mine, other)
+
+
+def halves(a, after):
+    rows, columns = a.shape
+
+    def kernel(a_ref, first, second):
+        first[...] = a_ref[: rows // 2]
+        second[...] = a_ref[rows // 2 :]
+
+    return call(kernel, [shape((rows // 2, columns), a.dtype)] * 2, a, after=after)
 
 
 def body(tokens, gate_weight, up_weight, down_weight, out_grad):
@@ -323,12 +360,15 @@
     grad_blocks = gather_p(grad_block)
 
     partial = back_hidden(hidden_blocks, down_weight, after=[grad_block])
-    down_weight_grad = hidden_weight_grad(hidden_blocks, grads, factor)
+    down_weight_grad, mark = hidden_weight_grad(hidden_blocks, grads, factor)
     partial = partial.reshape(rows, width)
     both = lax.psum_scatter(partial, "tensor", scatter_dimension=0, tiled=True, axis_index_groups=CORES)
-    done = [both[:shard], send_core(both[shard:])]
-    input_grad, ffn_output = reduce_z(*back(grad_blocks, transposed(gate_weight, up_weight), after=[down_weight_grad]), done)
-    gate_weight_grad, up_weight_grad = token_weight_grads(grad_blocks, *rows_of, factor)
+    weights = transposed(gate_weight, up_weight)
+    first = back(grad_blocks, weights, after=[mark])
+    gate_weight_grad, up_weight_grad, mark = token_weight_grads(grad_blocks, *rows_of, factor)
+    own, foreign = halves(both, after=[mark])
+    done = [own, send_core(foreign)]
+    input_grad, ffn_output = reduce_z(first, back_last(grad_blocks[-1], weights), done)
     return ffn_output, input_grad, gate_weight_grad, up_weight_grad, down_weight_grad
 
 

time: 191 us -> 184 us (0.963)
  waiting for transfers between devices: 75.6 us -> 71 us
  local copies, waits for them, and re-layouts: 12.7 us -> 9.72 us
  starting transfers between devices: 63.8 us -> 66.3 us
    ppermute x12, waiting for transfers between devices: 20.2 us -> 16.6 us  [send_p(): return lax.ppermute(a, BOTH, along(True, k % RING))]
    ppermute x3 -> x4, starting transfers between devices: 8.96 us -> 11.6 us  [send_core(): return lax.ppermute(a, 'tensor', [(i, i ^ 1) for i in range(2 * DEPTH)])]
    unnamed x58, local copies, waits for them, and re-layouts: 9.98 us -> 7.96 us
    pallas_call x21 -> x23, Pallas kernels: 23.9 us -> 22.3 us  [call(): pl.pallas_call(run, in_specs=[pl.BlockSpec(memory_space=pltpu.VMEM)] * le...]
    ppermute x3 -> x4, waiting for transfers between devices: 3.83 us -> 2.7 us  [send_core(): return lax.ppermute(a, 'tensor', [(i, i ^ 1) for i in range(2 * DEPTH)])]
  transfers between devices with their start and end apart: 31 -> 32, of which waited for: 12 -> 11; matrix products, arithmetic and copies ran while one was open for 1% -> 0% of each run, Pallas kernels for 11% -> 11%
where the time goes in v2:
time: 184 us
  waiting for transfers between devices  71 us (39%)
  starting transfers between devices  66.3 us (36%)
  Pallas kernels  22.3 us (12%)
  between operations  14.5 us (8%)
  local copies, waits for them, and re-layouts  9.72 us (5%)
    ppermute x12, starting transfers between devices, send_q(): return lax.ppermute(a, BOTH, along(False, k % RING))  22.9 us
    pallas_call x23, Pallas kernels, call(): pl.pallas_call(run, in_specs=[pl.BlockSpec(memory_space=pltpu.VMEM)] * le...  22.3 us
    ppermute x12, starting transfers between devices, send_p(): return lax.ppermute(a, BOTH, along(True, k % RING))  18.6 us
    all_to_all x1, waiting for transfers between devices, gather_z(): lax.all_to_all(copies, 'tensor', 0, 0, tiled=True, axis_index_groups=CORES)  17.2 us
    ppermute x12, waiting for transfers between devices, send_p(): return lax.ppermute(a, BOTH, along(True, k % RING))  16.6 us
    ppermute x12, waiting for transfers between devices, send_q(): return lax.ppermute(a, BOTH, along(False, k % RING))  15.5 us
    all_gather x1, waiting for transfers between devices, body(): grads = lax.all_gather(out_grad, 'tensor', axis=0)  11.9 us
    ppermute x4, starting transfers between devices, send_core(): return lax.ppermute(a, 'tensor', [(i, i ^ 1) for i in range(2 * DEPTH)])  11.6 us
  transfers between devices with their start and end apart: 32, of which 11 were waited for; matrix products, arithmetic and copies ran while one was open for 0% of the time, Pallas kernels for 11%

profile of v2, /device:TPU:1, one launch (start us, length us, event | category | flops | bytes accessed | tf_op | source)
XLA Modules:
  0.0 183.8 jit_solution(6931518039628742456)
XLA Ops:
  7.2 1.8 broadcast_in_dim.3
  8.9 9.0 %all-to-all-start = ((bf16[8,64,512]{2,1,0:T(8,128)(2,1)}), bf16[8,64,512]{2,1,0:T(8,128)(2,1)S(1)}, u32[]{:S(2)}, u32[]{:S(2)}) async-start(bf16[8,64,512]{2,1,0:T(8,128)(2,1)} %broadcast_in_dim.3), calls=%async_computation | async-start | bytes 1048576 | tf_op jit(solution)/shard_map/all_to_all | solution.py:106
  18.7 17.2 %all-to-all-done.refs_0_.refs_4_ = bf16[8,64,512]{2,1,0:T(8,128)(2,1)S(1)} async-done(((bf16[8,64,512]{2,1,0:T(8,128)(2,1)}), bf16[8,64,512]{2,1,0:T(8,128)(2,1)S(1)}, u32[]{:S(2)}, u32[]{:S(2)}) %all-to-all-start) | async-done | bytes 524320 | tf_op jit(solution)/shard_map/all_to_all | solution.py:106
  36.4 1.5 collective-permute-done.6.refs_1_.refs_5_
  37.9 1.2 copy-done.4
  39.1 1.6 shard_map.98
  40.8 2.9 %collective-permute-start.7 = (bf16[256,1792]{1,0:T(8,128)(2,1)}, bf16[256,1792]{1,0:T(8,128)(2,1)}, u32[]{:S(2)}, u32[]{:S(2)}) collective-permute-start(bf16[256,1792]{1,0:T(8,128)(2,1)} %shard_map.98), channel_id=1, source_target_pairs={{0,32},{1,129},{2,34},{3,131},{4,36},{5,133},{6,38},{7,135},{8,40}... | collective-permute-start | bytes 2752520 | tf_op jit(solution)/shard_map/ppermute | solution.py:71
  43.7 1.6 shard_map.99
  45.7 1.6 shard_map.100
  47.4 2.3 %collective-permute-start.9 = (bf16[256,1792]{1,0:T(8,128)(2,1)}, bf16[256,1792]{1,0:T(8,128)(2,1)}, u32[]{:S(2)}, u32[]{:S(2)}) collective-permute-start(bf16[256,1792]{1,0:T(8,128)(2,1)} %shard_map.100), channel_id=1, source_target_pairs={{0,48},{1,193},{2,50},{3,195},{4,52},{5,197},{6,54},{7,199},{8,56}... | collective-permute-start | bytes 2752520 | tf_op jit(solution)/shard_map/ppermute | solution.py:71
  49.7 11.9 %all-gather.3.cloned.1.call-done = bf16[1024,512]{1,0:T(8,128)(2,1)} async-done(((bf16[64,512]{1,0:T(8,128)(2,1)}), bf16[1024,512]{1,0:T(8,128)(2,1)}) %all-gather.3.cloned.1.call-update) | async-done | bytes 1048592 | tf_op jit(solution)/shard_map/all_gather | solution.py:347
  61.6 1.2 copy-done
  63.3 2.8 %collective-permute-start = (bf16[256,896]{1,0:T(8,128)(2,1)S(1)}, bf16[256,896]{1,0:T(8,128)(2,1)S(1)}, u32[]{:S(2)}, u32[]{:S(2)}) collective-permute-start(bf16[256,896]{1,0:T(8,128)(2,1)S(1)} %shard_map.93.refs_4_), channel_id=1, source_target_pairs={{0,32},{1,129},{2,34},{3,131},{4,36},{5,133},{6,38},{7,135},{8,40}... | collective-permute-start | bytes 1376264 | tf_op jit(solution)/shard_map/ppermute | solution.py:71
  67.5 2.4 %collective-permute-start.2 = (bf16[256,896]{1,0:T(8,128)(2,1)S(1)}, bf16[256,896]{1,0:T(8,128)(2,1)S(1)}, u32[]{:S(2)}, u32[]{:S(2)}) collective-permute-start(bf16[256,896]{1,0:T(8,128)(2,1)S(1)} %shard_map.95.refs_6_), channel_id=1, source_target_pairs={{0,48},{1,193},{2,50},{3,195},{4,52},{5,197},{6,54},{7,199},{8,56}... | collective-permute-start | bytes 1376264 | tf_op jit(solution)/shard_map/ppermute | solution.py:71
  70.6 2.2 %shard_map.101 = (f32[64,1792]{1,0:T(8,128)S(1)}, f32[64,1792]{1,0:T(8,128)S(1)}, f32[64,1792]{1,0:T(8,128)S(1)}, f32[64,1792]{1,0:T(8,128)S(1)}) custom-call(f32[256,1792]{1,0:T(8,128)S(1)} %shard_map.97.refs_0_, bf16[256,1792]{1,0:T(8,128)(2,1)} %collective-permute-done.7.refs_1_, bf16[256,1792]{1,0:T(8,128)(2,1)} %collective-permute-done.8.refs_2_, ...), custom_call_target="tpu_custom_call" | custom-call | tf_op jit(solution)/shard_map/pallas_call | solution.py:39
  72.8 2.8 %collective-permute-start.10 = (f32[64,1792]{1,0:T(8,128)S(1)}, f32[64,1792]{1,0:T(8,128)S(1)}, u32[]{:S(2)}, u32[]{:S(2)}) collective-permute-start(f32[64,1792]{1,0:T(8,128)S(1)} %get-tuple-element.36), channel_id=1, source_target_pairs={{0,128},{1,33},{2,130},{3,35},{4,132},{5,37},{6,134},{7,39},{8,136... | collective-permute-start | bytes 1376264 | tf_op jit(solution)/shard_map/ppermute | solution.py:75
  75.9 2.4 %collective-permute-start.12 = (f32[64,1792]{1,0:T(8,128)S(1)}, f32[64,1792]{1,0:T(8,128)S(1)}, u32[]{:S(2)}, u32[]{:S(2)}) collective-permute-start(f32[64,1792]{1,0:T(8,128)S(1)} %get-tuple-element.38), channel_id=1, source_target_pairs={{0,192},{1,49},{2,194},{3,51},{4,196},{5,53},{6,198},{7,55},{8,200... | collective-permute-start | bytes 1376264 | tf_op jit(solution)/shard_map/ppermute | solution.py:75
  78.9 7.3 %collective-permute-start.3 = (f32[64,896]{1,0:T(8,128)S(1)}, f32[64,896]{1,0:T(8,128)S(1)}, u32[]{:S(2)}, u32[]{:S(2)}) collective-permute-start(f32[64,896]{1,0:T(8,128)S(1)} %get-tuple-element.32), channel_id=1, source_target_pairs={{0,128},{1,33},{2,130},{3,35},{4,132},{5,37},{6,134},{7,39},{8,136... | collective-permute-start | bytes 688136 | tf_op jit(solution)/shard_map/ppermute | solution.py:75
  86.2 2.7 %collective-permute-start.5 = (f32[64,896]{1,0:T(8,128)S(1)}, f32[64,896]{1,0:T(8,128)S(1)}, u32[]{:S(2)}, u32[]{:S(2)}) collective-permute-start(f32[64,896]{1,0:T(8,128)S(1)} %get-tuple-element.34), channel_id=1, source_target_pairs={{0,192},{1,49},{2,194},{3,51},{4,196},{5,53},{6,198},{7,55},{8,200... | collective-permute-start | bytes 688136 | tf_op jit(solution)/shard_map/ppermute | solution.py:75
  89.1 1.3 collective-permute-start.18
  91.6 1.4 collective-permute-done.4.refs_2_.refs_5_
  93.1 2.5 %collective-permute-start.13 = (bf16[64,1792]{1,0:T(8,128)(2,1)S(1)}, bf16[64,1792]{1,0:T(8,128)(2,1)S(1)}, u32[]{:S(2)}, u32[]{:S(2)}) collective-permute-start(bf16[64,1792]{1,0:T(8,128)(2,1)S(1)} %shard_map.103.refs_0_), channel_id=1, source_target_pairs={{0,192},{1,49},{2,194},{3,51},{4,196},{5,53},{6,198},{7,55},{8,200... | collective-permute-start | bytes 688136 | tf_op jit(solution)/shard_map/ppermute | solution.py:75
  95.6 1.1 collective-permute-done.20.refs_3_
  96.8 2.8 %collective-permute-start.21 = (bf16[256,896]{1,0:T(8,128)(2,1)S(1)}, bf16[256,896]{1,0:T(8,128)(2,1)S(1)}, u32[]{:S(2)}, u32[]{:S(2)}) collective-permute-start(bf16[256,896]{1,0:T(8,128)(2,1)S(1)} %shard_map.106.refs_0_), channel_id=1, source_target_pairs={{0,48},{1,193},{2,50},{3,195},{4,52},{5,197},{6,54},{7,199},{8,56}... | collective-permute-start | bytes 1376264 | tf_op jit(solution)/shard_map/ppermute | solution.py:71
  99.6 1.2 collective-permute-start.22
  100.8 0.8 collective-permute-start.23
  101.6 2.2 %collective-permute-start.14 = (bf16[64,1792]{1,0:T(8,128)(2,1)S(1)}, bf16[64,1792]{1,0:T(8,128)(2,1)S(1)}, u32[]{:S(2)}, u32[]{:S(2)}) collective-permute-start(bf16[64,1792]{1,0:T(8,128)(2,1)S(1)} %shard_map.103.refs_0_), channel_id=1, source_target_pairs={{0,128},{1,33},{2,130},{3,35},{4,132},{5,37},{6,134},{7,39},{8,136... | collective-permute-start | bytes 688136 | tf_op jit(solution)/shard_map/ppermute | solution.py:75
  104.2 3.9 %collective-permute-done.14.refs_2_ = bf16[64,1792]{1,0:T(8,128)(2,1)S(1)} collective-permute-done((bf16[64,1792]{1,0:T(8,128)(2,1)S(1)}, bf16[64,1792]{1,0:T(8,128)(2,1)S(1)}, u32[]{:S(2)}, u32[]{:S(2)}) %collective-permute-start.14) | collective-permute-done | bytes 229408 | tf_op jit(solution)/shard_map/ppermute | solution.py:75
  108.0 9.0 %collective-permute-done.15.refs_3_ = bf16[64,1792]{1,0:T(8,128)(2,1)S(1)} collective-permute-done((bf16[64,1792]{1,0:T(8,128)(2,1)S(1)}, bf16[64,1792]{1,0:T(8,128)(2,1)S(1)}, u32[]{:S(2)}, u32[]{:S(2)}) %collective-permute-start.15) | collective-permute-done | bytes 229408 | tf_op jit(solution)/shard_map/ppermute | solution.py:75
  117.2 1.2 shard_map.111
  118.5 1.3 copy-done.12
  119.9 1.6 collective-permute-start.16
  121.5 0.9 collective-permute-start.17
  123.0 2.4 %shard_map.107 = (f32[896,512]{1,0:T(8,128)}, f32[8,128]{1,0:T(8,128)S(1)}) custom-call(bf16[256,896]{1,0:T(8,128)(2,1)S(1)} %copy-done.14, bf16[256,896]{1,0:T(8,128)(2,1)S(1)} %copy-done.22, bf16[256,896]{1,0:T(8,128)(2,1)S(1)} %copy-done.24, bf16[256,896]{1,0:T(8,128)(2,1)S(1)} %copy-done.26, bf16[16,64,512]{2,1,0:T(8,128)(2,1)S(1)} %bitcast.7), custom_call_target="tpu_custom_call" | custom-call | tf_op jit(solution)/shard_map/pallas_call | solution.py:39
  125.4 16.6 %collective-permute-done.16.refs_1_ = bf16[256,1792]{1,0:T(8,128)(2,1)S(1)} collective-permute-done((bf16[256,1792]{1,0:T(8,128)(2,1)}, bf16[256,1792]{1,0:T(8,128)(2,1)S(1)}, u32[]{:S(2)}, u32[]{:S(2)}) %collective-permute-start.16) | collective-permute-done | bytes 917536 | tf_op jit(solution)/shard_map/ppermute | solution.py:71
  142.0 2.2 %shard_map.108 = (f32[8,64,512]{2,1,0:T(8,128)S(1)}, f32[8,64,512]{2,1,0:T(8,128)S(1)}) custom-call(bf16[256,1792]{1,0:T(8,128)(2,1)S(1)} %copy-done.8, bf16[256,1792]{1,0:T(8,128)(2,1)S(1)} %collective-permute-done.16.refs_1_, bf16[256,1792]{1,0:T(8,128)(2,1)S(1)} %collective-permute-done.17.refs_2_, bf16[1792,512]{1,0:T(8,128)(2,1)S(1)} %shard_map.105.refs_3_.refs_1_, ...), custom_call_target="tpu_custom_call" | custom-call | tf_op jit(solution)/shard_map/pallas_call | solution.py:39
  144.3 6.1 %collective-permute-start.24 = (f32[8,64,512]{2,1,0:T(8,128)S(1)}, f32[8,64,512]{2,1,0:T(8,128)S(1)}, u32[]{:S(2)}, u32[]{:S(2)}) collective-permute-start(f32[8,64,512]{2,1,0:T(8,128)S(1)} %get-tuple-element.44), channel_id=1, source_target_pairs={{0,1},{1,0},{2,3},{3,2},{4,5},{5,4},{6,7},{7,6},{8,9},{9,8},{10,11... | collective-permute-start | bytes 3145736 | tf_op jit(solution)/shard_map/ppermute | solution.py:79
  151.1 1.6 collective-permute-start.26
  152.7 1.2 collective-permute-done.26.refs_3_
  154.1 0.8 copy-done.27
  154.9 4.1 %all-to-all-start.1 = ((bf16[8,64,512]{2,1,0:T(8,128)(2,1)}), bf16[8,64,512]{2,1,0:T(8,128)(2,1)S(1)}, u32[]{:S(2)}, u32[]{:S(2)}) async-start(bf16[8,64,512]{2,1,0:T(8,128)(2,1)} %copy-done.27), calls=%async_computation.1 | async-start | bytes 1048576 | tf_op jit(solution)/shard_map/all_to_all | solution.py:282
  159.0 1.2 copy-done.18
  160.2 1.2 copy-done.20
  161.4 4.0 %shard_map.112 = (f32[512,896]{1,0:T(8,128)}, f32[512,896]{1,0:T(8,128)}, f32[8,128]{1,0:T(8,128)S(1)}) custom-call(bf16[256,1792]{1,0:T(8,128)(2,1)S(1)} %copy-done.8, bf16[256,1792]{1,0:T(8,128)(2,1)S(1)} %copy-done.16, bf16[256,1792]{1,0:T(8,128)(2,1)S(1)} %copy-done.18, bf16[256,1792]{1,0:T(8,128)(2,1)S(1)} %copy-done.20, ...), custom_call_target="tpu_custom_call" | custom-call | tf_op jit(solution)/shard_map/pallas_call | solution.py:39
  165.4 0.9 copy-done.28
  166.3 3.4 %collective-permute-start.27 = (f32[64,512]{1,0:T(8,128)S(1)}, f32[64,512]{1,0:T(8,128)S(1)}, u32[]{:S(2)}, u32[]{:S(2)}) collective-permute-start(f32[64,512]{1,0:T(8,128)S(1)} %get-tuple-element.51), channel_id=1, source_target_pairs={{0,1},{1,0},{2,3},{3,2},{4,5},{5,4},{6,7},{7,6},{8,9},{9,8},{10,11... | collective-permute-start | bytes 393224 | tf_op jit(solution)/shard_map/ppermute | solution.py:79
  169.8 6.4 %all-to-all-done.1.refs_1_ = bf16[8,64,512]{2,1,0:T(8,128)(2,1)S(1)} async-done(((bf16[8,64,512]{2,1,0:T(8,128)(2,1)}), bf16[8,64,512]{2,1,0:T(8,128)(2,1)S(1)}, u32[]{:S(2)}, u32[]{:S(2)}) %all-to-all-start.1) | async-done | bytes 524320 | tf_op jit(solution)/shard_map/all_to_all | solution.py:282
  176.2 0.8 shard_map.114
  (100 shorter events, 8.7 us)
Async XLA Ops:
  7.2 30.8 %copy-start.3 = (bf16[512,896]{1,0:T(8,128)(2,1)S(1)}, bf16[512,896]{1,0:T(8,128)(2,1)}, u32[]{:S(2)}) copy-start(bf16[512,896]{1,0:T(8,128)(2,1)} %refs_0_.1) | copy-start | bytes 2752516
  8.9 27.0 %all-to-all-start = ((bf16[8,64,512]{2,1,0:T(8,128)(2,1)}), bf16[8,64,512]{2,1,0:T(8,128)(2,1)S(1)}, u32[]{:S(2)}, u32[]{:S(2)}) async-start(bf16[8,64,512]{2,1,0:T(8,128)(2,1)} %broadcast_in_dim.3), calls=%async_computation | async-start | bytes 1048576 | tf_op jit(solution)/shard_map/all_to_all | solution.py:106
  17.9 43.7 %all-gather.3.cloned.1.call-start = ((), (), s32[]{:S(2)}) async-start(), calls=%async_computation.4 | async-start | bytes 1114112 | tf_op jit(solution)/shard_map/all_gather | solution.py:347
  18.7 146.7 %reduce-scatter.2.cloned.1.call-start = ((), (), s32[]{:S(2)}) async-start(), calls=%async_computation.3 | async-start | bytes 2359296 | tf_op jit(solution)/shard_map/reduce_scatter | solution.py:365
  35.9 2.0 %collective-permute-start.6 = (bf16[8,64,512]{2,1,0:T(8,128)(2,1)S(1)}, bf16[8,64,512]{2,1,0:T(8,128)(2,1)S(1)}, u32[]{:S(2)}, u32[]{:S(2)}) collective-permute-start(bf16[8,64,512]{2,1,0:T(8,128)(2,1)S(1)} %all-to-all-done.refs_0_.refs_4_), channel_id=1, source_target_pairs={{0,1},{1,0},{2,3},{3,2},{4,5},{5,4},{6,7},{7,6},{8,9},{9,8},{10,11... | collective-permute-start | bytes 1572872 | tf_op jit(solution)/shard_map/ppermute | solution.py:79
  39.1 6.6 %copy-start.9 = (bf16[8,64,512]{2,1,0:T(8,128)(2,1)}, bf16[8,64,512]{2,1,0:T(8,128)(2,1)S(1)}, u32[]{:S(2)}) copy-start(bf16[8,64,512]{2,1,0:T(8,128)(2,1)S(1)} %collective-permute-done.6.refs_1_.refs_5_) | copy-start | bytes 1572868
  40.8 26.7 %collective-permute-start.7 = (bf16[256,1792]{1,0:T(8,128)(2,1)}, bf16[256,1792]{1,0:T(8,128)(2,1)}, u32[]{:S(2)}, u32[]{:S(2)}) collective-permute-start(bf16[256,1792]{1,0:T(8,128)(2,1)} %shard_map.98), channel_id=1, source_target_pairs={{0,32},{1,129},{2,34},{3,131},{4,36},{5,133},{6,38},{7,135},{8,40}... | collective-permute-start | bytes 2752520 | tf_op jit(solution)/shard_map/ppermute | solution.py:71
  45.3 16.3 %copy-start.2 = (bf16[896,512]{1,0:T(8,128)(2,1)S(1)}, bf16[896,512]{1,0:T(8,128)(2,1)}, u32[]{:S(2)}) copy-start(bf16[896,512]{1,0:T(8,128)(2,1)} %refs_4_.1) | copy-start | bytes 2752516
  45.3 25.3 %collective-permute-start.8 = (bf16[256,1792]{1,0:T(8,128)(2,1)}, bf16[256,1792]{1,0:T(8,128)(2,1)}, u32[]{:S(2)}, u32[]{:S(2)}) collective-permute-start(bf16[256,1792]{1,0:T(8,128)(2,1)} %shard_map.99), channel_id=1, source_target_pairs={{0,16},{1,65},{2,18},{3,67},{4,20},{5,69},{6,22},{7,71},{8,24},{9,... | collective-permute-start | bytes 2752520 | tf_op jit(solution)/shard_map/ppermute | solution.py:71
  47.4 23.2 %collective-permute-start.9 = (bf16[256,1792]{1,0:T(8,128)(2,1)}, bf16[256,1792]{1,0:T(8,128)(2,1)}, u32[]{:S(2)}, u32[]{:S(2)}) collective-permute-start(bf16[256,1792]{1,0:T(8,128)(2,1)} %shard_map.100), channel_id=1, source_target_pairs={{0,48},{1,193},{2,50},{3,195},{4,52},{5,197},{6,54},{7,199},{8,56}... | collective-permute-start | bytes 2752520 | tf_op jit(solution)/shard_map/ppermute | solution.py:71
  63.3 6.5 %copy-start.5 = (bf16[512,896]{1,0:T(8,128)(2,1)S(1)}, bf16[512,896]{1,0:T(8,128)(2,1)}, u32[]{:S(2)}) copy-start(bf16[512,896]{1,0:T(8,128)(2,1)} %refs_1_.9) | copy-start | bytes 2752516
  63.3 6.5 %copy-start.10 = (bf16[8,64,512]{2,1,0:T(8,128)(2,1)S(1)}, bf16[8,64,512]{2,1,0:T(8,128)(2,1)}, u32[]{:S(2)}) copy-start(bf16[8,64,512]{2,1,0:T(8,128)(2,1)} %copy-done.9) | copy-start | bytes 1572868
  63.3 12.5 %collective-permute-start = (bf16[256,896]{1,0:T(8,128)(2,1)S(1)}, bf16[256,896]{1,0:T(8,128)(2,1)S(1)}, u32[]{:S(2)}, u32[]{:S(2)}) collective-permute-start(bf16[256,896]{1,0:T(8,128)(2,1)S(1)} %shard_map.93.refs_4_), channel_id=1, source_target_pairs={{0,32},{1,129},{2,34},{3,131},{4,36},{5,133},{6,38},{7,135},{8,40}... | collective-permute-start | bytes 1376264 | tf_op jit(solution)/shard_map/ppermute | solution.py:71
  67.1 11.6 %collective-permute-start.1 = (bf16[256,896]{1,0:T(8,128)(2,1)S(1)}, bf16[256,896]{1,0:T(8,128)(2,1)S(1)}, u32[]{:S(2)}, u32[]{:S(2)}) collective-permute-start(bf16[256,896]{1,0:T(8,128)(2,1)S(1)} %shard_map.94.refs_5_), channel_id=1, source_target_pairs={{0,16},{1,65},{2,18},{3,67},{4,20},{5,69},{6,22},{7,71},{8,24},{9,... | collective-permute-start | bytes 1376264 | tf_op jit(solution)/shard_map/ppermute | solution.py:71
  67.5 11.3 %collective-permute-start.2 = (bf16[256,896]{1,0:T(8,128)(2,1)S(1)}, bf16[256,896]{1,0:T(8,128)(2,1)S(1)}, u32[]{:S(2)}, u32[]{:S(2)}) collective-permute-start(bf16[256,896]{1,0:T(8,128)(2,1)S(1)} %shard_map.95.refs_6_), channel_id=1, source_target_pairs={{0,48},{1,193},{2,50},{3,195},{4,52},{5,197},{6,54},{7,199},{8,56}... | collective-permute-start | bytes 1376264 | tf_op jit(solution)/shard_map/ppermute | solution.py:71
  70.6 7.7 %copy-start.1 = (bf16[1024,512]{1,0:T(8,128)(2,1)S(1)}, bf16[1024,512]{1,0:T(8,128)(2,1)}, u32[]{:S(2)}) copy-start(bf16[1024,512]{1,0:T(8,128)(2,1)} %all-gather.3.cloned.1.call-done) | copy-start | bytes 3145732
  72.8 13.4 %collective-permute-start.10 = (f32[64,1792]{1,0:T(8,128)S(1)}, f32[64,1792]{1,0:T(8,128)S(1)}, u32[]{:S(2)}, u32[]{:S(2)}) collective-permute-start(f32[64,1792]{1,0:T(8,128)S(1)} %get-tuple-element.36), channel_id=1, source_target_pairs={{0,128},{1,33},{2,130},{3,35},{4,132},{5,37},{6,134},{7,39},{8,136... | collective-permute-start | bytes 1376264 | tf_op jit(solution)/shard_map/ppermute | solution.py:75
  75.6 13.3 %collective-permute-start.11 = (f32[64,1792]{1,0:T(8,128)S(1)}, f32[64,1792]{1,0:T(8,128)S(1)}, u32[]{:S(2)}, u32[]{:S(2)}) collective-permute-start(f32[64,1792]{1,0:T(8,128)S(1)} %get-tuple-element.37), channel_id=1, source_target_pairs={{0,64},{1,17},{2,66},{3,19},{4,68},{5,21},{6,70},{7,23},{8,72},{9,... | collective-permute-start | bytes 1376264 | tf_op jit(solution)/shard_map/ppermute | solution.py:75
  75.9 13.0 %collective-permute-start.12 = (f32[64,1792]{1,0:T(8,128)S(1)}, f32[64,1792]{1,0:T(8,128)S(1)}, u32[]{:S(2)}, u32[]{:S(2)}) collective-permute-start(f32[64,1792]{1,0:T(8,128)S(1)} %get-tuple-element.38), channel_id=1, source_target_pairs={{0,192},{1,49},{2,194},{3,51},{4,196},{5,53},{6,198},{7,55},{8,200... | collective-permute-start | bytes 1376264 | tf_op jit(solution)/shard_map/ppermute | solution.py:75
  78.9 12.1 %collective-permute-start.3 = (f32[64,896]{1,0:T(8,128)S(1)}, f32[64,896]{1,0:T(8,128)S(1)}, u32[]{:S(2)}, u32[]{:S(2)}) collective-permute-start(f32[64,896]{1,0:T(8,128)S(1)} %get-tuple-element.32), channel_id=1, source_target_pairs={{0,128},{1,33},{2,130},{3,35},{4,132},{5,37},{6,134},{7,39},{8,136... | collective-permute-start | bytes 688136 | tf_op jit(solution)/shard_map/ppermute | solution.py:75
  86.2 6.7 %collective-permute-start.4 = (f32[64,896]{1,0:T(8,128)S(1)}, f32[64,896]{1,0:T(8,128)S(1)}, u32[]{:S(2)}, u32[]{:S(2)}) collective-permute-start(f32[64,896]{1,0:T(8,128)S(1)} %get-tuple-element.33), channel_id=1, source_target_pairs={{0,64},{1,17},{2,66},{3,19},{4,68},{5,21},{6,70},{7,23},{8,72},{9,... | collective-permute-start | bytes 688136 | tf_op jit(solution)/shard_map/ppermute | solution.py:75
  86.2 6.8 %collective-permute-start.5 = (f32[64,896]{1,0:T(8,128)S(1)}, f32[64,896]{1,0:T(8,128)S(1)}, u32[]{:S(2)}, u32[]{:S(2)}) collective-permute-start(f32[64,896]{1,0:T(8,128)S(1)} %get-tuple-element.34), channel_id=1, source_target_pairs={{0,192},{1,49},{2,194},{3,51},{4,196},{5,53},{6,198},{7,55},{8,200... | collective-permute-start | bytes 688136 | tf_op jit(solution)/shard_map/ppermute | solution.py:75
  89.1 6.5 %collective-permute-start.18 = (bf16[64,896]{1,0:T(8,128)(2,1)S(1)}, bf16[64,896]{1,0:T(8,128)(2,1)S(1)}, u32[]{:S(2)}, u32[]{:S(2)}) collective-permute-start(bf16[64,896]{1,0:T(8,128)(2,1)S(1)} %get-tuple-element.41.refs_0_), channel_id=1, source_target_pairs={{0,192},{1,49},{2,194},{3,51},{4,196},{5,53},{6,198},{7,55},{8,200... | collective-permute-start | bytes 344072 | tf_op jit(solution)/shard_map/ppermute | solution.py:75
  90.4 5.2 %collective-permute-start.19 = (bf16[64,896]{1,0:T(8,128)(2,1)S(1)}, bf16[64,896]{1,0:T(8,128)(2,1)S(1)}, u32[]{:S(2)}, u32[]{:S(2)}) collective-permute-start(bf16[64,896]{1,0:T(8,128)(2,1)S(1)} %get-tuple-element.41.refs_0_), channel_id=1, source_target_pairs={{0,128},{1,33},{2,130},{3,35},{4,132},{5,37},{6,134},{7,39},{8,136... | collective-permute-start | bytes 344072 | tf_op jit(solution)/shard_map/ppermute | solution.py:75
  91.0 5.7 %collective-permute-start.20 = (bf16[64,896]{1,0:T(8,128)(2,1)S(1)}, bf16[64,896]{1,0:T(8,128)(2,1)S(1)}, u32[]{:S(2)}, u32[]{:S(2)}) collective-permute-start(bf16[64,896]{1,0:T(8,128)(2,1)S(1)} %get-tuple-element.41.refs_0_), channel_id=1, source_target_pairs={{0,64},{1,17},{2,66},{3,19},{4,68},{5,21},{6,70},{7,23},{8,72},{9,... | collective-permute-start | bytes 344072 | tf_op jit(solution)/shard_map/ppermute | solution.py:75
  93.1 10.8 %collective-permute-start.13 = (bf16[64,1792]{1,0:T(8,128)(2,1)S(1)}, bf16[64,1792]{1,0:T(8,128)(2,1)S(1)}, u32[]{:S(2)}, u32[]{:S(2)}) collective-permute-start(bf16[64,1792]{1,0:T(8,128)(2,1)S(1)} %shard_map.103.refs_0_), channel_id=1, source_target_pairs={{0,192},{1,49},{2,194},{3,51},{4,196},{5,53},{6,198},{7,55},{8,200... | collective-permute-start | bytes 688136 | tf_op jit(solution)/shard_map/ppermute | solution.py:75
  96.8 21.6 %copy-start.13 = (bf16[256,896]{1,0:T(8,128)(2,1)}, bf16[256,896]{1,0:T(8,128)(2,1)S(1)}, u32[]{:S(2)}) copy-start(bf16[256,896]{1,0:T(8,128)(2,1)S(1)} %shard_map.106.refs_0_) | copy-start | bytes 1376260
  96.8 20.3 %collective-permute-start.21 = (bf16[256,896]{1,0:T(8,128)(2,1)S(1)}, bf16[256,896]{1,0:T(8,128)(2,1)S(1)}, u32[]{:S(2)}, u32[]{:S(2)}) collective-permute-start(bf16[256,896]{1,0:T(8,128)(2,1)S(1)} %shard_map.106.refs_0_), channel_id=1, source_target_pairs={{0,48},{1,193},{2,50},{3,195},{4,52},{5,197},{6,54},{7,199},{8,56}... | collective-permute-start | bytes 1376264 | tf_op jit(solution)/shard_map/ppermute | solution.py:71
  99.6 17.5 %collective-permute-start.22 = (bf16[256,896]{1,0:T(8,128)(2,1)S(1)}, bf16[256,896]{1,0:T(8,128)(2,1)S(1)}, u32[]{:S(2)}, u32[]{:S(2)}) collective-permute-start(bf16[256,896]{1,0:T(8,128)(2,1)S(1)} %shard_map.106.refs_0_), channel_id=1, source_target_pairs={{0,32},{1,129},{2,34},{3,131},{4,36},{5,133},{6,38},{7,135},{8,40}... | collective-permute-start | bytes 1376264 | tf_op jit(solution)/shard_map/ppermute | solution.py:71
  100.8 16.3 %collective-permute-start.23 = (bf16[256,896]{1,0:T(8,128)(2,1)S(1)}, bf16[256,896]{1,0:T(8,128)(2,1)S(1)}, u32[]{:S(2)}, u32[]{:S(2)}) collective-permute-start(bf16[256,896]{1,0:T(8,128)(2,1)S(1)} %shard_map.106.refs_0_), channel_id=1, source_target_pairs={{0,16},{1,65},{2,18},{3,67},{4,20},{5,69},{6,22},{7,71},{8,24},{9,... | collective-permute-start | bytes 1376264 | tf_op jit(solution)/shard_map/ppermute | solution.py:71
  101.6 6.4 %collective-permute-start.14 = (bf16[64,1792]{1,0:T(8,128)(2,1)S(1)}, bf16[64,1792]{1,0:T(8,128)(2,1)S(1)}, u32[]{:S(2)}, u32[]{:S(2)}) collective-permute-start(bf16[64,1792]{1,0:T(8,128)(2,1)S(1)} %shard_map.103.refs_0_), channel_id=1, source_target_pairs={{0,128},{1,33},{2,130},{3,35},{4,132},{5,37},{6,134},{7,39},{8,136... | collective-permute-start | bytes 688136 | tf_op jit(solution)/shard_map/ppermute | solution.py:75
  103.8 13.2 %collective-permute-start.15 = (bf16[64,1792]{1,0:T(8,128)(2,1)S(1)}, bf16[64,1792]{1,0:T(8,128)(2,1)S(1)}, u32[]{:S(2)}, u32[]{:S(2)}) collective-permute-start(bf16[64,1792]{1,0:T(8,128)(2,1)S(1)} %shard_map.103.refs_0_), channel_id=1, source_target_pairs={{0,64},{1,17},{2,66},{3,19},{4,68},{5,21},{6,70},{7,23},{8,72},{9,... | collective-permute-start | bytes 688136 | tf_op jit(solution)/shard_map/ppermute | solution.py:75
  119.8 2.7 %copy-start.6 = (bf16[512,896]{1,0:T(8,128)(2,1)S(1)}, bf16[512,896]{1,0:T(8,128)(2,1)}, u32[]{:S(2)}) copy-start(bf16[512,896]{1,0:T(8,128)(2,1)} %refs_1_.9) | copy-start | bytes 2752516
  119.8 3.2 %copy-start.14 = (bf16[256,896]{1,0:T(8,128)(2,1)S(1)}, bf16[256,896]{1,0:T(8,128)(2,1)}, u32[]{:S(2)}) copy-start(bf16[256,896]{1,0:T(8,128)(2,1)} %copy-done.13) | copy-start | bytes 1376260
  119.8 3.2 %copy-start.22 = (bf16[256,896]{1,0:T(8,128)(2,1)S(1)}, bf16[256,896]{1,0:T(8,128)(2,1)}, u32[]{:S(2)}) copy-start(bf16[256,896]{1,0:T(8,128)(2,1)} %copy-done.21) | copy-start | bytes 1376260
  119.8 3.2 %copy-start.24 = (bf16[256,896]{1,0:T(8,128)(2,1)S(1)}, bf16[256,896]{1,0:T(8,128)(2,1)}, u32[]{:S(2)}) copy-start(bf16[256,896]{1,0:T(8,128)(2,1)} %copy-done.23) | copy-start | bytes 1376260
  119.8 3.2 %copy-start.26 = (bf16[256,896]{1,0:T(8,128)(2,1)S(1)}, bf16[256,896]{1,0:T(8,128)(2,1)}, u32[]{:S(2)}) copy-start(bf16[256,896]{1,0:T(8,128)(2,1)} %copy-done.25) | copy-start | bytes 1376260
  119.9 22.2 %collective-permute-start.16 = (bf16[256,1792]{1,0:T(8,128)(2,1)}, bf16[256,1792]{1,0:T(8,128)(2,1)S(1)}, u32[]{:S(2)}, u32[]{:S(2)}) collective-permute-start(bf16[256,1792]{1,0:T(8,128)(2,1)} %copy-done.7), channel_id=1, source_target_pairs={{0,48},{1,193},{2,50},{3,195},{4,52},{5,197},{6,54},{7,199},{8,56}... | collective-permute-start | bytes 2752520 | tf_op jit(solution)/shard_map/ppermute | solution.py:71
  121.5 20.5 %collective-permute-start.17 = (bf16[256,1792]{1,0:T(8,128)(2,1)}, bf16[256,1792]{1,0:T(8,128)(2,1)S(1)}, u32[]{:S(2)}, u32[]{:S(2)}) collective-permute-start(bf16[256,1792]{1,0:T(8,128)(2,1)} %copy-done.7), channel_id=1, source_target_pairs={{0,32},{1,129},{2,34},{3,131},{4,36},{5,133},{6,38},{7,135},{8,40}... | collective-permute-start | bytes 2752520 | tf_op jit(solution)/shard_map/ppermute | solution.py:71
  122.4 27.9 %collective-permute-start.25 = (bf16[256,1792]{1,0:T(8,128)(2,1)}, bf16[256,1792]{1,0:T(8,128)(2,1)S(1)}, u32[]{:S(2)}, u32[]{:S(2)}) collective-permute-start(bf16[256,1792]{1,0:T(8,128)(2,1)} %copy-done.7), channel_id=1, source_target_pairs={{0,16},{1,65},{2,18},{3,67},{4,20},{5,69},{6,22},{7,71},{8,24},{9,... | collective-permute-start | bytes 2752520 | tf_op jit(solution)/shard_map/ppermute | solution.py:71
  123.0 19.0 %copy-start.8 = (bf16[256,1792]{1,0:T(8,128)(2,1)S(1)}, bf16[256,1792]{1,0:T(8,128)(2,1)}, u32[]{:S(2)}) copy-start(bf16[256,1792]{1,0:T(8,128)(2,1)} %copy-done.7) | copy-start | bytes 2752516
  144.3 9.6 %collective-permute-start.24 = (f32[8,64,512]{2,1,0:T(8,128)S(1)}, f32[8,64,512]{2,1,0:T(8,128)S(1)}, u32[]{:S(2)}, u32[]{:S(2)}) collective-permute-start(f32[8,64,512]{2,1,0:T(8,128)S(1)} %get-tuple-element.44), channel_id=1, source_target_pairs={{0,1},{1,0},{2,3},{3,2},{4,5},{5,4},{6,7},{7,6},{8,9},{9,8},{10,11... | collective-permute-start | bytes 3145736 | tf_op jit(solution)/shard_map/ppermute | solution.py:79
  150.3 3.7 %copy-start.19 = (bf16[256,1792]{1,0:T(8,128)(2,1)}, bf16[256,1792]{1,0:T(8,128)(2,1)S(1)}, u32[]{:S(2)}) copy-start(bf16[256,1792]{1,0:T(8,128)(2,1)S(1)} %collective-permute-done.25.refs_0_.refs_3_) | copy-start | bytes 2752516
  151.1 2.8 %collective-permute-start.26 = (f32[2,64,512]{2,1,0:T(8,128)S(1)}, f32[2,64,512]{2,1,0:T(8,128)S(1)}, u32[]{:S(2)}, u32[]{:S(2)}) collective-permute-start(f32[2,64,512]{2,1,0:T(8,128)S(1)} %get-tuple-element.46), channel_id=1, source_target_pairs={{0,1},{1,0},{2,3},{3,2},{4,5},{5,4},{6,7},{7,6},{8,9},{9,8},{10,11... | collective-permute-start | bytes 786440 | tf_op jit(solution)/shard_map/ppermute | solution.py:79
  153.8 5.1 %copy-start.11 = (bf16[8,64,512]{2,1,0:T(8,128)(2,1)S(1)}, bf16[8,64,512]{2,1,0:T(8,128)(2,1)}, u32[]{:S(2)}) copy-start(bf16[8,64,512]{2,1,0:T(8,128)(2,1)} %copy-done.9) | copy-start | bytes 1572868
  153.8 5.1 %copy-start.16 = (bf16[256,1792]{1,0:T(8,128)(2,1)S(1)}, bf16[256,1792]{1,0:T(8,128)(2,1)}, u32[]{:S(2)}) copy-start(bf16[256,1792]{1,0:T(8,128)(2,1)} %copy-done.15) | copy-start | bytes 2752516
  154.9 21.3 %all-to-all-start.1 = ((bf16[8,64,512]{2,1,0:T(8,128)(2,1)}), bf16[8,64,512]{2,1,0:T(8,128)(2,1)S(1)}, u32[]{:S(2)}, u32[]{:S(2)}) async-start(bf16[8,64,512]{2,1,0:T(8,128)(2,1)} %copy-done.27), calls=%async_computation.1 | async-start | bytes 1048576 | tf_op jit(solution)/shard_map/all_to_all | solution.py:282
  166.3 9.8 %collective-permute-start.27 = (f32[64,512]{1,0:T(8,128)S(1)}, f32[64,512]{1,0:T(8,128)S(1)}, u32[]{:S(2)}, u32[]{:S(2)}) collective-permute-start(f32[64,512]{1,0:T(8,128)S(1)} %get-tuple-element.51), channel_id=1, source_target_pairs={{0,1},{1,0},{2,3},{3,2},{4,5},{5,4},{6,7},{7,6},{8,9},{9,8},{10,11... | collective-permute-start | bytes 393224 | tf_op jit(solution)/shard_map/ppermute | solution.py:79
  (13 other events, 17.7 us)
Sparse Core Ops, SparseCore 0:
  20.6 40.9 all-gather.2
  119.9 40.9 reduce-scatter.1

commit v3 on v2

--- a/solution.py
+++ b/solution.py
@@ -79,7 +79,7 @@
     return lax.ppermute(a, "tensor", [(i, i ^ 1) for i in range(2 * DEPTH)])
 
 
-ORDER = (2, 1, 3)
+ORDER = (1, 3, 2)
 CORES = [[z * 2 + c for z in range(DEPTH)] for c in range(2)]
 
 

time: 184 us -> 181 us (0.984)
  starting transfers between devices: 66.3 us -> 50 us
  waiting for transfers between devices: 71 us -> 83.9 us
    ppermute x12, waiting for transfers between devices: 15.5 us -> 23.1 us  [send_q(): return lax.ppermute(a, BOTH, along(False, k % RING))]
    ppermute x12, starting transfers between devices: 22.9 us -> 17.4 us  [send_q(): return lax.ppermute(a, BOTH, along(False, k % RING))]
    ppermute x4, starting transfers between devices: 11.6 us -> 6.05 us  [send_core(): return lax.ppermute(a, 'tensor', [(i, i ^ 1) for i in range(2 * DEPTH)])]
    ppermute x12, starting transfers between devices: 18.6 us -> 13.4 us  [send_p(): return lax.ppermute(a, BOTH, along(True, k % RING))]
    ppermute x12, waiting for transfers between devices: 16.6 us -> 18.9 us  [send_p(): return lax.ppermute(a, BOTH, along(True, k % RING))]
  transfers between devices with their start and end apart: 32 -> 32, of which waited for: 11 -> 18; matrix products, arithmetic and copies ran while one was open for 0% -> 0% of each run, Pallas kernels for 11% -> 11%
where the time goes in v3:
time: 181 us; the launch traced here: 180 us
  waiting for transfers between devices  83.9 us (46%)
  starting transfers between devices  50 us (28%)
  Pallas kernels  22.3 us (12%)
  between operations  14.5 us (8%)
  local copies, waits for them, and re-layouts  9.7 us (5%)
    ppermute x12, waiting for transfers between devices, send_q(): return lax.ppermute(a, BOTH, along(False, k % RING))  23.1 us
    pallas_call x23, Pallas kernels, call(): pl.pallas_call(run, in_specs=[pl.BlockSpec(memory_space=pltpu.VMEM)] * le...  22.3 us
    ppermute x12, waiting for transfers between devices, send_p(): return lax.ppermute(a, BOTH, along(True, k % RING))  18.9 us
    ppermute x12, starting transfers between devices, send_q(): return lax.ppermute(a, BOTH, along(False, k % RING))  17.4 us
    all_to_all x1, waiting for transfers between devices, gather_z(): lax.all_to_all(copies, 'tensor', 0, 0, tiled=True, axis_index_groups=CORES)  17.2 us
    ppermute x12, starting transfers between devices, send_p(): return lax.ppermute(a, BOTH, along(True, k % RING))  13.4 us
    all_gather x1, waiting for transfers between devices, body(): grads = lax.all_gather(out_grad, 'tensor', axis=0)  13.2 us
    all_to_all x1, starting transfers between devices, gather_z(): lax.all_to_all(copies, 'tensor', 0, 0, tiled=True, axis_index_groups=CORES)  9.01 us
  transfers between devices with their start and end apart: 32, of which 18 were waited for; matrix products, arithmetic and copies ran while one was open for 0% of the time, Pallas kernels for 11%

profile of v3, /device:TPU:1, one launch (start us, length us, event | category | flops | bytes accessed | tf_op | source)
XLA Modules:
  0.0 180.3 jit_solution(5902172138365244482)
XLA Ops:
  7.2 1.8 broadcast_in_dim.3
  8.9 9.0 %all-to-all-start = ((bf16[8,64,512]{2,1,0:T(8,128)(2,1)}), bf16[8,64,512]{2,1,0:T(8,128)(2,1)S(1)}, u32[]{:S(2)}, u32[]{:S(2)}) async-start(bf16[8,64,512]{2,1,0:T(8,128)(2,1)} %broadcast_in_dim.3), calls=%async_computation | async-start | bytes 1048576 | tf_op jit(solution)/shard_map/all_to_all | solution.py:106
  18.7 17.2 %all-to-all-done.refs_0_.refs_4_ = bf16[8,64,512]{2,1,0:T(8,128)(2,1)S(1)} async-done(((bf16[8,64,512]{2,1,0:T(8,128)(2,1)}), bf16[8,64,512]{2,1,0:T(8,128)(2,1)S(1)}, u32[]{:S(2)}, u32[]{:S(2)}) %all-to-all-start) | async-done | bytes 524320 | tf_op jit(solution)/shard_map/all_to_all | solution.py:106
  36.4 1.5 collective-permute-done.6.refs_1_.refs_5_
  37.9 1.2 copy-done.4
  39.1 1.6 shard_map.98
  40.8 1.3 collective-permute-start.7
  42.1 1.6 shard_map.99
  43.7 1.4 collective-permute-start.8
  45.2 1.6 shard_map.100
  46.8 1.6 collective-permute-start.9
  48.4 13.2 %all-gather.3.cloned.1.call-done = bf16[1024,512]{1,0:T(8,128)(2,1)} async-done(((bf16[64,512]{1,0:T(8,128)(2,1)}), bf16[1024,512]{1,0:T(8,128)(2,1)}) %all-gather.3.cloned.1.call-update) | async-done | bytes 1048592 | tf_op jit(solution)/shard_map/all_gather | solution.py:347
  61.6 1.2 copy-done
  63.3 1.3 collective-permute-start
  65.6 1.5 collective-permute-start.1
  67.1 1.5 collective-permute-start.2
  69.4 2.2 %shard_map.101 = (f32[64,1792]{1,0:T(8,128)S(1)}, f32[64,1792]{1,0:T(8,128)S(1)}, f32[64,1792]{1,0:T(8,128)S(1)}, f32[64,1792]{1,0:T(8,128)S(1)}) custom-call(f32[256,1792]{1,0:T(8,128)S(1)} %shard_map.97.refs_0_, bf16[256,1792]{1,0:T(8,128)(2,1)} %collective-permute-done.7.refs_1_, bf16[256,1792]{1,0:T(8,128)(2,1)} %collective-permute-done.8.refs_2_, ...), custom_call_target="tpu_custom_call" | custom-call | tf_op jit(solution)/shard_map/pallas_call | solution.py:39
  71.6 1.2 collective-permute-start.10
  72.8 1.6 collective-permute-start.11
  74.3 1.4 collective-permute-start.12
  76.2 2.0 %collective-permute-done.2.refs_3_ = bf16[256,896]{1,0:T(8,128)(2,1)S(1)} collective-permute-done((bf16[256,896]{1,0:T(8,128)(2,1)S(1)}, bf16[256,896]{1,0:T(8,128)(2,1)S(1)}, u32[]{:S(2)}, u32[]{:S(2)}) %collective-permute-start.2) | collective-permute-done | bytes 458784 | tf_op jit(solution)/shard_map/ppermute | solution.py:71
  78.4 1.9 %collective-permute-start.3 = (f32[64,896]{1,0:T(8,128)S(1)}, f32[64,896]{1,0:T(8,128)S(1)}, u32[]{:S(2)}, u32[]{:S(2)}) collective-permute-start(f32[64,896]{1,0:T(8,128)S(1)} %get-tuple-element.32), channel_id=1, source_target_pairs={{0,64},{1,17},{2,66},{3,19},{4,68},{5,21},{6,70},{7,23},{8,72},{9,... | collective-permute-start | bytes 688136 | tf_op jit(solution)/shard_map/ppermute | solution.py:75
  80.3 2.2 %collective-permute-start.4 = (f32[64,896]{1,0:T(8,128)S(1)}, f32[64,896]{1,0:T(8,128)S(1)}, u32[]{:S(2)}, u32[]{:S(2)}) collective-permute-start(f32[64,896]{1,0:T(8,128)S(1)} %get-tuple-element.33), channel_id=1, source_target_pairs={{0,192},{1,49},{2,194},{3,51},{4,196},{5,53},{6,198},{7,55},{8,200... | collective-permute-start | bytes 688136 | tf_op jit(solution)/shard_map/ppermute | solution.py:75
  82.5 1.1 collective-permute-done.10.refs_1_
  84.2 4.0 %collective-permute-done.11.refs_2_ = f32[64,1792]{1,0:T(8,128)S(1)} collective-permute-done((f32[64,1792]{1,0:T(8,128)S(1)}, f32[64,1792]{1,0:T(8,128)S(1)}, u32[]{:S(2)}, u32[]{:S(2)}) %collective-permute-start.11) | collective-permute-done | bytes 458784 | tf_op jit(solution)/shard_map/ppermute | solution.py:75
  88.5 3.4 %collective-permute-start.18 = (bf16[64,896]{1,0:T(8,128)(2,1)S(1)}, bf16[64,896]{1,0:T(8,128)(2,1)S(1)}, u32[]{:S(2)}, u32[]{:S(2)}) collective-permute-start(bf16[64,896]{1,0:T(8,128)(2,1)S(1)} %get-tuple-element.41.refs_0_), channel_id=1, source_target_pairs={{0,192},{1,49},{2,194},{3,51},{4,196},{5,53},{6,198},{7,55},{8,200... | collective-permute-start | bytes 344072 | tf_op jit(solution)/shard_map/ppermute | solution.py:75
  93.6 3.1 %collective-permute-start.13 = (bf16[64,1792]{1,0:T(8,128)(2,1)S(1)}, bf16[64,1792]{1,0:T(8,128)(2,1)S(1)}, u32[]{:S(2)}, u32[]{:S(2)}) collective-permute-start(bf16[64,1792]{1,0:T(8,128)(2,1)S(1)} %shard_map.103.refs_0_), channel_id=1, source_target_pairs={{0,192},{1,49},{2,194},{3,51},{4,196},{5,53},{6,198},{7,55},{8,200... | collective-permute-start | bytes 688136 | tf_op jit(solution)/shard_map/ppermute | solution.py:75
  97.4 1.2 collective-permute-done.20.refs_3_
  98.6 2.2 %collective-permute-start.21 = (bf16[256,896]{1,0:T(8,128)(2,1)S(1)}, bf16[256,896]{1,0:T(8,128)(2,1)S(1)}, u32[]{:S(2)}, u32[]{:S(2)}) collective-permute-start(bf16[256,896]{1,0:T(8,128)(2,1)S(1)} %shard_map.106.refs_0_), channel_id=1, source_target_pairs={{0,48},{1,193},{2,50},{3,195},{4,52},{5,197},{6,54},{7,199},{8,56}... | collective-permute-start | bytes 1376264 | tf_op jit(solution)/shard_map/ppermute | solution.py:71
  101.7 1.2 collective-permute-start.14
  103.1 7.2 %collective-permute-done.14.refs_2_ = bf16[64,1792]{1,0:T(8,128)(2,1)S(1)} collective-permute-done((bf16[64,1792]{1,0:T(8,128)(2,1)S(1)}, bf16[64,1792]{1,0:T(8,128)(2,1)S(1)}, u32[]{:S(2)}, u32[]{:S(2)}) %collective-permute-start.14) | collective-permute-done | bytes 229408 | tf_op jit(solution)/shard_map/ppermute | solution.py:75
  110.3 7.8 %collective-permute-done.15.refs_3_ = bf16[64,1792]{1,0:T(8,128)(2,1)S(1)} collective-permute-done((bf16[64,1792]{1,0:T(8,128)(2,1)S(1)}, bf16[64,1792]{1,0:T(8,128)(2,1)S(1)}, u32[]{:S(2)}, u32[]{:S(2)}) %collective-permute-start.15) | collective-permute-done | bytes 229408 | tf_op jit(solution)/shard_map/ppermute | solution.py:75
  118.2 1.5 collective-permute-done.23.refs_3_
  119.8 1.2 shard_map.111
  121.1 1.3 copy-done.12
  124.6 2.4 %shard_map.107 = (f32[896,512]{1,0:T(8,128)}, f32[8,128]{1,0:T(8,128)S(1)}) custom-call(bf16[256,896]{1,0:T(8,128)(2,1)S(1)} %copy-done.14, bf16[256,896]{1,0:T(8,128)(2,1)S(1)} %copy-done.22, bf16[256,896]{1,0:T(8,128)(2,1)S(1)} %copy-done.24, bf16[256,896]{1,0:T(8,128)(2,1)S(1)} %copy-done.26, bf16[16,64,512]{2,1,0:T(8,128)(2,1)S(1)} %bitcast.7), custom_call_target="tpu_custom_call" | custom-call | tf_op jit(solution)/shard_map/pallas_call | solution.py:39
  127.0 8.4 %collective-permute-done.16.refs_1_ = bf16[256,1792]{1,0:T(8,128)(2,1)S(1)} collective-permute-done((bf16[256,1792]{1,0:T(8,128)(2,1)}, bf16[256,1792]{1,0:T(8,128)(2,1)S(1)}, u32[]{:S(2)}, u32[]{:S(2)}) %collective-permute-start.16) | collective-permute-done | bytes 917536 | tf_op jit(solution)/shard_map/ppermute | solution.py:71
  135.4 1.8 %collective-permute-done.17.refs_2_ = bf16[256,1792]{1,0:T(8,128)(2,1)S(1)} collective-permute-done((bf16[256,1792]{1,0:T(8,128)(2,1)}, bf16[256,1792]{1,0:T(8,128)(2,1)S(1)}, u32[]{:S(2)}, u32[]{:S(2)}) %collective-permute-start.17) | collective-permute-done | bytes 917536 | tf_op jit(solution)/shard_map/ppermute | solution.py:71
  137.2 2.2 %shard_map.108 = (f32[8,64,512]{2,1,0:T(8,128)S(1)}, f32[8,64,512]{2,1,0:T(8,128)S(1)}) custom-call(bf16[256,1792]{1,0:T(8,128)(2,1)S(1)} %copy-done.8, bf16[256,1792]{1,0:T(8,128)(2,1)S(1)} %collective-permute-done.16.refs_1_, bf16[256,1792]{1,0:T(8,128)(2,1)S(1)} %collective-permute-done.17.refs_2_, bf16[1792,512]{1,0:T(8,128)(2,1)S(1)} %shard_map.105.refs_3_.refs_1_, ...), custom_call_target="tpu_custom_call" | custom-call | tf_op jit(solution)/shard_map/pallas_call | solution.py:39
  139.5 2.5 %collective-permute-start.24 = (f32[8,64,512]{2,1,0:T(8,128)S(1)}, f32[8,64,512]{2,1,0:T(8,128)S(1)}, u32[]{:S(2)}, u32[]{:S(2)}) collective-permute-start(f32[8,64,512]{2,1,0:T(8,128)S(1)} %get-tuple-element.44), channel_id=1, source_target_pairs={{0,1},{1,0},{2,3},{3,2},{4,5},{5,4},{6,7},{7,6},{8,9},{9,8},{10,11... | collective-permute-start | bytes 3145736 | tf_op jit(solution)/shard_map/ppermute | solution.py:79
  142.0 5.2 %collective-permute-done.25.refs_0_.refs_3_ = bf16[256,1792]{1,0:T(8,128)(2,1)S(1)} collective-permute-done((bf16[256,1792]{1,0:T(8,128)(2,1)}, bf16[256,1792]{1,0:T(8,128)(2,1)S(1)}, u32[]{:S(2)}, u32[]{:S(2)}) %collective-permute-start.25) | collective-permute-done | bytes 917536 | tf_op jit(solution)/shard_map/ppermute | solution.py:71
  147.9 2.3 %collective-permute-start.26 = (f32[2,64,512]{2,1,0:T(8,128)S(1)}, f32[2,64,512]{2,1,0:T(8,128)S(1)}, u32[]{:S(2)}, u32[]{:S(2)}) collective-permute-start(f32[2,64,512]{2,1,0:T(8,128)S(1)} %get-tuple-element.46), channel_id=1, source_target_pairs={{0,1},{1,0},{2,3},{3,2},{4,5},{5,4},{6,7},{7,6},{8,9},{9,8},{10,11... | collective-permute-start | bytes 786440 | tf_op jit(solution)/shard_map/ppermute | solution.py:79
  150.2 1.2 collective-permute-done.26.refs_3_
  152.4 4.1 %all-to-all-start.1 = ((bf16[8,64,512]{2,1,0:T(8,128)(2,1)}), bf16[8,64,512]{2,1,0:T(8,128)(2,1)S(1)}, u32[]{:S(2)}, u32[]{:S(2)}) async-start(bf16[8,64,512]{2,1,0:T(8,128)(2,1)} %copy-done.27), calls=%async_computation.1 | async-start | bytes 1048576 | tf_op jit(solution)/shard_map/all_to_all | solution.py:282
  156.5 1.2 copy-done.18
  157.7 1.2 copy-done.20
  158.9 4.0 %shard_map.112 = (f32[512,896]{1,0:T(8,128)}, f32[512,896]{1,0:T(8,128)}, f32[8,128]{1,0:T(8,128)S(1)}) custom-call(bf16[256,1792]{1,0:T(8,128)(2,1)S(1)} %copy-done.8, bf16[256,1792]{1,0:T(8,128)(2,1)S(1)} %copy-done.16, bf16[256,1792]{1,0:T(8,128)(2,1)S(1)} %copy-done.18, bf16[256,1792]{1,0:T(8,128)(2,1)S(1)} %copy-done.20, ...), custom_call_target="tpu_custom_call" | custom-call | tf_op jit(solution)/shard_map/pallas_call | solution.py:39
  164.6 8.1 %all-to-all-done.1.refs_1_ = bf16[8,64,512]{2,1,0:T(8,128)(2,1)S(1)} async-done(((bf16[8,64,512]{2,1,0:T(8,128)(2,1)}), bf16[8,64,512]{2,1,0:T(8,128)(2,1)S(1)}, u32[]{:S(2)}, u32[]{:S(2)}) %all-to-all-start.1) | async-done | bytes 524320 | tf_op jit(solution)/shard_map/all_to_all | solution.py:282
  (100 shorter events, 14.7 us)
Async XLA Ops:
  7.2 30.8 %copy-start.3 = (bf16[512,896]{1,0:T(8,128)(2,1)S(1)}, bf16[512,896]{1,0:T(8,128)(2,1)}, u32[]{:S(2)}) copy-start(bf16[512,896]{1,0:T(8,128)(2,1)} %refs_0_.1) | copy-start | bytes 2752516
  8.9 27.0 %all-to-all-start = ((bf16[8,64,512]{2,1,0:T(8,128)(2,1)}), bf16[8,64,512]{2,1,0:T(8,128)(2,1)S(1)}, u32[]{:S(2)}, u32[]{:S(2)}) async-start(bf16[8,64,512]{2,1,0:T(8,128)(2,1)} %broadcast_in_dim.3), calls=%async_computation | async-start | bytes 1048576 | tf_op jit(solution)/shard_map/all_to_all | solution.py:106
  17.9 43.7 %all-gather.3.cloned.1.call-start = ((), (), s32[]{:S(2)}) async-start(), calls=%async_computation.4 | async-start | bytes 1114112 | tf_op jit(solution)/shard_map/all_gather | solution.py:347
  18.7 144.2 %reduce-scatter.2.cloned.1.call-start = ((), (), s32[]{:S(2)}) async-start(), calls=%async_computation.3 | async-start | bytes 2359296 | tf_op jit(solution)/shard_map/reduce_scatter | solution.py:365
  35.9 2.0 %collective-permute-start.6 = (bf16[8,64,512]{2,1,0:T(8,128)(2,1)S(1)}, bf16[8,64,512]{2,1,0:T(8,128)(2,1)S(1)}, u32[]{:S(2)}, u32[]{:S(2)}) collective-permute-start(bf16[8,64,512]{2,1,0:T(8,128)(2,1)S(1)} %all-to-all-done.refs_0_.refs_4_), channel_id=1, source_target_pairs={{0,1},{1,0},{2,3},{3,2},{4,5},{5,4},{6,7},{7,6},{8,9},{9,8},{10,11... | collective-permute-start | bytes 1572872 | tf_op jit(solution)/shard_map/ppermute | solution.py:79
  39.1 6.0 %copy-start.9 = (bf16[8,64,512]{2,1,0:T(8,128)(2,1)}, bf16[8,64,512]{2,1,0:T(8,128)(2,1)S(1)}, u32[]{:S(2)}) copy-start(bf16[8,64,512]{2,1,0:T(8,128)(2,1)S(1)} %collective-permute-done.6.refs_1_.refs_5_) | copy-start | bytes 1572868
  40.8 26.3 %collective-permute-start.7 = (bf16[256,1792]{1,0:T(8,128)(2,1)}, bf16[256,1792]{1,0:T(8,128)(2,1)}, u32[]{:S(2)}, u32[]{:S(2)}) collective-permute-start(bf16[256,1792]{1,0:T(8,128)(2,1)} %shard_map.98), channel_id=1, source_target_pairs={{0,16},{1,65},{2,18},{3,67},{4,20},{5,69},{6,22},{7,71},{8,24},{9,... | collective-permute-start | bytes 2752520 | tf_op jit(solution)/shard_map/ppermute | solution.py:71
  43.7 17.9 %copy-start.2 = (bf16[896,512]{1,0:T(8,128)(2,1)S(1)}, bf16[896,512]{1,0:T(8,128)(2,1)}, u32[]{:S(2)}) copy-start(bf16[896,512]{1,0:T(8,128)(2,1)} %refs_4_.1) | copy-start | bytes 2752516
  43.7 25.6 %collective-permute-start.8 = (bf16[256,1792]{1,0:T(8,128)(2,1)}, bf16[256,1792]{1,0:T(8,128)(2,1)}, u32[]{:S(2)}, u32[]{:S(2)}) collective-permute-start(bf16[256,1792]{1,0:T(8,128)(2,1)} %shard_map.99), channel_id=1, source_target_pairs={{0,48},{1,193},{2,50},{3,195},{4,52},{5,197},{6,54},{7,199},{8,56}... | collective-permute-start | bytes 2752520 | tf_op jit(solution)/shard_map/ppermute | solution.py:71
  46.8 22.6 %collective-permute-start.9 = (bf16[256,1792]{1,0:T(8,128)(2,1)}, bf16[256,1792]{1,0:T(8,128)(2,1)}, u32[]{:S(2)}, u32[]{:S(2)}) collective-permute-start(bf16[256,1792]{1,0:T(8,128)(2,1)} %shard_map.100), channel_id=1, source_target_pairs={{0,32},{1,129},{2,34},{3,131},{4,36},{5,133},{6,38},{7,135},{8,40}... | collective-permute-start | bytes 2752520 | tf_op jit(solution)/shard_map/ppermute | solution.py:71
  63.3 5.3 %copy-start.5 = (bf16[512,896]{1,0:T(8,128)(2,1)S(1)}, bf16[512,896]{1,0:T(8,128)(2,1)}, u32[]{:S(2)}) copy-start(bf16[512,896]{1,0:T(8,128)(2,1)} %refs_1_.9) | copy-start | bytes 2752516
  63.3 5.3 %copy-start.10 = (bf16[8,64,512]{2,1,0:T(8,128)(2,1)S(1)}, bf16[8,64,512]{2,1,0:T(8,128)(2,1)}, u32[]{:S(2)}) copy-start(bf16[8,64,512]{2,1,0:T(8,128)(2,1)} %copy-done.9) | copy-start | bytes 1572868
  63.3 11.0 %collective-permute-start = (bf16[256,896]{1,0:T(8,128)(2,1)S(1)}, bf16[256,896]{1,0:T(8,128)(2,1)S(1)}, u32[]{:S(2)}, u32[]{:S(2)}) collective-permute-start(bf16[256,896]{1,0:T(8,128)(2,1)S(1)} %shard_map.93.refs_4_), channel_id=1, source_target_pairs={{0,16},{1,65},{2,18},{3,67},{4,20},{5,69},{6,22},{7,71},{8,24},{9,... | collective-permute-start | bytes 1376264 | tf_op jit(solution)/shard_map/ppermute | solution.py:71
  65.6 10.7 %collective-permute-start.1 = (bf16[256,896]{1,0:T(8,128)(2,1)S(1)}, bf16[256,896]{1,0:T(8,128)(2,1)S(1)}, u32[]{:S(2)}, u32[]{:S(2)}) collective-permute-start(bf16[256,896]{1,0:T(8,128)(2,1)S(1)} %shard_map.94.refs_5_), channel_id=1, source_target_pairs={{0,48},{1,193},{2,50},{3,195},{4,52},{5,197},{6,54},{7,199},{8,56}... | collective-permute-start | bytes 1376264 | tf_op jit(solution)/shard_map/ppermute | solution.py:71
  67.1 11.1 %collective-permute-start.2 = (bf16[256,896]{1,0:T(8,128)(2,1)S(1)}, bf16[256,896]{1,0:T(8,128)(2,1)S(1)}, u32[]{:S(2)}, u32[]{:S(2)}) collective-permute-start(bf16[256,896]{1,0:T(8,128)(2,1)S(1)} %shard_map.95.refs_6_), channel_id=1, source_target_pairs={{0,32},{1,129},{2,34},{3,131},{4,36},{5,133},{6,38},{7,135},{8,40}... | collective-permute-start | bytes 1376264 | tf_op jit(solution)/shard_map/ppermute | solution.py:71
  69.4 6.4 %copy-start.1 = (bf16[1024,512]{1,0:T(8,128)(2,1)S(1)}, bf16[1024,512]{1,0:T(8,128)(2,1)}, u32[]{:S(2)}) copy-start(bf16[1024,512]{1,0:T(8,128)(2,1)} %all-gather.3.cloned.1.call-done) | copy-start | bytes 3145732
  71.6 12.1 %collective-permute-start.10 = (f32[64,1792]{1,0:T(8,128)S(1)}, f32[64,1792]{1,0:T(8,128)S(1)}, u32[]{:S(2)}, u32[]{:S(2)}) collective-permute-start(f32[64,1792]{1,0:T(8,128)S(1)} %get-tuple-element.36), channel_id=1, source_target_pairs={{0,64},{1,17},{2,66},{3,19},{4,68},{5,21},{6,70},{7,23},{8,72},{9,... | collective-permute-start | bytes 1376264 | tf_op jit(solution)/shard_map/ppermute | solution.py:75
  72.8 15.5 %collective-permute-start.11 = (f32[64,1792]{1,0:T(8,128)S(1)}, f32[64,1792]{1,0:T(8,128)S(1)}, u32[]{:S(2)}, u32[]{:S(2)}) collective-permute-start(f32[64,1792]{1,0:T(8,128)S(1)} %get-tuple-element.37), channel_id=1, source_target_pairs={{0,192},{1,49},{2,194},{3,51},{4,196},{5,53},{6,198},{7,55},{8,200... | collective-permute-start | bytes 1376264 | tf_op jit(solution)/shard_map/ppermute | solution.py:75
  74.3 14.1 %collective-permute-start.12 = (f32[64,1792]{1,0:T(8,128)S(1)}, f32[64,1792]{1,0:T(8,128)S(1)}, u32[]{:S(2)}, u32[]{:S(2)}) collective-permute-start(f32[64,1792]{1,0:T(8,128)S(1)} %get-tuple-element.38), channel_id=1, source_target_pairs={{0,128},{1,33},{2,130},{3,35},{4,132},{5,37},{6,134},{7,39},{8,136... | collective-permute-start | bytes 1376264 | tf_op jit(solution)/shard_map/ppermute | solution.py:75
  78.4 14.2 %collective-permute-start.3 = (f32[64,896]{1,0:T(8,128)S(1)}, f32[64,896]{1,0:T(8,128)S(1)}, u32[]{:S(2)}, u32[]{:S(2)}) collective-permute-start(f32[64,896]{1,0:T(8,128)S(1)} %get-tuple-element.32), channel_id=1, source_target_pairs={{0,64},{1,17},{2,66},{3,19},{4,68},{5,21},{6,70},{7,23},{8,72},{9,... | collective-permute-start | bytes 688136 | tf_op jit(solution)/shard_map/ppermute | solution.py:75
  80.3 12.3 %collective-permute-start.4 = (f32[64,896]{1,0:T(8,128)S(1)}, f32[64,896]{1,0:T(8,128)S(1)}, u32[]{:S(2)}, u32[]{:S(2)}) collective-permute-start(f32[64,896]{1,0:T(8,128)S(1)} %get-tuple-element.33), channel_id=1, source_target_pairs={{0,192},{1,49},{2,194},{3,51},{4,196},{5,53},{6,198},{7,55},{8,200... | collective-permute-start | bytes 688136 | tf_op jit(solution)/shard_map/ppermute | solution.py:75
  83.7 9.9 %collective-permute-start.5 = (f32[64,896]{1,0:T(8,128)S(1)}, f32[64,896]{1,0:T(8,128)S(1)}, u32[]{:S(2)}, u32[]{:S(2)}) collective-permute-start(f32[64,896]{1,0:T(8,128)S(1)} %get-tuple-element.34), channel_id=1, source_target_pairs={{0,128},{1,33},{2,130},{3,35},{4,132},{5,37},{6,134},{7,39},{8,136... | collective-permute-start | bytes 688136 | tf_op jit(solution)/shard_map/ppermute | solution.py:75
  88.5 8.2 %collective-permute-start.18 = (bf16[64,896]{1,0:T(8,128)(2,1)S(1)}, bf16[64,896]{1,0:T(8,128)(2,1)S(1)}, u32[]{:S(2)}, u32[]{:S(2)}) collective-permute-start(bf16[64,896]{1,0:T(8,128)(2,1)S(1)} %get-tuple-element.41.refs_0_), channel_id=1, source_target_pairs={{0,192},{1,49},{2,194},{3,51},{4,196},{5,53},{6,198},{7,55},{8,200... | collective-permute-start | bytes 344072 | tf_op jit(solution)/shard_map/ppermute | solution.py:75
  91.9 5.4 %collective-permute-start.19 = (bf16[64,896]{1,0:T(8,128)(2,1)S(1)}, bf16[64,896]{1,0:T(8,128)(2,1)S(1)}, u32[]{:S(2)}, u32[]{:S(2)}) collective-permute-start(bf16[64,896]{1,0:T(8,128)(2,1)S(1)} %get-tuple-element.41.refs_0_), channel_id=1, source_target_pairs={{0,128},{1,33},{2,130},{3,35},{4,132},{5,37},{6,134},{7,39},{8,136... | collective-permute-start | bytes 344072 | tf_op jit(solution)/shard_map/ppermute | solution.py:75
  92.6 6.0 %collective-permute-start.20 = (bf16[64,896]{1,0:T(8,128)(2,1)S(1)}, bf16[64,896]{1,0:T(8,128)(2,1)S(1)}, u32[]{:S(2)}, u32[]{:S(2)}) collective-permute-start(bf16[64,896]{1,0:T(8,128)(2,1)S(1)} %get-tuple-element.41.refs_0_), channel_id=1, source_target_pairs={{0,64},{1,17},{2,66},{3,19},{4,68},{5,21},{6,70},{7,23},{8,72},{9,... | collective-permute-start | bytes 344072 | tf_op jit(solution)/shard_map/ppermute | solution.py:75
  93.6 9.3 %collective-permute-start.13 = (bf16[64,1792]{1,0:T(8,128)(2,1)S(1)}, bf16[64,1792]{1,0:T(8,128)(2,1)S(1)}, u32[]{:S(2)}, u32[]{:S(2)}) collective-permute-start(bf16[64,1792]{1,0:T(8,128)(2,1)S(1)} %shard_map.103.refs_0_), channel_id=1, source_target_pairs={{0,192},{1,49},{2,194},{3,51},{4,196},{5,53},{6,198},{7,55},{8,200... | collective-permute-start | bytes 688136 | tf_op jit(solution)/shard_map/ppermute | solution.py:75
  98.6 22.4 %copy-start.13 = (bf16[256,896]{1,0:T(8,128)(2,1)}, bf16[256,896]{1,0:T(8,128)(2,1)S(1)}, u32[]{:S(2)}) copy-start(bf16[256,896]{1,0:T(8,128)(2,1)S(1)} %shard_map.106.refs_0_) | copy-start | bytes 1376260
  98.6 19.6 %collective-permute-start.21 = (bf16[256,896]{1,0:T(8,128)(2,1)S(1)}, bf16[256,896]{1,0:T(8,128)(2,1)S(1)}, u32[]{:S(2)}, u32[]{:S(2)}) collective-permute-start(bf16[256,896]{1,0:T(8,128)(2,1)S(1)} %shard_map.106.refs_0_), channel_id=1, source_target_pairs={{0,48},{1,193},{2,50},{3,195},{4,52},{5,197},{6,54},{7,199},{8,56}... | collective-permute-start | bytes 1376264 | tf_op jit(solution)/shard_map/ppermute | solution.py:71
  100.9 17.3 %collective-permute-start.22 = (bf16[256,896]{1,0:T(8,128)(2,1)S(1)}, bf16[256,896]{1,0:T(8,128)(2,1)S(1)}, u32[]{:S(2)}, u32[]{:S(2)}) collective-permute-start(bf16[256,896]{1,0:T(8,128)(2,1)S(1)} %shard_map.106.refs_0_), channel_id=1, source_target_pairs={{0,32},{1,129},{2,34},{3,131},{4,36},{5,133},{6,38},{7,135},{8,40}... | collective-permute-start | bytes 1376264 | tf_op jit(solution)/shard_map/ppermute | solution.py:71
  101.1 18.7 %collective-permute-start.23 = (bf16[256,896]{1,0:T(8,128)(2,1)S(1)}, bf16[256,896]{1,0:T(8,128)(2,1)S(1)}, u32[]{:S(2)}, u32[]{:S(2)}) collective-permute-start(bf16[256,896]{1,0:T(8,128)(2,1)S(1)} %shard_map.106.refs_0_), channel_id=1, source_target_pairs={{0,16},{1,65},{2,18},{3,67},{4,20},{5,69},{6,22},{7,71},{8,24},{9,... | collective-permute-start | bytes 1376264 | tf_op jit(solution)/shard_map/ppermute | solution.py:71
  101.7 8.6 %collective-permute-start.14 = (bf16[64,1792]{1,0:T(8,128)(2,1)S(1)}, bf16[64,1792]{1,0:T(8,128)(2,1)S(1)}, u32[]{:S(2)}, u32[]{:S(2)}) collective-permute-start(bf16[64,1792]{1,0:T(8,128)(2,1)S(1)} %shard_map.103.refs_0_), channel_id=1, source_target_pairs={{0,128},{1,33},{2,130},{3,35},{4,132},{5,37},{6,134},{7,39},{8,136... | collective-permute-start | bytes 688136 | tf_op jit(solution)/shard_map/ppermute | solution.py:75
  102.9 15.2 %collective-permute-start.15 = (bf16[64,1792]{1,0:T(8,128)(2,1)S(1)}, bf16[64,1792]{1,0:T(8,128)(2,1)S(1)}, u32[]{:S(2)}, u32[]{:S(2)}) collective-permute-start(bf16[64,1792]{1,0:T(8,128)(2,1)S(1)} %shard_map.103.refs_0_), channel_id=1, source_target_pairs={{0,64},{1,17},{2,66},{3,19},{4,68},{5,21},{6,70},{7,23},{8,72},{9,... | collective-permute-start | bytes 688136 | tf_op jit(solution)/shard_map/ppermute | solution.py:75
  118.2 2.9 %copy-start.7 = (bf16[256,1792]{1,0:T(8,128)(2,1)}, bf16[256,1792]{1,0:T(8,128)(2,1)S(1)}, u32[]{:S(2)}) copy-start(bf16[256,1792]{1,0:T(8,128)(2,1)S(1)} %shard_map.104.refs_0_.refs_5_) | copy-start | bytes 2752516
  118.2 2.8 %copy-start.21 = (bf16[256,896]{1,0:T(8,128)(2,1)}, bf16[256,896]{1,0:T(8,128)(2,1)S(1)}, u32[]{:S(2)}) copy-start(bf16[256,896]{1,0:T(8,128)(2,1)S(1)} %collective-permute-done.21.refs_1_) | copy-start | bytes 1376260
  118.2 2.8 %copy-start.23 = (bf16[256,896]{1,0:T(8,128)(2,1)}, bf16[256,896]{1,0:T(8,128)(2,1)S(1)}, u32[]{:S(2)}) copy-start(bf16[256,896]{1,0:T(8,128)(2,1)S(1)} %collective-permute-done.22.refs_2_) | copy-start | bytes 1376260
  122.5 12.9 %collective-permute-start.16 = (bf16[256,1792]{1,0:T(8,128)(2,1)}, bf16[256,1792]{1,0:T(8,128)(2,1)S(1)}, u32[]{:S(2)}, u32[]{:S(2)}) collective-permute-start(bf16[256,1792]{1,0:T(8,128)(2,1)} %copy-done.7), channel_id=1, source_target_pairs={{0,48},{1,193},{2,50},{3,195},{4,52},{5,197},{6,54},{7,199},{8,56}... | collective-permute-start | bytes 2752520 | tf_op jit(solution)/shard_map/ppermute | solution.py:71
  122.9 14.3 %collective-permute-start.17 = (bf16[256,1792]{1,0:T(8,128)(2,1)}, bf16[256,1792]{1,0:T(8,128)(2,1)S(1)}, u32[]{:S(2)}, u32[]{:S(2)}) collective-permute-start(bf16[256,1792]{1,0:T(8,128)(2,1)} %copy-done.7), channel_id=1, source_target_pairs={{0,32},{1,129},{2,34},{3,131},{4,36},{5,133},{6,38},{7,135},{8,40}... | collective-permute-start | bytes 2752520 | tf_op jit(solution)/shard_map/ppermute | solution.py:71
  123.9 23.2 %collective-permute-start.25 = (bf16[256,1792]{1,0:T(8,128)(2,1)}, bf16[256,1792]{1,0:T(8,128)(2,1)S(1)}, u32[]{:S(2)}, u32[]{:S(2)}) collective-permute-start(bf16[256,1792]{1,0:T(8,128)(2,1)} %copy-done.7), channel_id=1, source_target_pairs={{0,16},{1,65},{2,18},{3,67},{4,20},{5,69},{6,22},{7,71},{8,24},{9,... | collective-permute-start | bytes 2752520 | tf_op jit(solution)/shard_map/ppermute | solution.py:71
  124.6 12.6 %copy-start.8 = (bf16[256,1792]{1,0:T(8,128)(2,1)S(1)}, bf16[256,1792]{1,0:T(8,128)(2,1)}, u32[]{:S(2)}) copy-start(bf16[256,1792]{1,0:T(8,128)(2,1)} %copy-done.7) | copy-start | bytes 2752516
  135.4 4.1 %copy-start.15 = (bf16[256,1792]{1,0:T(8,128)(2,1)}, bf16[256,1792]{1,0:T(8,128)(2,1)S(1)}, u32[]{:S(2)}) copy-start(bf16[256,1792]{1,0:T(8,128)(2,1)S(1)} %collective-permute-done.16.refs_1_) | copy-start | bytes 2752516
  137.2 2.2 %copy-start.17 = (bf16[256,1792]{1,0:T(8,128)(2,1)}, bf16[256,1792]{1,0:T(8,128)(2,1)S(1)}, u32[]{:S(2)}) copy-start(bf16[256,1792]{1,0:T(8,128)(2,1)S(1)} %collective-permute-done.17.refs_2_) | copy-start | bytes 2752516
  139.5 11.9 %collective-permute-start.24 = (f32[8,64,512]{2,1,0:T(8,128)S(1)}, f32[8,64,512]{2,1,0:T(8,128)S(1)}, u32[]{:S(2)}, u32[]{:S(2)}) collective-permute-start(f32[8,64,512]{2,1,0:T(8,128)S(1)} %get-tuple-element.44), channel_id=1, source_target_pairs={{0,1},{1,0},{2,3},{3,2},{4,5},{5,4},{6,7},{7,6},{8,9},{9,8},{10,11... | collective-permute-start | bytes 3145736 | tf_op jit(solution)/shard_map/ppermute | solution.py:79
  147.1 4.5 %copy-start.19 = (bf16[256,1792]{1,0:T(8,128)(2,1)}, bf16[256,1792]{1,0:T(8,128)(2,1)S(1)}, u32[]{:S(2)}) copy-start(bf16[256,1792]{1,0:T(8,128)(2,1)S(1)} %collective-permute-done.25.refs_0_.refs_3_) | copy-start | bytes 2752516
  147.9 3.5 %collective-permute-start.26 = (f32[2,64,512]{2,1,0:T(8,128)S(1)}, f32[2,64,512]{2,1,0:T(8,128)S(1)}, u32[]{:S(2)}, u32[]{:S(2)}) collective-permute-start(f32[2,64,512]{2,1,0:T(8,128)S(1)} %get-tuple-element.46), channel_id=1, source_target_pairs={{0,1},{1,0},{2,3},{3,2},{4,5},{5,4},{6,7},{7,6},{8,9},{9,8},{10,11... | collective-permute-start | bytes 786440 | tf_op jit(solution)/shard_map/ppermute | solution.py:79
  151.4 5.1 %copy-start.11 = (bf16[8,64,512]{2,1,0:T(8,128)(2,1)S(1)}, bf16[8,64,512]{2,1,0:T(8,128)(2,1)}, u32[]{:S(2)}) copy-start(bf16[8,64,512]{2,1,0:T(8,128)(2,1)} %copy-done.9) | copy-start | bytes 1572868
  151.4 5.1 %copy-start.16 = (bf16[256,1792]{1,0:T(8,128)(2,1)S(1)}, bf16[256,1792]{1,0:T(8,128)(2,1)}, u32[]{:S(2)}) copy-start(bf16[256,1792]{1,0:T(8,128)(2,1)} %copy-done.15) | copy-start | bytes 2752516
  152.4 20.3 %all-to-all-start.1 = ((bf16[8,64,512]{2,1,0:T(8,128)(2,1)}), bf16[8,64,512]{2,1,0:T(8,128)(2,1)S(1)}, u32[]{:S(2)}, u32[]{:S(2)}) async-start(bf16[8,64,512]{2,1,0:T(8,128)(2,1)} %copy-done.27), calls=%async_computation.1 | async-start | bytes 1048576 | tf_op jit(solution)/shard_map/all_to_all | solution.py:282
  163.8 8.9 %collective-permute-start.27 = (f32[64,512]{1,0:T(8,128)S(1)}, f32[64,512]{1,0:T(8,128)S(1)}, u32[]{:S(2)}, u32[]{:S(2)}) collective-permute-start(f32[64,512]{1,0:T(8,128)S(1)} %get-tuple-element.51), channel_id=1, source_target_pairs={{0,1},{1,0},{2,3},{3,2},{4,5},{5,4},{6,7},{7,6},{8,9},{9,8},{10,11... | collective-permute-start | bytes 393224 | tf_op jit(solution)/shard_map/ppermute | solution.py:79
  (13 other events, 19.3 us)
Sparse Core Ops, SparseCore 0:
  20.6 40.9 all-gather.2
  122.6 34.4 reduce-scatter.1

commit v4 on v3

--- a/solution.py
+++ b/solution.py
@@ -211,14 +211,15 @@
 def back(blocks, weights, after=()):
     width = weights.shape[1]
     tile = blocks[0].shape[0] // RING
+    *early, late = ORDER
 
     def kernel(a, b, c, weights_ref, mine, other):
-        for i, block in enumerate((a, b, c)):
+        for i, block in zip((0, *early), (a, b, c)):
             store_tiles(mine, other, i, dot(block[...], weights_ref[...], (1, 0)))
-        store_tiles(mine, other, RING - 1, jnp.zeros((RING * tile, width), F32))
+        store_tiles(mine, other, late, jnp.zeros((RING * tile, width), F32))
 
     half = shape((DEPTH, tile, width), F32)
-    return call(kernel, [half, half], *blocks[:-1], weights, after=after)
+    return call(kernel, [half, half], *(blocks[i] for i in (0, *early)), weights, after=after)
 
 
 def back_last(block, weights):
@@ -228,7 +229,7 @@
     def kernel(block_ref, weights_ref, mine, other):
         result = dot(block_ref[...], weights_ref[...], (1, 0))
         for j in range(RING):
-            foreign, z = tile_at(RING - 1, j)
+            foreign, z = tile_at(ORDER[-1], j)
             store_tile(mine, other, foreign, z % 2, result[j * tile : (j + 1) * tile])
 
     half = shape((2, tile, width), F32)
@@ -267,7 +268,7 @@
 
     def split(mine_ref, arrived_ref, mine_last_ref, arrived_last_ref, own, out):
         p, q, z, _ = place()
-        last_mine, last_arrived = (p + RING - 1) % RING, (q + RING - 1) % RING
+        last_mine, last_arrived = (p + ORDER[-1]) % RING, (q + ORDER[-1]) % RING
 
         def total(k):
             a = jnp.where(k // 2 == last_mine, mine_last_ref[k % 2], mine_ref[k])
@@ -368,7 +369,7 @@
     gate_weight_grad, up_weight_grad, mark = token_weight_grads(grad_blocks, *rows_of, factor)
     own, foreign = halves(both, after=[mark])
     done = [own, send_core(foreign)]
-    input_grad, ffn_output = reduce_z(first, back_last(grad_blocks[-1], weights), done)
+    input_grad, ffn_output = reduce_z(first, back_last(grad_blocks[ORDER[-1]], weights), done)
     return ffn_output, input_grad, gate_weight_grad, up_weight_grad, down_weight_grad
 
 

time: 181 us -> 185 us (1.022)
  waiting for transfers between devices: 83.9 us -> 90.2 us
  starting transfers between devices: 50 us -> 48.1 us
    ppermute x12, waiting for transfers between devices: 18.9 us -> 22.8 us  [send_p(): return lax.ppermute(a, BOTH, along(True, k % RING))]
    ppermute x4, starting transfers between devices: 6.05 us -> 3.79 us  [send_core(): return lax.ppermute(a, 'tensor', [(i, i ^ 1) for i in range(2 * DEPTH)])]
  transfers between devices with their start and end apart: 32 -> 32, of which waited for: 18 -> 17; matrix products, arithmetic and copies ran while one was open for 0% -> 0% of each run, Pallas kernels for 11% -> 11%
where the time goes in v4:
time: 185 us
  waiting for transfers between devices  90.2 us (49%)
  starting transfers between devices  48.1 us (26%)
  Pallas kernels  22.3 us (12%)
  between operations  14.5 us (8%)
  local copies, waits for them, and re-layouts  9.68 us (5%)
    ppermute x12, waiting for transfers between devices, send_q(): return lax.ppermute(a, BOTH, along(False, k % RING))  23.1 us
    ppermute x12, waiting for transfers between devices, send_p(): return lax.ppermute(a, BOTH, along(True, k % RING))  22.8 us
    pallas_call x23, Pallas kernels, call(): pl.pallas_call(run, in_specs=[pl.BlockSpec(memory_space=pltpu.VMEM)] * le...  22.3 us
    ppermute x12, starting transfers between devices, send_q(): return lax.ppermute(a, BOTH, along(False, k % RING))  17.4 us
    all_to_all x1, waiting for transfers between devices, gather_z(): lax.all_to_all(copies, 'tensor', 0, 0, tiled=True, axis_index_groups=CORES)  17.2 us
    ppermute x12, starting transfers between devices, send_p(): return lax.ppermute(a, BOTH, along(True, k % RING))  13.8 us
    all_gather x1, waiting for transfers between devices, body(): grads = lax.all_gather(out_grad, 'tensor', axis=0)  13.2 us
    all_to_all x1, waiting for transfers between devices, reduce_z(): lax.all_to_all(parts, 'tensor', 0, 0, tiled=True, axis_index_groups=CORES)  9.84 us
  transfers between devices with their start and end apart: 32, of which 17 were waited for; matrix products, arithmetic and copies ran while one was open for 0% of the time, Pallas kernels for 11%

profile of v4, /device:TPU:1, one launch (start us, length us, event | category | flops | bytes accessed | tf_op | source)
XLA Modules:
  0.0 184.8 jit_solution(15119649901388736361)
XLA Ops:
  7.2 1.8 broadcast_in_dim.3
  8.9 9.0 %all-to-all-start = ((bf16[8,64,512]{2,1,0:T(8,128)(2,1)}), bf16[8,64,512]{2,1,0:T(8,128)(2,1)S(1)}, u32[]{:S(2)}, u32[]{:S(2)}) async-start(bf16[8,64,512]{2,1,0:T(8,128)(2,1)} %broadcast_in_dim.3), calls=%async_computation | async-start | bytes 1048576 | tf_op jit(solution)/shard_map/all_to_all | solution.py:106
  18.7 17.2 %all-to-all-done.refs_0_.refs_4_ = bf16[8,64,512]{2,1,0:T(8,128)(2,1)S(1)} async-done(((bf16[8,64,512]{2,1,0:T(8,128)(2,1)}), bf16[8,64,512]{2,1,0:T(8,128)(2,1)S(1)}, u32[]{:S(2)}, u32[]{:S(2)}) %all-to-all-start) | async-done | bytes 524320 | tf_op jit(solution)/shard_map/all_to_all | solution.py:106
  36.4 1.5 collective-permute-done.6.refs_1_.refs_5_
  37.9 1.2 copy-done.4
  39.1 1.6 shard_map.98
  40.8 1.3 collective-permute-start.7
  42.1 1.6 shard_map.99
  43.7 1.4 collective-permute-start.8
  45.2 1.6 shard_map.100
  46.8 1.6 collective-permute-start.9
  48.4 13.2 %all-gather.3.cloned.1.call-done = bf16[1024,512]{1,0:T(8,128)(2,1)} async-done(((bf16[64,512]{1,0:T(8,128)(2,1)}), bf16[1024,512]{1,0:T(8,128)(2,1)}) %all-gather.3.cloned.1.call-update) | async-done | bytes 1048592 | tf_op jit(solution)/shard_map/all_gather | solution.py:348
  61.6 1.2 copy-done
  63.3 1.3 collective-permute-start
  65.6 1.5 collective-permute-start.1
  67.1 1.5 collective-permute-start.2
  69.4 2.2 %shard_map.101 = (f32[64,1792]{1,0:T(8,128)S(1)}, f32[64,1792]{1,0:T(8,128)S(1)}, f32[64,1792]{1,0:T(8,128)S(1)}, f32[64,1792]{1,0:T(8,128)S(1)}) custom-call(f32[256,1792]{1,0:T(8,128)S(1)} %shard_map.97.refs_0_, bf16[256,1792]{1,0:T(8,128)(2,1)} %collective-permute-done.7.refs_1_, bf16[256,1792]{1,0:T(8,128)(2,1)} %collective-permute-done.8.refs_2_, ...), custom_call_target="tpu_custom_call" | custom-call | tf_op jit(solution)/shard_map/pallas_call | solution.py:39
  71.6 1.2 collective-permute-start.10
  72.8 1.6 collective-permute-start.11
  74.3 1.4 collective-permute-start.12
  76.2 2.0 %collective-permute-done.2.refs_3_ = bf16[256,896]{1,0:T(8,128)(2,1)S(1)} collective-permute-done((bf16[256,896]{1,0:T(8,128)(2,1)S(1)}, bf16[256,896]{1,0:T(8,128)(2,1)S(1)}, u32[]{:S(2)}, u32[]{:S(2)}) %collective-permute-start.2) | collective-permute-done | bytes 458784 | tf_op jit(solution)/shard_map/ppermute | solution.py:71
  78.4 1.9 %collective-permute-start.3 = (f32[64,896]{1,0:T(8,128)S(1)}, f32[64,896]{1,0:T(8,128)S(1)}, u32[]{:S(2)}, u32[]{:S(2)}) collective-permute-start(f32[64,896]{1,0:T(8,128)S(1)} %get-tuple-element.32), channel_id=1, source_target_pairs={{0,64},{1,17},{2,66},{3,19},{4,68},{5,21},{6,70},{7,23},{8,72},{9,... | collective-permute-start | bytes 688136 | tf_op jit(solution)/shard_map/ppermute | solution.py:75
  80.3 2.2 %collective-permute-start.4 = (f32[64,896]{1,0:T(8,128)S(1)}, f32[64,896]{1,0:T(8,128)S(1)}, u32[]{:S(2)}, u32[]{:S(2)}) collective-permute-start(f32[64,896]{1,0:T(8,128)S(1)} %get-tuple-element.33), channel_id=1, source_target_pairs={{0,192},{1,49},{2,194},{3,51},{4,196},{5,53},{6,198},{7,55},{8,200... | collective-permute-start | bytes 688136 | tf_op jit(solution)/shard_map/ppermute | solution.py:75
  82.5 1.1 collective-permute-done.10.refs_1_
  84.2 4.0 %collective-permute-done.11.refs_2_ = f32[64,1792]{1,0:T(8,128)S(1)} collective-permute-done((f32[64,1792]{1,0:T(8,128)S(1)}, f32[64,1792]{1,0:T(8,128)S(1)}, u32[]{:S(2)}, u32[]{:S(2)}) %collective-permute-start.11) | collective-permute-done | bytes 458784 | tf_op jit(solution)/shard_map/ppermute | solution.py:75
  88.5 3.4 %collective-permute-start.18 = (bf16[64,896]{1,0:T(8,128)(2,1)S(1)}, bf16[64,896]{1,0:T(8,128)(2,1)S(1)}, u32[]{:S(2)}, u32[]{:S(2)}) collective-permute-start(bf16[64,896]{1,0:T(8,128)(2,1)S(1)} %get-tuple-element.41.refs_0_), channel_id=1, source_target_pairs={{0,192},{1,49},{2,194},{3,51},{4,196},{5,53},{6,198},{7,55},{8,200... | collective-permute-start | bytes 344072 | tf_op jit(solution)/shard_map/ppermute | solution.py:75
  93.6 3.1 %collective-permute-start.13 = (bf16[64,1792]{1,0:T(8,128)(2,1)S(1)}, bf16[64,1792]{1,0:T(8,128)(2,1)S(1)}, u32[]{:S(2)}, u32[]{:S(2)}) collective-permute-start(bf16[64,1792]{1,0:T(8,128)(2,1)S(1)} %shard_map.103.refs_0_), channel_id=1, source_target_pairs={{0,192},{1,49},{2,194},{3,51},{4,196},{5,53},{6,198},{7,55},{8,200... | collective-permute-start | bytes 688136 | tf_op jit(solution)/shard_map/ppermute | solution.py:75
  97.4 1.2 collective-permute-done.20.refs_3_
  98.6 2.2 %collective-permute-start.21 = (bf16[256,896]{1,0:T(8,128)(2,1)S(1)}, bf16[256,896]{1,0:T(8,128)(2,1)S(1)}, u32[]{:S(2)}, u32[]{:S(2)}) collective-permute-start(bf16[256,896]{1,0:T(8,128)(2,1)S(1)} %shard_map.106.refs_0_), channel_id=1, source_target_pairs={{0,48},{1,193},{2,50},{3,195},{4,52},{5,197},{6,54},{7,199},{8,56}... | collective-permute-start | bytes 1376264 | tf_op jit(solution)/shard_map/ppermute | solution.py:71
  101.7 1.2 collective-permute-start.14
  103.1 7.2 %collective-permute-done.14.refs_2_ = bf16[64,1792]{1,0:T(8,128)(2,1)S(1)} collective-permute-done((bf16[64,1792]{1,0:T(8,128)(2,1)S(1)}, bf16[64,1792]{1,0:T(8,128)(2,1)S(1)}, u32[]{:S(2)}, u32[]{:S(2)}) %collective-permute-start.14) | collective-permute-done | bytes 229408 | tf_op jit(solution)/shard_map/ppermute | solution.py:75
  110.3 7.8 %collective-permute-done.15.refs_3_ = bf16[64,1792]{1,0:T(8,128)(2,1)S(1)} collective-permute-done((bf16[64,1792]{1,0:T(8,128)(2,1)S(1)}, bf16[64,1792]{1,0:T(8,128)(2,1)S(1)}, u32[]{:S(2)}, u32[]{:S(2)}) %collective-permute-start.15) | collective-permute-done | bytes 229408 | tf_op jit(solution)/shard_map/ppermute | solution.py:75
  118.2 1.5 collective-permute-done.23.refs_3_
  119.8 1.2 shard_map.111
  121.1 1.3 copy-done.12
  122.9 1.1 collective-permute-start.17
  125.1 2.4 %shard_map.107 = (f32[896,512]{1,0:T(8,128)}, f32[8,128]{1,0:T(8,128)S(1)}) custom-call(bf16[256,896]{1,0:T(8,128)(2,1)S(1)} %copy-done.14, bf16[256,896]{1,0:T(8,128)(2,1)S(1)} %copy-done.22, bf16[256,896]{1,0:T(8,128)(2,1)S(1)} %copy-done.24, bf16[256,896]{1,0:T(8,128)(2,1)S(1)} %copy-done.26, bf16[16,64,512]{2,1,0:T(8,128)(2,1)S(1)} %bitcast.7), custom_call_target="tpu_custom_call" | custom-call | tf_op jit(solution)/shard_map/pallas_call | solution.py:39
  127.4 8.0 %collective-permute-done.16.refs_1_ = bf16[256,1792]{1,0:T(8,128)(2,1)S(1)} collective-permute-done((bf16[256,1792]{1,0:T(8,128)(2,1)}, bf16[256,1792]{1,0:T(8,128)(2,1)S(1)}, u32[]{:S(2)}, u32[]{:S(2)}) %collective-permute-start.16) | collective-permute-done | bytes 917536 | tf_op jit(solution)/shard_map/ppermute | solution.py:71
  135.4 11.3 %collective-permute-done.17.refs_2_.refs_3_ = bf16[256,1792]{1,0:T(8,128)(2,1)S(1)} collective-permute-done((bf16[256,1792]{1,0:T(8,128)(2,1)}, bf16[256,1792]{1,0:T(8,128)(2,1)S(1)}, u32[]{:S(2)}, u32[]{:S(2)}) %collective-permute-start.17) | collective-permute-done | bytes 917536 | tf_op jit(solution)/shard_map/ppermute | solution.py:71
  146.7 2.2 %shard_map.108 = (f32[8,64,512]{2,1,0:T(8,128)S(1)}, f32[8,64,512]{2,1,0:T(8,128)S(1)}) custom-call(bf16[256,1792]{1,0:T(8,128)(2,1)S(1)} %copy-done.8, bf16[256,1792]{1,0:T(8,128)(2,1)S(1)} %collective-permute-done.16.refs_1_, bf16[256,1792]{1,0:T(8,128)(2,1)S(1)} %collective-permute-done.17.refs_2_.refs_3_, ...), custom_call_target="tpu_custom_call" | custom-call | tf_op jit(solution)/shard_map/pallas_call | solution.py:39
  149.0 2.4 %collective-permute-start.24 = (f32[8,64,512]{2,1,0:T(8,128)S(1)}, f32[8,64,512]{2,1,0:T(8,128)S(1)}, u32[]{:S(2)}, u32[]{:S(2)}) collective-permute-start(f32[8,64,512]{2,1,0:T(8,128)S(1)} %get-tuple-element.44), channel_id=1, source_target_pairs={{0,1},{1,0},{2,3},{3,2},{4,5},{5,4},{6,7},{7,6},{8,9},{9,8},{10,11... | collective-permute-start | bytes 3145736 | tf_op jit(solution)/shard_map/ppermute | solution.py:79
  152.3 1.8 collective-permute-done.26.refs_3_
  155.1 4.1 %all-to-all-start.1 = ((bf16[8,64,512]{2,1,0:T(8,128)(2,1)}), bf16[8,64,512]{2,1,0:T(8,128)(2,1)S(1)}, u32[]{:S(2)}, u32[]{:S(2)}) async-start(bf16[8,64,512]{2,1,0:T(8,128)(2,1)} %copy-done.27), calls=%async_computation.1 | async-start | bytes 1048576 | tf_op jit(solution)/shard_map/all_to_all | solution.py:283
  159.2 1.2 copy-done.18
  160.4 1.2 copy-done.20
  161.6 4.0 %shard_map.112 = (f32[512,896]{1,0:T(8,128)}, f32[512,896]{1,0:T(8,128)}, f32[8,128]{1,0:T(8,128)S(1)}) custom-call(bf16[256,1792]{1,0:T(8,128)(2,1)S(1)} %copy-done.8, bf16[256,1792]{1,0:T(8,128)(2,1)S(1)} %copy-done.16, bf16[256,1792]{1,0:T(8,128)(2,1)S(1)} %copy-done.20, bf16[256,1792]{1,0:T(8,128)(2,1)S(1)} %copy-done.18, ...), custom_call_target="tpu_custom_call" | custom-call | tf_op jit(solution)/shard_map/pallas_call | solution.py:39
  165.6 0.9 copy-done.28
  167.3 9.8 %all-to-all-done.1.refs_1_ = bf16[8,64,512]{2,1,0:T(8,128)(2,1)S(1)} async-done(((bf16[8,64,512]{2,1,0:T(8,128)(2,1)}), bf16[8,64,512]{2,1,0:T(8,128)(2,1)S(1)}, u32[]{:S(2)}, u32[]{:S(2)}) %all-to-all-start.1) | async-done | bytes 524320 | tf_op jit(solution)/shard_map/all_to_all | solution.py:283
  (100 shorter events, 13.3 us)
Async XLA Ops:
  7.2 30.8 %copy-start.3 = (bf16[512,896]{1,0:T(8,128)(2,1)S(1)}, bf16[512,896]{1,0:T(8,128)(2,1)}, u32[]{:S(2)}) copy-start(bf16[512,896]{1,0:T(8,128)(2,1)} %refs_0_.1) | copy-start | bytes 2752516
  8.9 27.0 %all-to-all-start = ((bf16[8,64,512]{2,1,0:T(8,128)(2,1)}), bf16[8,64,512]{2,1,0:T(8,128)(2,1)S(1)}, u32[]{:S(2)}, u32[]{:S(2)}) async-start(bf16[8,64,512]{2,1,0:T(8,128)(2,1)} %broadcast_in_dim.3), calls=%async_computation | async-start | bytes 1048576 | tf_op jit(solution)/shard_map/all_to_all | solution.py:106
  17.9 43.7 %all-gather.3.cloned.1.call-start = ((), (), s32[]{:S(2)}) async-start(), calls=%async_computation.4 | async-start | bytes 1114112 | tf_op jit(solution)/shard_map/all_gather | solution.py:348
  18.7 146.9 %reduce-scatter.2.cloned.1.call-start = ((), (), s32[]{:S(2)}) async-start(), calls=%async_computation.3 | async-start | bytes 2359296 | tf_op jit(solution)/shard_map/reduce_scatter | solution.py:366
  35.9 2.0 %collective-permute-start.6 = (bf16[8,64,512]{2,1,0:T(8,128)(2,1)S(1)}, bf16[8,64,512]{2,1,0:T(8,128)(2,1)S(1)}, u32[]{:S(2)}, u32[]{:S(2)}) collective-permute-start(bf16[8,64,512]{2,1,0:T(8,128)(2,1)S(1)} %all-to-all-done.refs_0_.refs_4_), channel_id=1, source_target_pairs={{0,1},{1,0},{2,3},{3,2},{4,5},{5,4},{6,7},{7,6},{8,9},{9,8},{10,11... | collective-permute-start | bytes 1572872 | tf_op jit(solution)/shard_map/ppermute | solution.py:79
  39.1 6.0 %copy-start.9 = (bf16[8,64,512]{2,1,0:T(8,128)(2,1)}, bf16[8,64,512]{2,1,0:T(8,128)(2,1)S(1)}, u32[]{:S(2)}) copy-start(bf16[8,64,512]{2,1,0:T(8,128)(2,1)S(1)} %collective-permute-done.6.refs_1_.refs_5_) | copy-start | bytes 1572868
  40.8 26.3 %collective-permute-start.7 = (bf16[256,1792]{1,0:T(8,128)(2,1)}, bf16[256,1792]{1,0:T(8,128)(2,1)}, u32[]{:S(2)}, u32[]{:S(2)}) collective-permute-start(bf16[256,1792]{1,0:T(8,128)(2,1)} %shard_map.98), channel_id=1, source_target_pairs={{0,16},{1,65},{2,18},{3,67},{4,20},{5,69},{6,22},{7,71},{8,24},{9,... | collective-permute-start | bytes 2752520 | tf_op jit(solution)/shard_map/ppermute | solution.py:71
  43.7 17.9 %copy-start.2 = (bf16[896,512]{1,0:T(8,128)(2,1)S(1)}, bf16[896,512]{1,0:T(8,128)(2,1)}, u32[]{:S(2)}) copy-start(bf16[896,512]{1,0:T(8,128)(2,1)} %refs_4_.1) | copy-start | bytes 2752516
  43.7 25.6 %collective-permute-start.8 = (bf16[256,1792]{1,0:T(8,128)(2,1)}, bf16[256,1792]{1,0:T(8,128)(2,1)}, u32[]{:S(2)}, u32[]{:S(2)}) collective-permute-start(bf16[256,1792]{1,0:T(8,128)(2,1)} %shard_map.99), channel_id=1, source_target_pairs={{0,48},{1,193},{2,50},{3,195},{4,52},{5,197},{6,54},{7,199},{8,56}... | collective-permute-start | bytes 2752520 | tf_op jit(solution)/shard_map/ppermute | solution.py:71
  46.8 22.6 %collective-permute-start.9 = (bf16[256,1792]{1,0:T(8,128)(2,1)}, bf16[256,1792]{1,0:T(8,128)(2,1)}, u32[]{:S(2)}, u32[]{:S(2)}) collective-permute-start(bf16[256,1792]{1,0:T(8,128)(2,1)} %shard_map.100), channel_id=1, source_target_pairs={{0,32},{1,129},{2,34},{3,131},{4,36},{5,133},{6,38},{7,135},{8,40}... | collective-permute-start | bytes 2752520 | tf_op jit(solution)/shard_map/ppermute | solution.py:71
  63.3 5.3 %copy-start.5 = (bf16[512,896]{1,0:T(8,128)(2,1)S(1)}, bf16[512,896]{1,0:T(8,128)(2,1)}, u32[]{:S(2)}) copy-start(bf16[512,896]{1,0:T(8,128)(2,1)} %refs_1_.9) | copy-start | bytes 2752516
  63.3 5.3 %copy-start.10 = (bf16[8,64,512]{2,1,0:T(8,128)(2,1)S(1)}, bf16[8,64,512]{2,1,0:T(8,128)(2,1)}, u32[]{:S(2)}) copy-start(bf16[8,64,512]{2,1,0:T(8,128)(2,1)} %copy-done.9) | copy-start | bytes 1572868
  63.3 11.0 %collective-permute-start = (bf16[256,896]{1,0:T(8,128)(2,1)S(1)}, bf16[256,896]{1,0:T(8,128)(2,1)S(1)}, u32[]{:S(2)}, u32[]{:S(2)}) collective-permute-start(bf16[256,896]{1,0:T(8,128)(2,1)S(1)} %shard_map.93.refs_4_), channel_id=1, source_target_pairs={{0,16},{1,65},{2,18},{3,67},{4,20},{5,69},{6,22},{7,71},{8,24},{9,... | collective-permute-start | bytes 1376264 | tf_op jit(solution)/shard_map/ppermute | solution.py:71
  65.6 10.7 %collective-permute-start.1 = (bf16[256,896]{1,0:T(8,128)(2,1)S(1)}, bf16[256,896]{1,0:T(8,128)(2,1)S(1)}, u32[]{:S(2)}, u32[]{:S(2)}) collective-permute-start(bf16[256,896]{1,0:T(8,128)(2,1)S(1)} %shard_map.94.refs_5_), channel_id=1, source_target_pairs={{0,48},{1,193},{2,50},{3,195},{4,52},{5,197},{6,54},{7,199},{8,56}... | collective-permute-start | bytes 1376264 | tf_op jit(solution)/shard_map/ppermute | solution.py:71
  67.1 11.1 %collective-permute-start.2 = (bf16[256,896]{1,0:T(8,128)(2,1)S(1)}, bf16[256,896]{1,0:T(8,128)(2,1)S(1)}, u32[]{:S(2)}, u32[]{:S(2)}) collective-permute-start(bf16[256,896]{1,0:T(8,128)(2,1)S(1)} %shard_map.95.refs_6_), channel_id=1, source_target_pairs={{0,32},{1,129},{2,34},{3,131},{4,36},{5,133},{6,38},{7,135},{8,40}... | collective-permute-start | bytes 1376264 | tf_op jit(solution)/shard_map/ppermute | solution.py:71
  69.4 6.4 %copy-start.1 = (bf16[1024,512]{1,0:T(8,128)(2,1)S(1)}, bf16[1024,512]{1,0:T(8,128)(2,1)}, u32[]{:S(2)}) copy-start(bf16[1024,512]{1,0:T(8,128)(2,1)} %all-gather.3.cloned.1.call-done) | copy-start | bytes 3145732
  71.6 12.1 %collective-permute-start.10 = (f32[64,1792]{1,0:T(8,128)S(1)}, f32[64,1792]{1,0:T(8,128)S(1)}, u32[]{:S(2)}, u32[]{:S(2)}) collective-permute-start(f32[64,1792]{1,0:T(8,128)S(1)} %get-tuple-element.36), channel_id=1, source_target_pairs={{0,64},{1,17},{2,66},{3,19},{4,68},{5,21},{6,70},{7,23},{8,72},{9,... | collective-permute-start | bytes 1376264 | tf_op jit(solution)/shard_map/ppermute | solution.py:75
  72.8 15.5 %collective-permute-start.11 = (f32[64,1792]{1,0:T(8,128)S(1)}, f32[64,1792]{1,0:T(8,128)S(1)}, u32[]{:S(2)}, u32[]{:S(2)}) collective-permute-start(f32[64,1792]{1,0:T(8,128)S(1)} %get-tuple-element.37), channel_id=1, source_target_pairs={{0,192},{1,49},{2,194},{3,51},{4,196},{5,53},{6,198},{7,55},{8,200... | collective-permute-start | bytes 1376264 | tf_op jit(solution)/shard_map/ppermute | solution.py:75
  74.3 14.1 %collective-permute-start.12 = (f32[64,1792]{1,0:T(8,128)S(1)}, f32[64,1792]{1,0:T(8,128)S(1)}, u32[]{:S(2)}, u32[]{:S(2)}) collective-permute-start(f32[64,1792]{1,0:T(8,128)S(1)} %get-tuple-element.38), channel_id=1, source_target_pairs={{0,128},{1,33},{2,130},{3,35},{4,132},{5,37},{6,134},{7,39},{8,136... | collective-permute-start | bytes 1376264 | tf_op jit(solution)/shard_map/ppermute | solution.py:75
  78.4 14.2 %collective-permute-start.3 = (f32[64,896]{1,0:T(8,128)S(1)}, f32[64,896]{1,0:T(8,128)S(1)}, u32[]{:S(2)}, u32[]{:S(2)}) collective-permute-start(f32[64,896]{1,0:T(8,128)S(1)} %get-tuple-element.32), channel_id=1, source_target_pairs={{0,64},{1,17},{2,66},{3,19},{4,68},{5,21},{6,70},{7,23},{8,72},{9,... | collective-permute-start | bytes 688136 | tf_op jit(solution)/shard_map/ppermute | solution.py:75
  80.3 12.3 %collective-permute-start.4 = (f32[64,896]{1,0:T(8,128)S(1)}, f32[64,896]{1,0:T(8,128)S(1)}, u32[]{:S(2)}, u32[]{:S(2)}) collective-permute-start(f32[64,896]{1,0:T(8,128)S(1)} %get-tuple-element.33), channel_id=1, source_target_pairs={{0,192},{1,49},{2,194},{3,51},{4,196},{5,53},{6,198},{7,55},{8,200... | collective-permute-start | bytes 688136 | tf_op jit(solution)/shard_map/ppermute | solution.py:75
  83.7 9.9 %collective-permute-start.5 = (f32[64,896]{1,0:T(8,128)S(1)}, f32[64,896]{1,0:T(8,128)S(1)}, u32[]{:S(2)}, u32[]{:S(2)}) collective-permute-start(f32[64,896]{1,0:T(8,128)S(1)} %get-tuple-element.34), channel_id=1, source_target_pairs={{0,128},{1,33},{2,130},{3,35},{4,132},{5,37},{6,134},{7,39},{8,136... | collective-permute-start | bytes 688136 | tf_op jit(solution)/shard_map/ppermute | solution.py:75
  88.5 8.2 %collective-permute-start.18 = (bf16[64,896]{1,0:T(8,128)(2,1)S(1)}, bf16[64,896]{1,0:T(8,128)(2,1)S(1)}, u32[]{:S(2)}, u32[]{:S(2)}) collective-permute-start(bf16[64,896]{1,0:T(8,128)(2,1)S(1)} %get-tuple-element.41.refs_0_), channel_id=1, source_target_pairs={{0,192},{1,49},{2,194},{3,51},{4,196},{5,53},{6,198},{7,55},{8,200... | collective-permute-start | bytes 344072 | tf_op jit(solution)/shard_map/ppermute | solution.py:75
  91.9 5.4 %collective-permute-start.19 = (bf16[64,896]{1,0:T(8,128)(2,1)S(1)}, bf16[64,896]{1,0:T(8,128)(2,1)S(1)}, u32[]{:S(2)}, u32[]{:S(2)}) collective-permute-start(bf16[64,896]{1,0:T(8,128)(2,1)S(1)} %get-tuple-element.41.refs_0_), channel_id=1, source_target_pairs={{0,128},{1,33},{2,130},{3,35},{4,132},{5,37},{6,134},{7,39},{8,136... | collective-permute-start | bytes 344072 | tf_op jit(solution)/shard_map/ppermute | solution.py:75
  92.6 6.0 %collective-permute-start.20 = (bf16[64,896]{1,0:T(8,128)(2,1)S(1)}, bf16[64,896]{1,0:T(8,128)(2,1)S(1)}, u32[]{:S(2)}, u32[]{:S(2)}) collective-permute-start(bf16[64,896]{1,0:T(8,128)(2,1)S(1)} %get-tuple-element.41.refs_0_), channel_id=1, source_target_pairs={{0,64},{1,17},{2,66},{3,19},{4,68},{5,21},{6,70},{7,23},{8,72},{9,... | collective-permute-start | bytes 344072 | tf_op jit(solution)/shard_map/ppermute | solution.py:75
  93.6 9.3 %collective-permute-start.13 = (bf16[64,1792]{1,0:T(8,128)(2,1)S(1)}, bf16[64,1792]{1,0:T(8,128)(2,1)S(1)}, u32[]{:S(2)}, u32[]{:S(2)}) collective-permute-start(bf16[64,1792]{1,0:T(8,128)(2,1)S(1)} %shard_map.103.refs_0_), channel_id=1, source_target_pairs={{0,192},{1,49},{2,194},{3,51},{4,196},{5,53},{6,198},{7,55},{8,200... | collective-permute-start | bytes 688136 | tf_op jit(solution)/shard_map/ppermute | solution.py:75
  98.6 22.4 %copy-start.13 = (bf16[256,896]{1,0:T(8,128)(2,1)}, bf16[256,896]{1,0:T(8,128)(2,1)S(1)}, u32[]{:S(2)}) copy-start(bf16[256,896]{1,0:T(8,128)(2,1)S(1)} %shard_map.106.refs_0_) | copy-start | bytes 1376260
  98.6 19.6 %collective-permute-start.21 = (bf16[256,896]{1,0:T(8,128)(2,1)S(1)}, bf16[256,896]{1,0:T(8,128)(2,1)S(1)}, u32[]{:S(2)}, u32[]{:S(2)}) collective-permute-start(bf16[256,896]{1,0:T(8,128)(2,1)S(1)} %shard_map.106.refs_0_), channel_id=1, source_target_pairs={{0,48},{1,193},{2,50},{3,195},{4,52},{5,197},{6,54},{7,199},{8,56}... | collective-permute-start | bytes 1376264 | tf_op jit(solution)/shard_map/ppermute | solution.py:71
  100.9 17.3 %collective-permute-start.22 = (bf16[256,896]{1,0:T(8,128)(2,1)S(1)}, bf16[256,896]{1,0:T(8,128)(2,1)S(1)}, u32[]{:S(2)}, u32[]{:S(2)}) collective-permute-start(bf16[256,896]{1,0:T(8,128)(2,1)S(1)} %shard_map.106.refs_0_), channel_id=1, source_target_pairs={{0,32},{1,129},{2,34},{3,131},{4,36},{5,133},{6,38},{7,135},{8,40}... | collective-permute-start | bytes 1376264 | tf_op jit(solution)/shard_map/ppermute | solution.py:71
  101.1 18.7 %collective-permute-start.23 = (bf16[256,896]{1,0:T(8,128)(2,1)S(1)}, bf16[256,896]{1,0:T(8,128)(2,1)S(1)}, u32[]{:S(2)}, u32[]{:S(2)}) collective-permute-start(bf16[256,896]{1,0:T(8,128)(2,1)S(1)} %shard_map.106.refs_0_), channel_id=1, source_target_pairs={{0,16},{1,65},{2,18},{3,67},{4,20},{5,69},{6,22},{7,71},{8,24},{9,... | collective-permute-start | bytes 1376264 | tf_op jit(solution)/shard_map/ppermute | solution.py:71
  101.7 8.6 %collective-permute-start.14 = (bf16[64,1792]{1,0:T(8,128)(2,1)S(1)}, bf16[64,1792]{1,0:T(8,128)(2,1)S(1)}, u32[]{:S(2)}, u32[]{:S(2)}) collective-permute-start(bf16[64,1792]{1,0:T(8,128)(2,1)S(1)} %shard_map.103.refs_0_), channel_id=1, source_target_pairs={{0,128},{1,33},{2,130},{3,35},{4,132},{5,37},{6,134},{7,39},{8,136... | collective-permute-start | bytes 688136 | tf_op jit(solution)/shard_map/ppermute | solution.py:75
  102.9 15.2 %collective-permute-start.15 = (bf16[64,1792]{1,0:T(8,128)(2,1)S(1)}, bf16[64,1792]{1,0:T(8,128)(2,1)S(1)}, u32[]{:S(2)}, u32[]{:S(2)}) collective-permute-start(bf16[64,1792]{1,0:T(8,128)(2,1)S(1)} %shard_map.103.refs_0_), channel_id=1, source_target_pairs={{0,64},{1,17},{2,66},{3,19},{4,68},{5,21},{6,70},{7,23},{8,72},{9,... | collective-permute-start | bytes 688136 | tf_op jit(solution)/shard_map/ppermute | solution.py:75
  118.2 2.9 %copy-start.7 = (bf16[256,1792]{1,0:T(8,128)(2,1)}, bf16[256,1792]{1,0:T(8,128)(2,1)S(1)}, u32[]{:S(2)}) copy-start(bf16[256,1792]{1,0:T(8,128)(2,1)S(1)} %shard_map.104.refs_0_.refs_5_) | copy-start | bytes 2752516
  118.2 2.8 %copy-start.21 = (bf16[256,896]{1,0:T(8,128)(2,1)}, bf16[256,896]{1,0:T(8,128)(2,1)S(1)}, u32[]{:S(2)}) copy-start(bf16[256,896]{1,0:T(8,128)(2,1)S(1)} %collective-permute-done.21.refs_1_) | copy-start | bytes 1376260
  118.2 2.8 %copy-start.23 = (bf16[256,896]{1,0:T(8,128)(2,1)}, bf16[256,896]{1,0:T(8,128)(2,1)S(1)}, u32[]{:S(2)}) copy-start(bf16[256,896]{1,0:T(8,128)(2,1)S(1)} %collective-permute-done.22.refs_2_) | copy-start | bytes 1376260
  122.4 2.6 %copy-start.14 = (bf16[256,896]{1,0:T(8,128)(2,1)S(1)}, bf16[256,896]{1,0:T(8,128)(2,1)}, u32[]{:S(2)}) copy-start(bf16[256,896]{1,0:T(8,128)(2,1)} %copy-done.13) | copy-start | bytes 1376260
  122.5 12.9 %collective-permute-start.16 = (bf16[256,1792]{1,0:T(8,128)(2,1)}, bf16[256,1792]{1,0:T(8,128)(2,1)S(1)}, u32[]{:S(2)}, u32[]{:S(2)}) collective-permute-start(bf16[256,1792]{1,0:T(8,128)(2,1)} %copy-done.7), channel_id=1, source_target_pairs={{0,48},{1,193},{2,50},{3,195},{4,52},{5,197},{6,54},{7,199},{8,56}... | collective-permute-start | bytes 2752520 | tf_op jit(solution)/shard_map/ppermute | solution.py:71
  122.9 23.8 %collective-permute-start.17 = (bf16[256,1792]{1,0:T(8,128)(2,1)}, bf16[256,1792]{1,0:T(8,128)(2,1)S(1)}, u32[]{:S(2)}, u32[]{:S(2)}) collective-permute-start(bf16[256,1792]{1,0:T(8,128)(2,1)} %copy-done.7), channel_id=1, source_target_pairs={{0,16},{1,65},{2,18},{3,67},{4,20},{5,69},{6,22},{7,71},{8,24},{9,... | collective-permute-start | bytes 2752520 | tf_op jit(solution)/shard_map/ppermute | solution.py:71
  124.0 27.4 %collective-permute-start.25 = (bf16[256,1792]{1,0:T(8,128)(2,1)}, bf16[256,1792]{1,0:T(8,128)(2,1)S(1)}, u32[]{:S(2)}, u32[]{:S(2)}) collective-permute-start(bf16[256,1792]{1,0:T(8,128)(2,1)} %copy-done.7), channel_id=1, source_target_pairs={{0,32},{1,129},{2,34},{3,131},{4,36},{5,133},{6,38},{7,135},{8,40}... | collective-permute-start | bytes 2752520 | tf_op jit(solution)/shard_map/ppermute | solution.py:71
  125.0 21.7 %copy-start.8 = (bf16[256,1792]{1,0:T(8,128)(2,1)S(1)}, bf16[256,1792]{1,0:T(8,128)(2,1)}, u32[]{:S(2)}) copy-start(bf16[256,1792]{1,0:T(8,128)(2,1)} %copy-done.7) | copy-start | bytes 2752516
  135.4 13.6 %copy-start.15 = (bf16[256,1792]{1,0:T(8,128)(2,1)}, bf16[256,1792]{1,0:T(8,128)(2,1)S(1)}, u32[]{:S(2)}) copy-start(bf16[256,1792]{1,0:T(8,128)(2,1)S(1)} %collective-permute-done.16.refs_1_) | copy-start | bytes 2752516
  149.0 5.1 %collective-permute-start.24 = (f32[8,64,512]{2,1,0:T(8,128)S(1)}, f32[8,64,512]{2,1,0:T(8,128)S(1)}, u32[]{:S(2)}, u32[]{:S(2)}) collective-permute-start(f32[8,64,512]{2,1,0:T(8,128)S(1)} %get-tuple-element.44), channel_id=1, source_target_pairs={{0,1},{1,0},{2,3},{3,2},{4,5},{5,4},{6,7},{7,6},{8,9},{9,8},{10,11... | collective-permute-start | bytes 3145736 | tf_op jit(solution)/shard_map/ppermute | solution.py:79
  151.4 2.9 %copy-start.19 = (bf16[256,1792]{1,0:T(8,128)(2,1)}, bf16[256,1792]{1,0:T(8,128)(2,1)S(1)}, u32[]{:S(2)}) copy-start(bf16[256,1792]{1,0:T(8,128)(2,1)S(1)} %collective-permute-done.25.refs_0_.refs_2_) | copy-start | bytes 2752516
  152.2 1.9 %collective-permute-start.26 = (f32[2,64,512]{2,1,0:T(8,128)S(1)}, f32[2,64,512]{2,1,0:T(8,128)S(1)}, u32[]{:S(2)}, u32[]{:S(2)}) collective-permute-start(f32[2,64,512]{2,1,0:T(8,128)S(1)} %get-tuple-element.46), channel_id=1, source_target_pairs={{0,1},{1,0},{2,3},{3,2},{4,5},{5,4},{6,7},{7,6},{8,9},{9,8},{10,11... | collective-permute-start | bytes 786440 | tf_op jit(solution)/shard_map/ppermute | solution.py:79
  154.1 5.1 %copy-start.11 = (bf16[8,64,512]{2,1,0:T(8,128)(2,1)S(1)}, bf16[8,64,512]{2,1,0:T(8,128)(2,1)}, u32[]{:S(2)}) copy-start(bf16[8,64,512]{2,1,0:T(8,128)(2,1)} %copy-done.9) | copy-start | bytes 1572868
  154.1 5.1 %copy-start.16 = (bf16[256,1792]{1,0:T(8,128)(2,1)S(1)}, bf16[256,1792]{1,0:T(8,128)(2,1)}, u32[]{:S(2)}) copy-start(bf16[256,1792]{1,0:T(8,128)(2,1)} %copy-done.15) | copy-start | bytes 2752516
  155.1 22.0 %all-to-all-start.1 = ((bf16[8,64,512]{2,1,0:T(8,128)(2,1)}), bf16[8,64,512]{2,1,0:T(8,128)(2,1)S(1)}, u32[]{:S(2)}, u32[]{:S(2)}) async-start(bf16[8,64,512]{2,1,0:T(8,128)(2,1)} %copy-done.27), calls=%async_computation.1 | async-start | bytes 1048576 | tf_op jit(solution)/shard_map/all_to_all | solution.py:283
  166.5 10.6 %collective-permute-start.27 = (f32[64,512]{1,0:T(8,128)S(1)}, f32[64,512]{1,0:T(8,128)S(1)}, u32[]{:S(2)}, u32[]{:S(2)}) collective-permute-start(f32[64,512]{1,0:T(8,128)S(1)} %get-tuple-element.51), channel_id=1, source_target_pairs={{0,1},{1,0},{2,3},{3,2},{4,5},{5,4},{6,7},{7,6},{8,9},{9,8},{10,11... | collective-permute-start | bytes 393224 | tf_op jit(solution)/shard_map/ppermute | solution.py:79
  (13 other events, 21.1 us)
Sparse Core Ops, SparseCore 0:
  20.6 40.9 all-gather.2
  122.6 34.4 reduce-scatter.1
